TPU v7x, 512 devices: a whole 4x4x16 slice. The times are simulated.
512 devices in a mesh: row: 8 (over x, core), col: 64 (over y, z).
Axes of the slice: x: 4, y: 4, z: 16, core: 2. Of those that a mesh axis runs over, the one named last changes fastest.
Arguments:
- blocks: bfloat16 [8, 64, 8, 512, 512], P('row', 'col'), may hold values from -0.0234375 to 0.0234375
- block_rows: int32 [8, 64, 8], P('row', 'col'), may hold values from 0 to 3, as said below
- block_cols: int32 [8, 64, 8], P('row', 'col'), may hold values from 0 to 3
- sketch: bfloat16 [16384, 32], P('row'), may hold values from -6 to 6
- theta: float32 [131072], P('col'), may hold values from 0.1 to 10
- rhs: float32 [16384], P('row'), may hold values from -6 to 6
Outputs:
- solution: float32 [16384], P(('row', 'col'))
- residual: float32 [16384], P(('row', 'col'))
- precond_residual: float32 [16384], P(('row', 'col'))
Inputs may be any that keep to these rules, and one draw needn't show every extreme that they name: Within one tile the pairs (block_rows, block_cols) are all different.
All inputs are finite; a program needn't handle non-finite values.
Results may differ from a plain program's by a relative error of at most 0.005.
Values may be sent and summed in bfloat16 or wider, within the bound.
No kernel may reach another device: no remote copies, remote signals or barrier semaphores. Data moves between devices by JAX's collectives and lax.ppermute only.
A program may use at most 64 MiB of HBM per device.

v0:
```python
import jax
import jax.numpy as jnp
from jax import lax
from jax.sharding import PartitionSpec as P

precond_shift = 1.0
regularize = 0.5


def tile_transpose(values, rows_idx, cols_idx, inputs, col_count):
    order = values.shape[1]
    width = inputs.shape[1]
    picked = inputs.reshape(-1, order, width)[rows_idx]
    product = jnp.einsum("nab,nak->nbk", values, picked, preferred_element_type=jnp.float32)
    onehot = (cols_idx[:, None] == jnp.arange(col_count, dtype=jnp.int32)[None, :]).astype(
        jnp.float32
    )
    merged = jnp.einsum("nj,nbk->jbk", onehot, product, precision=lax.Precision.HIGHEST)
    return merged.reshape(col_count * order, width)


def tile_forward(values, rows_idx, cols_idx, inputs, row_count):
    order = values.shape[1]
    width = inputs.shape[1]
    picked = inputs.reshape(-1, order, width)[cols_idx]
    product = jnp.einsum("nab,nbk->nak", values, picked, preferred_element_type=jnp.float32)
    onehot = (rows_idx[:, None] == jnp.arange(row_count, dtype=jnp.int32)[None, :]).astype(
        jnp.float32
    )
    merged = jnp.einsum("ni,nak->iak", onehot, product, precision=lax.Precision.HIGHEST)
    return merged.reshape(row_count * order, width)


def solve_gram(factor, vector):
    middle = lax.linalg.triangular_solve(factor, vector[:, None], left_side=True, lower=True)
    result = lax.linalg.triangular_solve(
        factor, middle, left_side=True, lower=True, transpose_a=True
    )
    return result[:, 0]


def shards(blocks, block_rows, block_cols, sketch, theta, rhs):
    values = blocks[0, 0]
    rows_idx = block_rows[0, 0]
    cols_idx = block_cols[0, 0]
    order = values.shape[1]
    local_rows = sketch.shape[0]
    row_count = local_rows // order
    col_count = theta.shape[0] // order
    share = local_rows // lax.axis_size("col")
    offset = lax.axis_index("col") * share
    sketch_f = sketch.astype(jnp.float32)
    sketch_part = lax.dynamic_slice_in_dim(sketch_f, offset, share, 0)
    rhs_part = lax.dynamic_slice_in_dim(rhs, offset, share, 0)
    col_terms = tile_transpose(values, rows_idx, cols_idx, sketch, col_count)
    sketch_cols = lax.psum(col_terms, "row")
    scaled = (theta[:, None] * sketch_cols).astype(jnp.bfloat16)
    row_terms = tile_forward(values, rows_idx, cols_idx, scaled, row_count)
    ysketch = lax.psum(row_terms, "col") + regularize * sketch_f
    y_part = lax.dynamic_slice_in_dim(ysketch, offset, share, 0)
    cross = jnp.dot(sketch_part.T, y_part, precision=lax.Precision.HIGHEST)
    gram_terms = precond_shift * 0.5 * (cross + cross.T) + jnp.dot(
        y_part.T, y_part, precision=lax.Precision.HIGHEST
    )
    yb_terms = jnp.dot(rhs_part, y_part, precision=lax.Precision.HIGHEST)
    gram, sketched_rhs = lax.psum((gram_terms, yb_terms), ("row", "col"))
    factor = jnp.linalg.cholesky(gram)
    coeffs = solve_gram(factor, sketched_rhs)
    direction_full = (
        rhs - jnp.dot(ysketch, coeffs, precision=lax.Precision.HIGHEST)
    ) / precond_shift
    direction = lax.dynamic_slice_in_dim(direction_full, offset, share, 0)
    dir_low = direction_full.astype(jnp.bfloat16)
    image_terms = tile_transpose(values, rows_idx, cols_idx, dir_low[:, None], col_count)[:, 0]
    image_cols = lax.psum(image_terms, "row")
    image_scaled = (theta * image_cols).astype(jnp.bfloat16)
    product_terms = tile_forward(values, rows_idx, cols_idx, image_scaled[:, None], row_count)[:, 0]
    image_full = lax.psum(product_terms, "col")
    image = lax.dynamic_slice_in_dim(image_full, offset, share, 0) + regularize * direction
    along = lax.psum(jnp.sum(rhs_part * direction), ("row", "col"))
    curvature = lax.psum(jnp.sum(direction * image), ("row", "col"))
    alpha = along / curvature
    residual = rhs_part - alpha * image
    sketched_res = lax.psum(
        jnp.dot(residual, y_part, precision=lax.Precision.HIGHEST), ("row", "col")
    )
    solution = alpha * direction
    res_coeffs = solve_gram(factor, sketched_res)
    precond_residual = (
        residual - jnp.dot(y_part, res_coeffs, precision=lax.Precision.HIGHEST)
    ) / precond_shift
    return (solution, residual, precond_residual)


def solution(mesh):
    in_specs = (
        P("row", "col", None, None, None),
        P("row", "col", None),
        P("row", "col", None),
        P("row", None),
        P("col"),
        P("row"),
    )
    out_specs = (P(("row", "col")), P(("row", "col")), P(("row", "col")))
    return jax.shard_map(shards, mesh=mesh, in_specs=in_specs, out_specs=out_specs, check_vma=False)
```

profile of v0, /device:TPU:1, one launch (start us, length us, event | category | flops | bytes accessed | tf_op | source)
XLA Modules:
  0.0 843.5 jit_solution(10636436678318148877)
XLA Ops:
  7.2 0.0 copy-start.4
  7.2 0.0 all-reduce.5.cloned.1.call-start
  7.2 0.9 copy.48
  8.1 0.7 fusion.47
  8.8 0.0 copy-start.1
  8.8 0.6 gather_fusion
  9.4 3.0 fusion.8
  12.4 0.0 copy-done.4
  12.4 0.7 fusion.17
  13.1 0.0 copy-start.5
  13.1 0.8 copy.25
  13.9 0.0 all-reduce.5.cloned.1.call-update
  13.9 0.0 all-reduce.7.cloned.1.call-start
  14.0 79.1 %all-reduce.5.cloned.1.call-done = f32[2048,32]{0,1:T(8,128)} async-done(((f32[2048,32]{0,1:T(8,128)}), f32[2048,32]{0,1:T(8,128)}) %all-reduce.5.cloned.1.call-update) | async-done | bytes 262160 | tf_op jit(solution)/shard_map/psum | solution.py:56
  93.1 0.0 copy-done.1
  93.1 1.0 multiply_convert_fusion
  94.1 0.0 copy-start
  94.1 0.6 gather_fusion.1
  94.6 0.0 copy-start.2
  94.7 3.5 fusion.11
  98.2 0.0 copy-done.5
  98.2 0.7 fusion.15
  98.8 0.8 copy.26
  99.6 0.0 all-reduce.7.cloned.1.call-update
  99.7 252.7 %all-reduce.7.cloned.1.call-done = f32[2048,32]{0,1:T(8,128)} async-done(((f32[2048,32]{0,1:T(8,128)}), f32[2048,32]{0,1:T(8,128)}) %all-reduce.7.cloned.1.call-update) | async-done | bytes 262160 | tf_op jit(solution)/shard_map/psum | solution.py:59
  352.4 0.0 copy-done
  352.4 1.0 multiply_add_fusion
  353.4 0.2 fusion.36
  353.6 0.1 copy.17
  353.6 0.2 convolution_add_fusion
  353.9 0.0 copy-done.2
  353.9 0.2 convolution_bitcast_fusion.8
  354.1 110.4 %all-reduce.1 = (f32[32,1]{0,1:T(1,128)S(1)}, f32[32,32]{1,0:T(8,128)S(1)}) all-reduce(f32[32,1]{0,1:T(1,128)S(1)} %convolution_bitcast_fusion.8, f32[32,32]{1,0:T(8,128)S(1)} %convolution_add_fusion), channel_id=1, replica_groups=mesh['row'=8,'col'=64] {'row','col'}, use_global_device_ids=true, to_apply=%region_5.6 | all-reduce | flops 1056 | bytes 8448 | tf_op jit(solution)/shard_map/psum | solution.py:66
  464.5 0.1 copy.18
  464.6 2.9 cholesky.18
  467.5 0.6 compare_reduce_fusion
  468.2 0.7 fusion.19
  468.8 2.4 custom-call.12
  471.3 0.2 convolution_bitcast_fusion.7
  471.4 0.1 convolution_bitcast_fusion.6
  471.6 0.3 fusion.58
  471.9 0.6 gather_fusion.2
  472.4 2.8 fusion.2
  475.3 0.1 convolution_bitcast_fusion.1
  475.4 12.9 %psum.68 = f32[2048]{0:T(1024)S(1)} all-reduce(f32[2048]{0:T(1024)S(1)} %bitcast.149), channel_id=1, replica_groups=mesh['row'=8,'col'=64] {'row'}, use_global_device_ids=true, to_apply=%region_8.11 | all-reduce | flops 2048 | bytes 16384 | tf_op jit(solution)/shard_map/psum | solution.py:75
  488.3 0.6 gather_fusion.3
  488.9 3.4 fusion
  492.3 0.1 convolution_bitcast_fusion
  492.4 114.6 %psum.69 = f32[2048]{0:T(1024)S(1)} all-reduce(f32[2048]{0:T(1024)S(1)} %bitcast.150), channel_id=1, replica_groups=mesh['row'=8,'col'=64] {'col'}, use_global_device_ids=true, to_apply=%region_9.12 | all-reduce | flops 2048 | bytes 16384 | tf_op jit(solution)/shard_map/psum | solution.py:78
  607.0 0.7 multiply_reduce_fusion
  607.7 125.3 %all-reduce = (f32[]{:T(128)}, f32[]{:T(128)}) all-reduce(f32[]{:T(128)} %get-tuple-element.6, f32[]{:T(128)} %get-tuple-element.5), channel_id=1, replica_groups=mesh['row'=8,'col'=64] {'row','col'}, use_global_device_ids=true, to_apply=%region_7.10 | all-reduce | flops 2 | bytes 16 | tf_op jit(solution)/shard_map/psum | solution.py:80
  734.4 0.6 multiply_subtract_fusion
  734.9 0.0 copy-start.3
  734.9 0.2 convolution_bitcast_fusion.5
  735.1 100.5 %psum.71 = f32[32,1]{0,1:T(1,128)S(1)} all-reduce(f32[32,1]{0,1:T(1,128)S(1)} %convolution_bitcast_fusion.5), channel_id=1, replica_groups=mesh['row'=8,'col'=64] {'row','col'}, use_global_device_ids=true, to_apply=%region_12.15 | all-reduce | flops 32 | bytes 256 | tf_op jit(solution)/shard_map/psum | solution.py:84
  835.6 0.1 convolution_bitcast_fusion.4
  835.7 0.1 convolution_bitcast_fusion.3
  835.9 0.7 fusion.14
  836.6 0.0 copy-done.3
  (12 shorter events, 0.1 us)
Async XLA Ops:
  7.2 5.2 copy-start.4
  7.2 85.9 %all-reduce.5.cloned.1.call-start = ((), (), s32[]{:S(2)}) async-start(), calls=%async_computation | async-start | bytes 524288 | tf_op jit(solution)/shard_map/psum | solution.py:56
  8.8 84.3 %copy-start.1 = (f32[2048]{0:T(1024)S(1)}, f32[2048]{0:T(1024)}, u32[]{:S(2)}) copy-start(f32[2048]{0:T(1024)} %param.14) | copy-start | bytes 24580
  13.1 85.1 %copy-start.5 = (s32[1,1,8]{2,1,0:T(1,128)S(1)}, s32[1,1,8]{2,1,0:T(1,128)}, u32[]{:S(2)}) copy-start(s32[1,1,8]{2,1,0:T(1,128)} %param.11) | copy-start | bytes 100
  13.9 338.5 %all-reduce.7.cloned.1.call-start = ((), (), s32[]{:S(2)}) async-start(), calls=%async_computation.1 | async-start | bytes 524288 | tf_op jit(solution)/shard_map/psum | solution.py:59
  94.1 258.3 %copy-start = (bf16[2048,32]{0,1:T(8,128)(2,1)S(1)}, bf16[2048,32]{0,1:T(8,128)(2,1)}, u32[]{:S(2)}) copy-start(bf16[2048,32]{0,1:T(8,128)(2,1)} %param.13) | copy-start | bytes 393220
  94.6 259.2 %copy-start.2 = (f32[2048]{0:T(1024)S(1)}, f32[2048]{0:T(1024)}, u32[]{:S(2)}) copy-start(f32[2048]{0:T(1024)} %param.15) | copy-start | bytes 24580
  734.9 101.7 %copy-start.3 = (f32[32]{0:T(128)}, f32[32]{0:T(128)S(1)}, u32[]{:S(2)}) copy-start(f32[32]{0:T(128)S(1)} %get-tuple-element.13) | copy-start | bytes 388
Sparse Core Ops, SparseCore 0:
  14.0 79.0 all-reduce.4
  99.8 252.5 all-reduce.6
where the time goes:
time: 844 us; the launch traced here: 843 us
  blocking collectives  464 us (55%)
  waiting for transfers between devices  332 us (39%)
  matrix products  16.7 us (2%)
  between operations  15.6 us (2%)
  other arithmetic  10.6 us (1%)
    psum x1, waiting for transfers between devices, shards(): ysketch = lax.psum(row_terms, 'col') + regularize * sketch_f  253 us
    psum x1, blocking collectives, shards(): along = lax.psum(jnp.sum(rhs_part * direction), ('row', 'col'))  125 us
    psum x1, blocking collectives, shards(): image_full = lax.psum(product_terms, 'col')  115 us
    psum x1, blocking collectives, shards(): gram, sketched_rhs = lax.psum((gram_terms, yb_terms), ('row', 'col'))  110 us
    psum x1, blocking collectives, shards(): lax.psum(jnp.dot(residual, y_part, precision=lax.Precision.HIGHEST), ('ro...  100 us
    psum x1, waiting for transfers between devices, shards(): sketch_cols = lax.psum(col_terms, 'row')  79.1 us
  transfers between devices with their start and end apart: 2, of which 2 were waited for; matrix products, arithmetic and copies ran while one was open for 0% of the time, Pallas kernels for 0%

commit v1 on v0

v1 whole, which is shorter than its diff:
```python
import jax
import jax.numpy as jnp
from jax import lax
from jax.experimental import pallas as pl
from jax.experimental.pallas import tpu as pltpu
from jax.sharding import PartitionSpec as P

precond_shift = 1.0
regularize = 0.5

F32 = jnp.float32
BF16 = jnp.bfloat16
HIGHEST = lax.Precision.HIGHEST
LANES = 128
ROW_PARTS = 8
COL_PARTS = 64
BLOCKS = 8
ORDER = 512
LOCAL = 2048
WIDTH = 32
PIECE = LOCAL // ROW_PARTS
TILES = LOCAL // LANES
GROUPS = WIDTH // 8
VMEM_LIMIT = 24 * 1024 * 1024

NT = (((1,), (1,)), ((), ()))


def vmem():
    return pl.BlockSpec(memory_space=pltpu.VMEM)


def smem():
    return pl.BlockSpec(memory_space=pltpu.SMEM)


def iota(shape, axis):
    return lax.broadcasted_iota(jnp.int32, shape, axis)


def call(body, in_specs, out_shape, scratch=(), flops=0, name=None):
    out_specs = jax.tree.map(lambda _: vmem(), out_shape)
    return pl.pallas_call(
        body,
        in_specs=in_specs,
        out_specs=out_specs,
        out_shape=out_shape,
        scratch_shapes=list(scratch),
        compiler_params=pltpu.CompilerParams(vmem_limit_bytes=VMEM_LIMIT),
        cost_estimate=pl.CostEstimate(flops=flops, bytes_accessed=1 << 20, transcendentals=0),
        name=name,
    )


def sketch_body(rows_ref, cols_ref, omega_ref, blocks_ref, out_ref):
    out_ref[...] = jnp.zeros(out_ref.shape, F32)
    for n in range(BLOCKS):
        start = pl.multiple_of(rows_ref[n] * ORDER, ORDER)
        product = jnp.dot(
            omega_ref[:, pl.ds(start, ORDER)], blocks_ref[n], preferred_element_type=F32
        )
        place = cols_ref[n] * 2
        out_ref[place] += product[:, :PIECE]
        out_ref[place + 1] += product[:, PIECE:]


def scale_body(me_ref, parts_ref, theta_ref, out_ref):
    total = parts_ref[0]
    for i in range(1, ROW_PARTS):
        total += parts_ref[i]
    scaled = (theta_ref[pl.ds(me_ref[0], 1), :] * total).astype(BF16)
    for i in range(ROW_PARTS):
        out_ref[i] = scaled


def forward_body(rows_ref, cols_ref, scaled_ref, blocks_ref, out_ref):
    out_ref[...] = jnp.zeros(out_ref.shape, F32)
    for n in range(BLOCKS):
        place = cols_ref[n] * 2
        left = jnp.concatenate([scaled_ref[place], scaled_ref[place + 1]], axis=1)
        product = lax.dot_general(left, blocks_ref[n], NT, preferred_element_type=F32)
        first = rows_ref[n] * (ORDER // LANES)
        for g in range(GROUPS):
            for q in range(ORDER // LANES):
                out_ref[g * TILES + first + q] += product[
                    8 * g : 8 * g + 8, LANES * q : LANES * (q + 1)
                ]


def spread_body(parts_ref, out_ref):
    sums = [parts_ref[i] for i in range(8)]
    for i in range(8, COL_PARTS):
        sums[i % 8] += parts_ref[i]
    while len(sums) > 1:
        sums = [a + b for a, b in zip(sums[::2], sums[1::2])]
    for i in range(COL_PARTS):
        out_ref[i] = sums[0]


def gram_body(
    rows_ref, cols_ref, tiles_ref, omega_ref, rhs_ref, blocks_ref, y_ref, out_ref, all_ref, cut_ref, acc_ref
):
    for g in range(GROUPS):
        for t in range(TILES):
            y_ref[8 * g : 8 * g + 8, LANES * t : LANES * (t + 1)] = tiles_ref[g * TILES + t]
    omega = omega_ref[...].astype(F32)
    ysketch = y_ref[...] + regularize * omega
    y_ref[...] = ysketch
    top = ysketch.astype(BF16)
    rest = ysketch - top.astype(F32)
    middle = rest.astype(BF16)
    low = (rest - middle.astype(F32)).astype(BF16)
    cut_ref[0:WIDTH, :] = top
    cut_ref[WIDTH : 2 * WIDTH, :] = middle
    cut_ref[2 * WIDTH : 3 * WIDTH, :] = low
    rhs = rhs_ref[...]
    rhs_top = rhs.astype(BF16).astype(F32)
    rhs_rest = rhs - rhs_top
    rhs_middle = rhs_rest.astype(BF16).astype(F32)
    rhs_low = rhs_rest - rhs_middle
    spot = iota((16, LOCAL), 0)
    rhs_cut = jnp.where(
        spot == 0, rhs_top, jnp.where(spot == 1, rhs_middle, jnp.where(spot == 2, rhs_low, 0.0))
    )
    cut_ref[3 * WIDTH :, :] = rhs_cut.astype(BF16)
    all_ref[0:WIDTH, :] = ysketch
    all_ref[WIDTH : 2 * WIDTH, :] = omega
    all_ref[2 * WIDTH :, :] = jnp.where(iota((LANES - 2 * WIDTH, LOCAL), 0) == 0, rhs, 0.0)

    products = lax.dot_general(
        all_ref[0 : 2 * WIDTH + 8, :], all_ref[...], NT, precision=HIGHEST, preferred_element_type=F32
    )
    lane = iota((WIDTH, LANES), 1)
    upper = products[0:WIDTH]
    cross = 0.5 * (upper + pltpu.roll(products[WIDTH : 2 * WIDTH], WIDTH, 1))
    gram = jnp.where(lane < WIDTH, upper, jnp.where(lane < 2 * WIDTH, cross, 0.0))
    for i in range(ROW_PARTS):
        out_ref[i, 0:WIDTH, PIECE:] = gram
        out_ref[i, WIDTH:, PIECE:] = products[2 * WIDTH :]

    acc_ref[...] = jnp.zeros(acc_ref.shape, F32)
    for n in range(BLOCKS):
        start = pl.multiple_of(rows_ref[n] * ORDER, ORDER)
        acc_ref[cols_ref[n]] += jnp.dot(
            cut_ref[:, pl.ds(start, ORDER)], blocks_ref[n], preferred_element_type=F32
        )
    for j in range(LOCAL // ORDER):
        image = acc_ref[j, 0:WIDTH] + (acc_ref[j, WIDTH : 2 * WIDTH] + acc_ref[j, 2 * WIDTH : 3 * WIDTH])
        rhs_image = jnp.sum(acc_ref[j, 3 * WIDTH :], axis=0, keepdims=True)
        for h in range(2):
            out_ref[2 * j + h, 0:WIDTH, 0:PIECE] = image[:, PIECE * h : PIECE * (h + 1)]
            out_ref[2 * j + h, WIDTH:, 0:PIECE] = jnp.broadcast_to(
                rhs_image[:, PIECE * h : PIECE * (h + 1)], (8, PIECE)
            )


def to_column(row, shift):
    lane = iota((WIDTH, LANES), 1)
    return jnp.sum(
        jnp.where(lane == iota((WIDTH, LANES), 0) + shift, row, 0.0), axis=1, keepdims=True
    )


def to_row(column, shift):
    lane = iota((WIDTH, LANES), 1)
    return jnp.sum(
        jnp.where(lane == iota((WIDTH, LANES), 0) + shift, column, 0.0), axis=0, keepdims=True
    )


def solve_gram(inverse, diagonal, row):
    half = jnp.sum(inverse * pltpu.roll(row, WIDTH, 1), axis=1, keepdims=True) / diagonal
    return jnp.sum(inverse * half, axis=0, keepdims=True)


def factor_body(me_ref, parts_ref, theta_ref, out_ref, keep_ref):
    total = parts_ref[0]
    for i in range(1, ROW_PARTS):
        total += parts_ref[i]
    gram = total[0:WIDTH, PIECE:]
    lane = iota((WIDTH, LANES), 1)
    spot = iota((WIDTH, LANES), 0)
    work = jnp.where(
        lane < WIDTH,
        gram + pltpu.roll(gram, LANES - WIDTH, 1),
        jnp.where(lane == spot + WIDTH, 1.0, 0.0),
    )
    for k in range(WIDTH - 1):
        pivot = work[k : k + 1, :]
        factor = work[:, k : k + 1] / pivot[:, k : k + 1]
        work = work - jnp.where(spot > k, factor, 0.0) * pivot
    diagonal = jnp.sum(jnp.where(lane == spot, work, 0.0), axis=1, keepdims=True)
    inverse = jnp.where((lane >= WIDTH) & (lane < 2 * WIDTH), work, 0.0)

    tail = total[WIDTH:, PIECE:]
    sketched_rhs = jnp.where(iota((1, LANES), 1) < WIDTH, tail[0:1], 0.0)
    coeffs = solve_gram(inverse, diagonal, sketched_rhs)
    column = to_column(coeffs, WIDTH)
    crossed = jnp.sum(jnp.where((lane >= WIDTH) & (lane < 2 * WIDTH), gram * column, 0.0), axis=0, keepdims=True)

    image_sketch = total[0:WIDTH, 0:PIECE]
    image_cols = total[WIDTH : WIDTH + 1, 0:PIECE] - jnp.sum(image_sketch * column, axis=0, keepdims=True)
    scaled = (theta_ref[pl.ds(me_ref[0], 1), :] * image_cols).astype(BF16).astype(F32)
    sketched = to_row(jnp.sum(image_sketch * scaled, axis=1, keepdims=True), 0)
    curvature = jnp.sum(image_cols * scaled, axis=1, keepdims=True)
    sums = jnp.where(iota((1, LANES), 1) == WIDTH, curvature, sketched)
    where = iota((8, LANES), 0) % 4
    pack = jnp.where(
        where == 0,
        scaled[:, :LANES],
        jnp.where(where == 1, scaled[:, LANES:], jnp.where(where == 2, sums, 0.0)),
    )
    for i in range(ROW_PARTS // 2):
        out_ref[8 * i : 8 * i + 8, :] = pack
    keep_ref[0:WIDTH, :] = inverse
    keep_ref[WIDTH : 2 * WIDTH, :] = jnp.broadcast_to(diagonal, (WIDTH, LANES))
    keep_ref[2 * WIDTH : 2 * WIDTH + 8, :] = tail
    keep_ref[2 * WIDTH + 8 : 2 * WIDTH + 16, :] = jnp.broadcast_to(coeffs, (8, LANES))
    keep_ref[2 * WIDTH + 16 :, :] = jnp.broadcast_to(crossed, (8, LANES))


def image_body(rows_ref, cols_ref, parts_ref, blocks_ref, out_ref, scaled_ref, acc_ref):
    sums = parts_ref[2:3, :]
    for i in range(1, ROW_PARTS):
        sums += parts_ref[4 * i + 2 : 4 * i + 3, :]
    for j in range(LOCAL // ORDER):
        line = jnp.concatenate(
            [parts_ref[4 * (2 * j + h) + s : 4 * (2 * j + h) + s + 1, :] for h in range(2) for s in range(2)],
            axis=1,
        )
        scaled_ref[j] = jnp.broadcast_to(line, (16, ORDER)).astype(BF16)
    acc_ref[...] = jnp.zeros(acc_ref.shape, F32)
    for n in range(BLOCKS):
        product = lax.dot_general(
            scaled_ref[cols_ref[n]], blocks_ref[n], NT, preferred_element_type=F32
        )
        acc_ref[rows_ref[n]] += product[0:8]
    even = iota((8, LANES), 0) % 2 == 0
    for t in range(TILES):
        at = LANES * (t % 4)
        out_ref[8 * t : 8 * t + 8, :] = jnp.where(even, acc_ref[t // 4, :, at : at + LANES], sums)


def step_body(me_ref, parts_ref, keep_ref, y_ref, rhs_ref, out_ref):
    total = parts_ref[0:8, :]
    for i in range(1, COL_PARTS // 4):
        total += parts_ref[8 * i : 8 * i + 8, :]
    even = iota((8, LANES), 0) % 2 == 0
    image_rows = jnp.sum(jnp.where(even, total, 0.0), axis=0, keepdims=True)
    sums = jnp.sum(jnp.where(even, 0.0, total), axis=0, keepdims=True)

    lane = iota((1, LANES), 1)
    first = lane < WIDTH
    inverse = keep_ref[0:WIDTH, :]
    diagonal = keep_ref[WIDTH : 2 * WIDTH, 0:1]
    tail = keep_ref[2 * WIDTH : 2 * WIDTH + 1, :]
    coeffs = keep_ref[2 * WIDTH + 8 : 2 * WIDTH + 9, :]
    crossed = keep_ref[2 * WIDTH + 16 : 2 * WIDTH + 17, :]
    sketched_rhs = jnp.where(first, tail, 0.0)
    square = jnp.sum(jnp.where(lane == 2 * WIDTH, tail, 0.0), axis=1, keepdims=True)
    along = square - jnp.sum(pltpu.roll(sketched_rhs, WIDTH, 1) * coeffs, axis=1, keepdims=True)
    length = along - jnp.sum(crossed * coeffs, axis=1, keepdims=True)
    curvature = jnp.sum(jnp.where(lane == WIDTH, sums, 0.0), axis=1, keepdims=True) + regularize * length
    alpha = along / curvature

    start = pl.multiple_of((me_ref[0] // 4) * LANES, LANES)
    ysketch = y_ref[:, pl.ds(start, LANES)]
    rhs = rhs_ref[:, pl.ds(start, LANES)]
    direction = (rhs - jnp.sum(ysketch * to_column(coeffs, WIDTH), axis=0, keepdims=True)) / precond_shift
    image = image_rows + regularize * direction
    residual = rhs - alpha * image
    sketched_image = jnp.where(first, sums, 0.0) + regularize * pltpu.roll(crossed, LANES - WIDTH, 1)
    sketched_res = sketched_rhs - alpha * sketched_image
    res_coeffs = solve_gram(inverse, diagonal, sketched_res)
    precond_residual = (
        residual - jnp.sum(ysketch * to_column(res_coeffs, WIDTH), axis=0, keepdims=True)
    ) / precond_shift
    which = iota((8, LANES), 0)
    pack = jnp.where(
        which == 0, alpha * direction, jnp.where(which == 1, residual, precond_residual)
    )
    out_ref[...] = pltpu.roll(pack, ((4 - me_ref[0] % 4) % 4) * WIDTH, 1)


def exchange(value, axis):
    return lax.all_to_all(value, axis, 0, 0, tiled=True)


def shards(blocks, block_rows, block_cols, sketch, theta, rhs):
    values = blocks[0, 0]
    rows_idx = block_rows[0, 0]
    cols_idx = block_cols[0, 0]
    omega = sketch.T
    theta_pieces = theta.reshape(ROW_PARTS, PIECE)
    rhs_line = rhs.reshape(1, LOCAL)
    my_row = lax.axis_index("row").astype(jnp.int32).reshape(1)
    my_col = lax.axis_index("col").astype(jnp.int32).reshape(1)
    shape = jax.ShapeDtypeStruct
    work = 2 * BLOCKS * ORDER * ORDER

    with jax.named_scope("sketch_cols"):
        terms = call(
            sketch_body,
            [smem(), smem(), vmem(), vmem()],
            shape((ROW_PARTS, WIDTH, PIECE), F32),
            flops=work * WIDTH,
            name="sketch_cols",
        )(rows_idx, cols_idx, omega, values)
        parts = exchange(terms, "row")
    with jax.named_scope("scaled"):
        scaled = call(
            scale_body,
            [smem(), vmem(), vmem()],
            shape((ROW_PARTS, WIDTH, PIECE), BF16),
            name="scaled",
        )(my_row, parts, theta_pieces)
        scaled = exchange(scaled, "row")
    with jax.named_scope("ysketch"):
        terms = call(
            forward_body,
            [smem(), smem(), vmem(), vmem()],
            shape((COL_PARTS, 8, LANES), F32),
            flops=work * WIDTH,
            name="ysketch",
        )(rows_idx, cols_idx, scaled, values)
        parts = exchange(terms, "col")
        parts = call(
            spread_body, [vmem()], shape((COL_PARTS, 8, LANES), F32), name="ysketch_spread"
        )(parts)
        tiles = exchange(parts, "col")
    with jax.named_scope("gram"):
        ysketch, terms = call(
            gram_body,
            [smem(), smem(), vmem(), vmem(), vmem(), vmem()],
            (shape((WIDTH, LOCAL), F32), shape((ROW_PARTS, WIDTH + 8, PIECE + LANES), F32)),
            scratch=[
                pltpu.VMEM((LANES, LOCAL), F32),
                pltpu.VMEM((3 * WIDTH + 16, LOCAL), BF16),
                pltpu.VMEM((LOCAL // ORDER, 3 * WIDTH + 16, ORDER), F32),
            ],
            flops=work * WIDTH * 3,
            name="gram",
        )(rows_idx, cols_idx, tiles, omega, rhs_line, values)
        parts = exchange(terms, "row")
    with jax.named_scope("image_scaled"):
        terms, keep = call(
            factor_body,
            [smem(), vmem(), vmem()],
            (shape((4 * ROW_PARTS, LANES), F32), shape((2 * WIDTH + 24, LANES), F32)),
            name="image_scaled",
        )(my_row, parts, theta_pieces)
        parts = exchange(terms.reshape(ROW_PARTS, 4, LANES), "row").reshape(4 * ROW_PARTS, LANES)
    with jax.named_scope("image"):
        terms = call(
            image_body,
            [smem(), smem(), vmem(), vmem()],
            shape((2 * COL_PARTS, LANES), F32),
            scratch=[
                pltpu.VMEM((LOCAL // ORDER, 16, ORDER), BF16),
                pltpu.VMEM((LOCAL // ORDER, 8, ORDER), F32),
            ],
            flops=work,
            name="image",
        )(rows_idx, cols_idx, parts, values)
        parts = exchange(terms.reshape(COL_PARTS, 2, LANES), "col").reshape(2 * COL_PARTS, LANES)
    with jax.named_scope("step"):
        out = call(
            step_body,
            [smem(), vmem(), vmem(), vmem(), vmem()],
            shape((8, LANES), F32),
            name="step",
        )(my_col, parts, keep, ysketch, rhs_line)
    share = LOCAL // COL_PARTS
    return (out[0, :share], out[1, :share], out[2, :share])


def solution(mesh):
    in_specs = (
        P("row", "col", None, None, None),
        P("row", "col", None),
        P("row", "col", None),
        P("row", None),
        P("col"),
        P("row"),
    )
    out_specs = (P(("row", "col")), P(("row", "col")), P(("row", "col")))
    return jax.shard_map(shards, mesh=mesh, in_specs=in_specs, out_specs=out_specs, check_vma=False)
```

time: 844 us -> 147 us (0.17)
  blocking collectives: 464 us -> 90.5 us
  waiting for transfers between devices: 332 us -> 20 us
  matrix products: 16.7 us -> 0 us
  starting transfers between devices: 0.08 us -> 16.5 us
  between operations: 15.6 us -> 0.72 us
  Pallas kernels: 0 us -> 11.8 us
  other arithmetic: 10.6 us -> 0 us
    psum x5 -> x0, blocking collectives: 464 us -> none  [the longest x1 125 us: shards(): along = lax.psum(jnp.sum(rhs_part * direction), ('row', 'col'))]
    psum x2 -> x0, waiting for transfers between devices: 332 us -> none  [the longest x1 253 us: shards(): ysketch = lax.psum(row_terms, 'col') + regularize * sketch_f]
    all_to_all x0 -> x5, blocking collectives: none -> 90.5 us  [exchange(): return lax.all_to_all(value, axis, 0, 0, tiled=True)]
    all_to_all x0 -> x2, waiting for transfers between devices: none -> 20 us  [exchange(): return lax.all_to_all(value, axis, 0, 0, tiled=True)]
    all_to_all x0 -> x2, starting transfers between devices: none -> 16.5 us  [exchange(): return lax.all_to_all(value, axis, 0, 0, tiled=True)]
    dot_general x14 -> x0, matrix products: 16.2 us -> none  [the longest x2 6.87 us: tile_forward(): jnp.einsum('nab,nbk->nak', values, picked, preferred_element_type=jnp.flo...]
    pallas_call x0 -> x8, Pallas kernels: none -> 11.8 us  [the longest x1 2.89 us: shards(): call(factor_body, [smem(), vmem(), vmem()], (shape((4 * ROW_PARTS, LANES)...]
where the time goes in v1:
time: 147 us
  blocking collectives  90.5 us (62%)
  waiting for transfers between devices  20 us (14%)
  starting transfers between devices  16.5 us (11%)
  Pallas kernels  11.8 us (8%)
  local copies, waits for them, and re-layouts  7.16 us (5%)
    all_to_all x5, blocking collectives, exchange(): return lax.all_to_all(value, axis, 0, 0, tiled=True)  90.5 us
    all_to_all x2, waiting for transfers between devices, exchange(): return lax.all_to_all(value, axis, 0, 0, tiled=True)  20 us
    all_to_all x2, starting transfers between devices, exchange(): return lax.all_to_all(value, axis, 0, 0, tiled=True)  16.5 us
    unnamed x22, local copies, waits for them, and re-layouts  6.62 us
  transfers between devices with their start and end apart: 2, of which 2 were waited for; matrix products, arithmetic and copies ran while one was open for 0% of the time, Pallas kernels for 0%

profile of v1, /device:TPU:1, one launch (start us, length us, event | category | flops | bytes accessed | tf_op | source)
XLA Modules:
  0.0 146.6 jit_solution(4338566633431935050)
XLA Ops:
  0.6 0.0 copy-start.9
  0.6 0.0 copy-start.7
  0.7 0.0 copy-start
  0.7 2.2 %copy-done = bf16[1,1,8,512,512]{4,3,2,1,0:T(8,128)(2,1)S(1)} copy-done((bf16[1,1,8,512,512]{4,3,2,1,0:T(8,128)(2,1)S(1)}, bf16[1,1,8,512,512]{4,3,2,1,0:T(8,128)(2,1)}, u32[]{:S(2)}) %copy-start) | copy-done | bytes 4194328
  2.9 0.0 copy-start.3
  2.9 0.9 copy-done.3
  3.8 0.0 copy-start.6
  3.8 0.7 copy-done.6
  4.4 0.0 copy-start.8
  4.4 0.7 copy-done.8
  5.1 0.0 copy-start.10
  5.1 2.1 %sketch_cols.1 = f32[8,32,256]{2,1,0:T(8,128)} custom-call(s32[8]{0:T(128)S(1)} %bitcast.28, s32[8]{0:T(128)S(1)} %bitcast.32, bf16[32,2048]{1,0:T(8,128)(2,1)S(1)} %bitcast.21, bf16[8,512,512]{2,1,0:T(8,128)(2,1)S(1)} %bitcast.17), custom_call_target="tpu_custom_call" | custom-call | flops 134217728 | bytes 1048576 | tf_op jit(solution)/shard_map/sketch_cols/sketch_cols/pallas_call | solution.py:302
  7.1 0.0 copy-start.4
  7.1 0.0 copy-start.5
  7.1 10.3 %all-to-all-start = ((f32[8,32,256]{2,1,0:T(8,128)}), f32[8,32,256]{2,1,0:T(8,128)S(1)}, u32[]{:S(2)}, u32[]{:S(2)}) async-start(f32[8,32,256]{2,1,0:T(8,128)} %sketch_cols.1), calls=%async_computation | async-start | bytes 524288 | tf_op jit(solution)/shard_map/sketch_cols/all_to_all | solution.py:286
  17.5 0.0 copy-done.10
  17.5 6.5 %all-to-all-done.parts_ref = f32[8,32,256]{2,1,0:T(8,128)S(1)} async-done(((f32[8,32,256]{2,1,0:T(8,128)}), f32[8,32,256]{2,1,0:T(8,128)S(1)}, u32[]{:S(2)}, u32[]{:S(2)}) %all-to-all-start) | async-done | bytes 262176 | tf_op jit(solution)/shard_map/sketch_cols/all_to_all | solution.py:286
  24.0 8.7 %all_to_all.35.scaled_ref = bf16[8,32,256]{2,1,0:T(8,128)(2,1)S(1)} all-to-all(bf16[8,32,256]{2,1,0:T(8,128)(2,1)S(1)} %scaled.1), channel_id=1, replica_groups=mesh['row'=8,'col'=64] {'row'}, dimensions={0} | all-to-all | bytes 262144 | tf_op jit(solution)/shard_map/scaled/all_to_all | solution.py:286
  32.7 0.0 copy-done.9
  32.7 0.0 copy-done.7
  32.7 0.0 copy-start.1
  32.7 2.2 %copy-done.1 = bf16[1,1,8,512,512]{4,3,2,1,0:T(8,128)(2,1)S(1)} copy-done((bf16[1,1,8,512,512]{4,3,2,1,0:T(8,128)(2,1)S(1)}, bf16[1,1,8,512,512]{4,3,2,1,0:T(8,128)(2,1)}, u32[]{:S(2)}) %copy-start.1) | copy-done | bytes 4194328
  34.9 0.0 copy-start.2
  34.9 1.9 %ysketch.1 = f32[64,8,128]{2,1,0:T(8,128)S(1)} custom-call(s32[8]{0:T(128)S(1)} %bitcast.29, s32[8]{0:T(128)S(1)} %bitcast.33, bf16[8,32,256]{2,1,0:T(8,128)(2,1)S(1)} %all_to_all.35.scaled_ref, bf16[8,512,512]{2,1,0:T(8,128)(2,1)S(1)} %bitcast.18), custom_call_target="tpu_custom_call" | custom-call | flops 134217728 | bytes 1048576 | tf_op jit(solution)/shard_map/ysketch/ysketch/pallas_call | solution.py:319
  36.8 32.6 %all_to_all.36.parts_ref = f32[64,8,128]{2,1,0:T(8,128)S(1)} all-to-all(f32[64,8,128]{2,1,0:T(8,128)S(1)} %ysketch.1), channel_id=1, replica_groups=mesh['row'=8,'col'=64] {'col'}, dimensions={0} | all-to-all | bytes 524288 | tf_op jit(solution)/shard_map/ysketch/all_to_all | solution.py:286
  69.3 26.1 %all_to_all.37.tiles_ref = f32[64,8,128]{2,1,0:T(8,128)S(1)} all-to-all(f32[64,8,128]{2,1,0:T(8,128)S(1)} %ysketch_spread.1), channel_id=1, replica_groups=mesh['row'=8,'col'=64] {'col'}, dimensions={0} | all-to-all | bytes 524288 | tf_op jit(solution)/shard_map/ysketch/all_to_all | solution.py:286
  95.5 0.0 copy-done.4
  95.5 0.0 copy-done.5
  95.5 0.0 copy-done.2
  95.5 2.0 %gram.1 = (f32[32,2048]{1,0:T(8,128)S(1)}, f32[8,40,384]{2,1,0:T(8,128)S(1)}) custom-call(s32[8]{0:T(128)S(1)} %bitcast.30, s32[8]{0:T(128)S(1)} %bitcast.34, f32[64,8,128]{2,1,0:T(8,128)S(1)} %all_to_all.37.tiles_ref, bf16[32,2048]{1,0:T(8,128)(2,1)S(1)} %bitcast.22, f32[1,2048]{1,0:T(1,128)S(1)} %bitcast.25, bf16[8,512,512]{2,1,0:T(8,128)(2,1)S(1)} %bitcast.19), custom_call_target="tpu_custom_call" | custom-call | flops 402653184 | bytes 1048576 | tf_op jit(solution)/shard_map/gram/gram/pallas_call | solution.py:332
  97.5 15.1 %all_to_all.38.parts_ref = f32[8,40,384]{2,1,0:T(8,128)S(1)} all-to-all(f32[8,40,384]{2,1,0:T(8,128)S(1)} %get-tuple-element.7), channel_id=1, replica_groups=mesh['row'=8,'col'=64] {'row'}, dimensions={0} | all-to-all | bytes 983040 | tf_op jit(solution)/shard_map/gram/all_to_all | solution.py:286
  112.6 2.9 %image_scaled.1 = (f32[32,128]{1,0:T(8,128)S(1)}, f32[88,128]{1,0:T(8,128)S(1)}) custom-call(s32[1]{0:T(128)} %bitcast.3.me_ref, f32[8,40,384]{2,1,0:T(8,128)S(1)} %all_to_all.38.parts_ref, f32[8,256]{1,0:T(8,128)S(1)} %reshape.32.theta_ref), custom_call_target="tpu_custom_call" | custom-call | bytes 1048576 | tf_op jit(solution)/shard_map/image_scaled/image_scaled/pallas_call | solution.py:346
  115.5 8.0 %all_to_all.39 = f32[8,4,128]{2,1,0:T(4,128)S(1)} all-to-all(f32[8,4,128]{2,1,0:T(4,128)S(1)} %bitcast.27), channel_id=1, replica_groups=mesh['row'=8,'col'=64] {'row'}, dimensions={0} | all-to-all | bytes 32768 | tf_op jit(solution)/shard_map/image_scaled/all_to_all | solution.py:286
  123.5 2.4 %image.1 = f32[128,128]{1,0:T(8,128)} custom-call(s32[8]{0:T(128)S(1)} %bitcast.31, s32[8]{0:T(128)S(1)} %bitcast.35, f32[32,128]{1,0:T(8,128)S(1)} %bitcast.24, bf16[8,512,512]{2,1,0:T(8,128)(2,1)S(1)} %bitcast.20), custom_call_target="tpu_custom_call" | custom-call | flops 4194304 | bytes 1048576 | tf_op jit(solution)/shard_map/image/image/pallas_call | solution.py:354
  125.9 6.1 %all-to-all-start.6 = ((f32[64,2,128]{2,1,0:T(2,128)}), f32[64,2,128]{2,1,0:T(2,128)S(1)}, u32[]{:S(2)}, u32[]{:S(2)}) async-start(f32[64,2,128]{2,1,0:T(2,128)} %bitcast.9), calls=%async_computation.6 | async-start | bytes 131072 | tf_op jit(solution)/shard_map/image/all_to_all | solution.py:286
  132.1 13.5 %all-to-all-done.6 = f32[64,2,128]{2,1,0:T(2,128)S(1)} async-done(((f32[64,2,128]{2,1,0:T(2,128)}), f32[64,2,128]{2,1,0:T(2,128)S(1)}, u32[]{:S(2)}, u32[]{:S(2)}) %all-to-all-start.6) | async-done | bytes 65568 | tf_op jit(solution)/shard_map/image/all_to_all | solution.py:286
  145.6 0.5 step.1
  146.1 0.5 slice_bitcast_fusion
  (3 shorter events, 0.1 us)
Async XLA Ops:
  0.6 32.1 %copy-start.9 = (s32[1,1,8]{2,1,0:T(1,128)S(1)}, s32[1,1,8]{2,1,0:T(1,128)}, u32[]{:S(2)}) copy-start(s32[1,1,8]{2,1,0:T(1,128)} %param.8) | copy-start | bytes 100
  0.6 32.1 %copy-start.7 = (s32[1,1,8]{2,1,0:T(1,128)S(1)}, s32[1,1,8]{2,1,0:T(1,128)}, u32[]{:S(2)}) copy-start(s32[1,1,8]{2,1,0:T(1,128)} %param.7) | copy-start | bytes 100
  0.7 2.2 %copy-start = (bf16[1,1,8,512,512]{4,3,2,1,0:T(8,128)(2,1)S(1)}, bf16[1,1,8,512,512]{4,3,2,1,0:T(8,128)(2,1)}, u32[]{:S(2)}) copy-start(bf16[1,1,8,512,512]{4,3,2,1,0:T(8,128)(2,1)} %param.6) | copy-start | bytes 12582916
  2.9 0.9 copy-start.3
  3.8 0.7 copy-start.6
  4.4 0.7 copy-start.8
  5.1 12.4 %copy-start.10 = (f32[2048]{0:T(1024)S(1)}, f32[2048]{0:T(1024)}, u32[]{:S(2)}) copy-start(f32[2048]{0:T(1024)} %param.10) | copy-start | bytes 24580
  7.1 88.3 %copy-start.4 = (bf16[2048,32]{0,1:T(8,128)(2,1)S(1)}, bf16[2048,32]{0,1:T(8,128)(2,1)}, u32[]{:S(2)}) copy-start(bf16[2048,32]{0,1:T(8,128)(2,1)} %param.9) | copy-start | bytes 393220
  7.1 88.3 %copy-start.5 = (f32[2048]{0:T(1024)S(1)}, f32[2048]{0:T(1024)}, u32[]{:S(2)}) copy-start(f32[2048]{0:T(1024)} %param.11) | copy-start | bytes 24580
  7.1 16.8 %all-to-all-start = ((f32[8,32,256]{2,1,0:T(8,128)}), f32[8,32,256]{2,1,0:T(8,128)S(1)}, u32[]{:S(2)}, u32[]{:S(2)}) async-start(f32[8,32,256]{2,1,0:T(8,128)} %sketch_cols.1), calls=%async_computation | async-start | bytes 524288 | tf_op jit(solution)/shard_map/sketch_cols/all_to_all | solution.py:286
  32.7 2.2 %copy-start.1 = (bf16[1,1,8,512,512]{4,3,2,1,0:T(8,128)(2,1)S(1)}, bf16[1,1,8,512,512]{4,3,2,1,0:T(8,128)(2,1)}, u32[]{:S(2)}) copy-start(bf16[1,1,8,512,512]{4,3,2,1,0:T(8,128)(2,1)} %param.6) | copy-start | bytes 12582916
  34.9 60.6 %copy-start.2 = (bf16[1,1,8,512,512]{4,3,2,1,0:T(8,128)(2,1)S(1)}, bf16[1,1,8,512,512]{4,3,2,1,0:T(8,128)(2,1)}, u32[]{:S(2)}) copy-start(bf16[1,1,8,512,512]{4,3,2,1,0:T(8,128)(2,1)} %param.6) | copy-start | bytes 12582916
  125.9 19.7 %all-to-all-start.6 = ((f32[64,2,128]{2,1,0:T(2,128)}), f32[64,2,128]{2,1,0:T(2,128)S(1)}, u32[]{:S(2)}, u32[]{:S(2)}) async-start(f32[64,2,128]{2,1,0:T(2,128)} %bitcast.9), calls=%async_computation.6 | async-start | bytes 131072 | tf_op jit(solution)/shard_map/image/all_to_all | solution.py:286

commit v2 on v1

v2 whole, which is shorter than its diff:
```python
import jax
import jax.numpy as jnp
from jax import lax
from jax.experimental import pallas as pl
from jax.experimental.pallas import tpu as pltpu
from jax.sharding import PartitionSpec as P

precond_shift = 1.0
regularize = 0.5

F32 = jnp.float32
BF16 = jnp.bfloat16
HIGHEST = lax.Precision.HIGHEST
LANES = 128
CORES = 2
X_PARTS = 4
Y_PARTS = 4
Z_PARTS = 16
COL_PARTS = Y_PARTS * Z_PARTS
BLOCKS = 8
ORDER = 512
LOCAL = 2048
WIDTH = 32
HALF = LOCAL // CORES
HALF_TILES = HALF // LANES
TILES = LOCAL // LANES
GROUPS = WIDTH // 8
IMAGE_TILES = GROUPS * HALF_TILES + 1
SENT_TILES = IMAGE_TILES + 3
VMEM_LIMIT = 24 * 1024 * 1024

NT = (((1,), (1,)), ((), ()))


def vmem():
    return pl.BlockSpec(memory_space=pltpu.VMEM)


def hbm():
    return pl.BlockSpec(memory_space=pltpu.HBM)


def smem():
    return pl.BlockSpec(memory_space=pltpu.SMEM)


def iota(shape, axis):
    return lax.broadcasted_iota(jnp.int32, shape, axis)


def call(body, in_specs, out_shape, scratch=(), flops=0, name=None):
    out_specs = jax.tree.map(lambda _: vmem(), out_shape)
    return pl.pallas_call(
        body,
        in_specs=in_specs,
        out_specs=out_specs,
        out_shape=out_shape,
        scratch_shapes=list(scratch),
        compiler_params=pltpu.CompilerParams(vmem_limit_bytes=VMEM_LIMIT),
        cost_estimate=pl.CostEstimate(flops=flops, bytes_accessed=1 << 20, transcendentals=0),
        name=name,
    )


def sketch_body(
    rows_hbm, cols_hbm, omega_hbm, blocks_hbm, out_ref, blocks_ref, rows_ref, cols_ref, omega_ref, sems
):
    copies = [
        pltpu.make_async_copy(rows_hbm, rows_ref, sems.at[0]),
        pltpu.make_async_copy(cols_hbm, cols_ref, sems.at[1]),
        pltpu.make_async_copy(omega_hbm, omega_ref, sems.at[2]),
    ]
    for n in range(BLOCKS):
        copies.append(pltpu.make_async_copy(blocks_hbm.at[n], blocks_ref.at[n], sems.at[3 + n]))
    for copy in copies:
        copy.start()
    out_ref[...] = jnp.zeros(out_ref.shape, F32)
    for copy in copies[:3]:
        copy.wait()
    for n in range(BLOCKS):
        copies[3 + n].wait()
        start = pl.multiple_of(rows_ref[0, n] * ORDER, ORDER)
        place = pl.multiple_of(cols_ref[0, n] % 2 * ORDER, ORDER)
        out_ref[cols_ref[0, n] // 2, :, pl.ds(place, ORDER)] += jnp.dot(
            omega_ref[:, pl.ds(start, ORDER)], blocks_ref[n], preferred_element_type=F32
        )


def pair_body(core_ref, parts_ref, out_ref):
    half = core_ref[0]
    total = (parts_ref[half] + parts_ref[CORES + half]).astype(BF16)
    for i in range(X_PARTS):
        out_ref[i] = total


def scale_body(core_ref, parts_ref, theta_ref, out_ref):
    total = parts_ref[0].astype(F32)
    for i in range(1, X_PARTS):
        total += parts_ref[i].astype(F32)
    out_ref[...] = (theta_ref[pl.ds(core_ref[0], 1), :] * total).astype(BF16)


def forward_body(rows_ref, cols_ref, scaled_ref, blocks_ref, out_ref):
    out_ref[...] = jnp.zeros(out_ref.shape, F32)
    for n in range(BLOCKS):
        place = pl.multiple_of(cols_ref[n] % 2 * ORDER, ORDER)
        left = scaled_ref[cols_ref[n] // 2, :, pl.ds(place, ORDER)]
        product = lax.dot_general(left, blocks_ref[n], NT, preferred_element_type=F32)
        first = rows_ref[n] * (ORDER // LANES)
        for g in range(GROUPS):
            for q in range(ORDER // LANES):
                out_ref[g, first + q] += product[8 * g : 8 * g + 8, LANES * q : LANES * (q + 1)]


def pack_square(square):
    packed = square[0:8]
    for g in range(1, GROUPS):
        packed += pltpu.roll(square[8 * g : 8 * g + 8], WIDTH * g, 1)
    return packed


def unpack_square(packed):
    lane = iota((8, LANES), 1)
    parts = [packed] + [pltpu.roll(packed, LANES - WIDTH * g, 1) for g in range(1, GROUPS)]
    return jnp.concatenate([jnp.where(lane < WIDTH, part, 0.0) for part in parts], axis=0)


def gram_body(
    rows_ref, cols_ref, tiles_ref, omega_ref, rhs_ref, blocks_ref, y_ref, out_ref, all_ref, cut_ref, acc_ref
):
    for g in range(GROUPS):
        for t in range(TILES):
            y_ref[8 * g : 8 * g + 8, LANES * t : LANES * (t + 1)] = tiles_ref[g, t]
    omega = omega_ref[...].astype(F32)
    ysketch = y_ref[...] + regularize * omega
    y_ref[...] = ysketch
    top = ysketch.astype(BF16)
    rest = ysketch - top.astype(F32)
    middle = rest.astype(BF16)
    low = (rest - middle.astype(F32)).astype(BF16)
    cut_ref[0:WIDTH, :] = top
    cut_ref[WIDTH : 2 * WIDTH, :] = middle
    cut_ref[2 * WIDTH : 3 * WIDTH, :] = low
    rhs = rhs_ref[...]
    rhs_top = rhs.astype(BF16).astype(F32)
    rhs_rest = rhs - rhs_top
    rhs_middle = rhs_rest.astype(BF16).astype(F32)
    rhs_low = rhs_rest - rhs_middle
    spot = iota((16, LOCAL), 0)
    rhs_cut = jnp.where(
        spot == 0, rhs_top, jnp.where(spot == 1, rhs_middle, jnp.where(spot == 2, rhs_low, 0.0))
    )
    cut_ref[3 * WIDTH :, :] = rhs_cut.astype(BF16)
    all_ref[0:WIDTH, :] = ysketch
    all_ref[WIDTH : 2 * WIDTH, :] = omega
    all_ref[2 * WIDTH :, :] = jnp.where(iota((LANES - 2 * WIDTH, LOCAL), 0) == 0, rhs, 0.0)

    products = lax.dot_general(
        all_ref[0 : 2 * WIDTH + 8, :], all_ref[...], NT, precision=HIGHEST, preferred_element_type=F32
    )
    lane = iota((WIDTH, LANES), 1)
    upper = products[0:WIDTH]
    middle = products[WIDTH : 2 * WIDTH]
    cross = jnp.where(lane < WIDTH, 0.5 * (middle + pltpu.roll(upper, LANES - WIDTH, 1)), 0.0)
    gram = jnp.where(lane < WIDTH, upper, 0.0) + precond_shift * cross
    out_ref[CORES * IMAGE_TILES] = pack_square(gram)
    out_ref[CORES * IMAGE_TILES + 1] = pack_square(cross)
    out_ref[CORES * IMAGE_TILES + 2] = products[2 * WIDTH :]

    acc_ref[...] = jnp.zeros(acc_ref.shape, F32)
    for n in range(BLOCKS):
        start = pl.multiple_of(rows_ref[n] * ORDER, ORDER)
        acc_ref[cols_ref[n]] += jnp.dot(
            cut_ref[:, pl.ds(start, ORDER)], blocks_ref[n], preferred_element_type=F32
        )
    spot = iota((8, LANES), 0)
    per_block = ORDER // LANES
    for h in range(CORES):
        rhs_tile = jnp.zeros((8, LANES), F32)
        for t in range(HALF_TILES):
            j = h * (HALF_TILES // per_block) + t // per_block
            at = LANES * (t % per_block)
            for g in range(GROUPS):
                out_ref[h * IMAGE_TILES + g * HALF_TILES + t] = acc_ref[
                    j, 8 * g : 8 * g + 8, at : at + LANES
                ] + (
                    acc_ref[j, WIDTH + 8 * g : WIDTH + 8 * g + 8, at : at + LANES]
                    + acc_ref[j, 2 * WIDTH + 8 * g : 2 * WIDTH + 8 * g + 8, at : at + LANES]
                )
            line = jnp.sum(acc_ref[j, 3 * WIDTH :, at : at + LANES], axis=0, keepdims=True)
            rhs_tile = jnp.where(spot == t, line, rhs_tile)
        out_ref[h * IMAGE_TILES + IMAGE_TILES - 1] = rhs_tile


def pair_image_body(core_ref, parts_ref, out_ref):
    first = core_ref[0] * IMAGE_TILES
    for k in range(SENT_TILES):
        at = first + k if k < IMAGE_TILES else (CORES - 1) * IMAGE_TILES + k
        tile = parts_ref[0, at] + parts_ref[1, at]
        for i in range(X_PARTS):
            out_ref[i, k] = tile


def to_column(row, shift):
    lane = iota((WIDTH, LANES), 1)
    return jnp.sum(
        jnp.where(lane == iota((WIDTH, LANES), 0) + shift, row, 0.0), axis=1, keepdims=True
    )


def to_row(column, shift):
    lane = iota((WIDTH, LANES), 1)
    return jnp.sum(
        jnp.where(lane == iota((WIDTH, LANES), 0) + shift, column, 0.0), axis=0, keepdims=True
    )


def solve_gram(inverse, diagonal, row):
    half = jnp.sum(inverse * pltpu.roll(row, WIDTH, 1), axis=1, keepdims=True) / diagonal
    return jnp.sum(inverse * half, axis=0, keepdims=True)


def factor_body(core_ref, parts_ref, theta_ref, out_ref, keep_ref, sum_ref):
    sum_ref[...] = (parts_ref[0] + parts_ref[1]) + (parts_ref[2] + parts_ref[3])
    gram = unpack_square(sum_ref[IMAGE_TILES])
    cross = unpack_square(sum_ref[IMAGE_TILES + 1])
    tail = sum_ref[IMAGE_TILES + 2]
    lane = iota((WIDTH, LANES), 1)
    spot = iota((WIDTH, LANES), 0)
    work = jnp.where(lane == spot + WIDTH, 1.0, gram)
    for k in range(WIDTH - 1):
        pivot = work[k : k + 1, :]
        scaled_pivot = pivot / pivot[:, k : k + 1]
        work = work - jnp.where(spot > k, work[:, k : k + 1], 0.0) * scaled_pivot
    diagonal = jnp.sum(jnp.where(lane == spot, work, 0.0), axis=1, keepdims=True)
    inverse = jnp.where((lane >= WIDTH) & (lane < 2 * WIDTH), work, 0.0)

    sketched_rhs = jnp.where(iota((1, LANES), 1) < WIDTH, tail[0:1], 0.0)
    coeffs = solve_gram(inverse, diagonal, sketched_rhs)
    column = to_column(coeffs, WIDTH)
    crossed = jnp.sum(cross * column, axis=0, keepdims=True)

    row = iota((8, LANES), 0)
    image = sum_ref[IMAGE_TILES - 1]
    for t in range(HALF_TILES):
        part = sum_ref[t] * column[0:8]
        for g in range(1, GROUPS):
            part += sum_ref[g * HALF_TILES + t] * column[8 * g : 8 * g + 8]
        image -= jnp.where(row == t, jnp.sum(part, axis=0, keepdims=True), 0.0)
    scaled = (theta_ref[core_ref[0]] * image).astype(BF16).astype(F32)
    groups = []
    for g in range(GROUPS):
        part = sum_ref[g * HALF_TILES] * scaled[0:1]
        for t in range(1, HALF_TILES):
            part += sum_ref[g * HALF_TILES + t] * scaled[t : t + 1]
        groups.append(jnp.sum(part, axis=1, keepdims=True))
    sketched = to_row(jnp.concatenate(groups, axis=0), 0)
    curvature = jnp.sum(jnp.sum(image * scaled, axis=0, keepdims=True), axis=1, keepdims=True)
    out_ref[0] = scaled
    out_ref[1] = jnp.where(
        row == 0, jnp.where(iota((8, LANES), 1) == WIDTH, curvature, sketched), 0.0
    )
    keep_ref[0:WIDTH, :] = inverse
    keep_ref[WIDTH : 2 * WIDTH, :] = jnp.broadcast_to(diagonal, (WIDTH, LANES))
    keep_ref[2 * WIDTH : 2 * WIDTH + 8, :] = tail
    keep_ref[2 * WIDTH + 8 : 2 * WIDTH + 16, :] = jnp.broadcast_to(coeffs, (8, LANES))
    keep_ref[2 * WIDTH + 16 :, :] = jnp.broadcast_to(crossed, (8, LANES))


def image_body(rows_ref, cols_ref, parts_ref, blocks_ref, out_ref, scaled_ref, acc_ref):
    sums = parts_ref[0, 1, 0:1, :] + parts_ref[1, 1, 0:1, :]
    per_block = ORDER // LANES
    for j in range(LOCAL // ORDER):
        h, first = j // 2, j % 2 * per_block
        line = jnp.concatenate(
            [parts_ref[h, 0, first + q : first + q + 1, :] for q in range(per_block)], axis=1
        )
        scaled_ref[j] = jnp.broadcast_to(line, (16, ORDER)).astype(BF16)
    acc_ref[...] = jnp.zeros(acc_ref.shape, F32)
    for n in range(BLOCKS):
        product = lax.dot_general(
            scaled_ref[cols_ref[n]], blocks_ref[n], NT, preferred_element_type=F32
        )
        acc_ref[rows_ref[n]] += product[0:8]
    even = iota((8, LANES), 0) % 2 == 0
    for t in range(TILES):
        at = LANES * (t % per_block)
        out_ref[8 * t : 8 * t + 8, :] = jnp.where(
            even, acc_ref[t // per_block, :, at : at + LANES], sums
        )


def step_body(me_ref, parts_ref, keep_ref, y_ref, rhs_ref, out_ref):
    total = parts_ref[0:8, :]
    for i in range(1, COL_PARTS // 4):
        total += parts_ref[8 * i : 8 * i + 8, :]
    even = iota((8, LANES), 0) % 2 == 0
    image_rows = jnp.sum(jnp.where(even, total, 0.0), axis=0, keepdims=True)
    sums = jnp.sum(jnp.where(even, 0.0, total), axis=0, keepdims=True)

    lane = iota((1, LANES), 1)
    first = lane < WIDTH
    inverse = keep_ref[0:WIDTH, :]
    diagonal = keep_ref[WIDTH : 2 * WIDTH, 0:1]
    tail = keep_ref[2 * WIDTH : 2 * WIDTH + 1, :]
    coeffs = keep_ref[2 * WIDTH + 8 : 2 * WIDTH + 9, :]
    crossed = keep_ref[2 * WIDTH + 16 : 2 * WIDTH + 17, :]
    sketched_rhs = jnp.where(first, tail, 0.0)
    square = jnp.sum(jnp.where(lane == 2 * WIDTH, tail, 0.0), axis=1, keepdims=True)
    along = square - jnp.sum(pltpu.roll(sketched_rhs, WIDTH, 1) * coeffs, axis=1, keepdims=True)
    length = along - jnp.sum(pltpu.roll(crossed, WIDTH, 1) * coeffs, axis=1, keepdims=True)
    curvature = jnp.sum(jnp.where(lane == WIDTH, sums, 0.0), axis=1, keepdims=True) + regularize * length
    alpha = along / curvature

    start = pl.multiple_of((me_ref[0] // 4) * LANES, LANES)
    ysketch = y_ref[:, pl.ds(start, LANES)]
    rhs = rhs_ref[:, pl.ds(start, LANES)]
    direction = (rhs - jnp.sum(ysketch * to_column(coeffs, WIDTH), axis=0, keepdims=True)) / precond_shift
    image = image_rows + regularize * direction
    residual = rhs - alpha * image
    sketched_image = jnp.where(first, sums, 0.0) + regularize * crossed
    sketched_res = sketched_rhs - alpha * sketched_image
    res_coeffs = solve_gram(inverse, diagonal, sketched_res)
    precond_residual = (
        residual - jnp.sum(ysketch * to_column(res_coeffs, WIDTH), axis=0, keepdims=True)
    ) / precond_shift
    which = iota((8, LANES), 0)
    pack = jnp.where(
        which == 0, alpha * direction, jnp.where(which == 1, residual, precond_residual)
    )
    out_ref[...] = pltpu.roll(pack, ((4 - me_ref[0] % 4) % 4) * WIDTH, 1)


def exchange(value, axis):
    return lax.all_to_all(value, axis, 0, 0, tiled=True)


def copies(value, count):
    return jnp.broadcast_to(value[None], (count,) + value.shape)


def shards(blocks, block_rows, block_cols, sketch, theta, rhs):
    values = blocks[0, 0]
    rows_idx = block_rows[0, 0]
    cols_idx = block_cols[0, 0]
    omega = sketch.T
    rhs_line = rhs.reshape(1, LOCAL)
    my_core = lax.axis_index("core").astype(jnp.int32).reshape(1)
    my_col = lax.axis_index(("y", "z")).astype(jnp.int32).reshape(1)
    shape = jax.ShapeDtypeStruct
    work = 2 * BLOCKS * ORDER * ORDER

    with jax.named_scope("sketch_cols"):
        terms, values = call(
            sketch_body,
            [hbm(), hbm(), hbm(), hbm()],
            (shape((CORES, WIDTH, HALF), F32), shape(values.shape, BF16)),
            scratch=[
                pltpu.SMEM((1, BLOCKS), jnp.int32),
                pltpu.SMEM((1, BLOCKS), jnp.int32),
                pltpu.VMEM((WIDTH, LOCAL), BF16),
                pltpu.SemaphoreType.DMA((3 + BLOCKS,)),
            ],
            flops=work * WIDTH,
            name="sketch_cols",
        )(block_rows[0], block_cols[0], omega, values)
        parts = lax.all_gather(terms, "core", tiled=True)
        parts = call(
            pair_body, [smem(), vmem()], shape((X_PARTS, WIDTH, HALF), BF16), name="pair"
        )(my_core, parts)
        parts = exchange(parts, "x")
    with jax.named_scope("scaled"):
        scaled = call(
            scale_body, [smem(), vmem(), vmem()], shape((WIDTH, HALF), BF16), name="scaled"
        )(my_core, parts, theta.reshape(CORES, HALF))
        scaled = lax.all_gather(scaled, "core")
    with jax.named_scope("ysketch"):
        terms = call(
            forward_body,
            [smem(), smem(), vmem(), vmem()],
            shape((GROUPS, TILES, 8, LANES), F32),
            flops=work * WIDTH,
            name="ysketch",
        )(rows_idx, cols_idx, scaled, values)
        parts = jnp.sum(exchange(terms, "y"), axis=0)
        parts = jnp.sum(exchange(parts, "z"), axis=0)
        parts = exchange(copies(parts, Z_PARTS), "z")
        tiles = exchange(copies(parts, Y_PARTS), "y")
    with jax.named_scope("gram"):
        ysketch, terms = call(
            gram_body,
            [smem(), smem(), vmem(), vmem(), vmem(), vmem()],
            (shape((WIDTH, LOCAL), F32), shape((CORES * IMAGE_TILES + 3, 8, LANES), F32)),
            scratch=[
                pltpu.VMEM((LANES, LOCAL), F32),
                pltpu.VMEM((3 * WIDTH + 16, LOCAL), BF16),
                pltpu.VMEM((LOCAL // ORDER, 3 * WIDTH + 16, ORDER), F32),
            ],
            flops=work * WIDTH * 3,
            name="gram",
        )(rows_idx, cols_idx, tiles, omega, rhs_line, values)
        parts = lax.all_gather(terms, "core")
        parts = call(
            pair_image_body,
            [smem(), vmem()],
            shape((X_PARTS, SENT_TILES, 8, LANES), F32),
            name="pair_image",
        )(my_core, parts)
        parts = exchange(parts, "x")
    with jax.named_scope("image_scaled"):
        terms, keep = call(
            factor_body,
            [smem(), vmem(), vmem()],
            (shape((2, 8, LANES), F32), shape((2 * WIDTH + 24, LANES), F32)),
            scratch=[pltpu.VMEM((SENT_TILES, 8, LANES), F32)],
            name="image_scaled",
        )(my_core, parts, theta.reshape(CORES, HALF_TILES, LANES))
        parts = lax.all_gather(terms, "core")
    with jax.named_scope("image"):
        terms = call(
            image_body,
            [smem(), smem(), vmem(), vmem()],
            shape((2 * COL_PARTS, LANES), F32),
            scratch=[
                pltpu.VMEM((LOCAL // ORDER, 16, ORDER), BF16),
                pltpu.VMEM((LOCAL // ORDER, 8, ORDER), F32),
            ],
            flops=work,
            name="image",
        )(rows_idx, cols_idx, parts, values)
        parts = exchange(terms.reshape(COL_PARTS, 2, LANES), ("y", "z")).reshape(2 * COL_PARTS, LANES)
    with jax.named_scope("step"):
        out = call(
            step_body,
            [smem(), vmem(), vmem(), vmem(), vmem()],
            shape((8, LANES), F32),
            name="step",
        )(my_col, parts, keep, ysketch, rhs_line)
    share = LOCAL // COL_PARTS
    return (out[0, :share], out[1, :share], out[2, :share])


def solution(mesh):
    row, col = ("x", "core"), ("y", "z")
    fine = jax.sharding.Mesh(
        mesh.devices.reshape(X_PARTS, CORES, Y_PARTS, Z_PARTS), ("x", "core", "y", "z")
    )
    in_specs = (
        P(row, col, None, None, None),
        P(row, col, None),
        P(row, col, None),
        P(row, None),
        P(col),
        P(row),
    )
    out_specs = (P(row + col), P(row + col), P(row + col))
    return jax.shard_map(shards, mesh=fine, in_specs=in_specs, out_specs=out_specs, check_vma=False)
```

time: 147 us -> 141 us (0.959)
  starting transfers between devices: 16.5 us -> 8 us
  local copies, waits for them, and re-layouts: 7.16 us -> 11.3 us
  blocking collectives: 90.5 us -> 87.9 us
    all_to_all x5, blocking collectives: 90.5 us -> 65.7 us  [exchange(): return lax.all_to_all(value, axis, 0, 0, tiled=True)]
    all_gather x0 -> x4, blocking collectives: none -> 22.2 us  [the longest x2 10.5 us: shards(): parts = lax.all_gather(terms, 'core')]
    all_to_all x2, starting transfers between devices: 16.5 us -> 8 us  [exchange(): return lax.all_to_all(value, axis, 0, 0, tiled=True)]
    unnamed x22 -> x26, local copies, waits for them, and re-layouts: 6.62 us -> 10.8 us
    pallas_call x5 -> x6, Pallas kernels: 6.85 us -> 7.81 us  [the longest x1 2.9 us: shards(): call(factor_body, [smem(), vmem(), vmem()], (shape((2, 8, LANES), F32), s...]
where the time goes in v2:
time: 141 us; the launch traced here: 140 us
  blocking collectives  87.9 us (62%)
  waiting for transfers between devices  19.6 us (14%)
  Pallas kernels  12.7 us (9%)
  local copies, waits for them, and re-layouts  11.3 us (8%)
  starting transfers between devices  8 us (6%)
    all_to_all x5, blocking collectives, exchange(): return lax.all_to_all(value, axis, 0, 0, tiled=True)  65.7 us
    all_to_all x2, waiting for transfers between devices, exchange(): return lax.all_to_all(value, axis, 0, 0, tiled=True)  19.6 us
    unnamed x26, local copies, waits for them, and re-layouts  10.8 us
    all_gather x2, blocking collectives, shards(): parts = lax.all_gather(terms, 'core')  10.5 us
    all_gather x1, blocking collectives, shards(): parts = lax.all_gather(terms, 'core', tiled=True)  8.67 us
    all_to_all x2, starting transfers between devices, exchange(): return lax.all_to_all(value, axis, 0, 0, tiled=True)  8 us
    all_gather x1, blocking collectives, shards(): scaled = lax.all_gather(scaled, 'core')  3.04 us
    pallas_call x1, Pallas kernels, shards(): call(factor_body, [smem(), vmem(), vmem()], (shape((2, 8, LANES), F32), s...  2.9 us
  transfers between devices with their start and end apart: 2, of which 2 were waited for; matrix products, arithmetic and copies ran while one was open for 0% of the time, Pallas kernels for 0%

profile of v2, /device:TPU:1, one launch (start us, length us, event | category | flops | bytes accessed | tf_op | source)
XLA Modules:
  0.0 140.3 jit_solution(40510029786360116)
XLA Ops:
  0.6 0.0 copy-start.10
  0.6 0.0 copy-start.12
  0.7 0.0 copy-start.8
  0.7 0.0 copy-start.4
  0.7 2.2 %copy-done.4 = bf16[1,1,8,512,512]{4,3,2,1,0:T(8,128)(2,1)S(1)} copy-done((bf16[1,1,8,512,512]{4,3,2,1,0:T(8,128)(2,1)S(1)}, bf16[1,1,8,512,512]{4,3,2,1,0:T(8,128)(2,1)}, u32[]{:S(2)}) %copy-start.4) | copy-done | bytes 4194328
  2.9 0.0 copy-start.5
  2.9 0.9 copy-done.5
  3.8 0.0 copy-start.9
  3.8 0.7 copy-done.9
  4.4 0.0 copy-start.11
  4.4 0.7 copy-done.11
  5.1 2.2 %sketch_cols.1 = (f32[2,32,1024]{2,1,0:T(8,128)S(1)}, bf16[8,512,512]{2,1,0:T(8,128)(2,1)S(1)}) custom-call(s32[1,8]{1,0:T(1,128)S(1)} %bitcast.31, s32[1,8]{1,0:T(1,128)S(1)} %bitcast.35, bf16[32,2048]{1,0:T(8,128)(2,1)S(1)} %bitcast.23, bf16[8,512,512]{2,1,0:T(8,128)(2,1)S(1)} %bitcast.21), custom_call_target="tpu_custom_call" | custom-call | flops 134217728 | bytes 1048576 | tf_op jit(solution)/shard_map/sketch_cols/sketch_cols/pallas_call | solution.py:354
  7.3 0.0 copy-start
  7.4 1.9 %copy-done = bf16[8,512,512]{2,1,0:T(8,128)(2,1)} copy-done((bf16[8,512,512]{2,1,0:T(8,128)(2,1)}, bf16[8,512,512]{2,1,0:T(8,128)(2,1)S(1)}, u32[]{:S(2)}) %copy-start) | copy-done | bytes 4194328
  9.3 8.7 %all_gather.21.parts_ref = f32[4,32,1024]{2,1,0:T(8,128)S(1)} all-gather(f32[2,32,1024]{2,1,0:T(8,128)S(1)} %get-tuple-element.9), channel_id=1, replica_groups=mesh['x'=4,'core'=2,'y'=4,'z'=16] {'core'}, dimensions={0}, use_global_device_ids=true | all-gather | bytes 786432 | tf_op jit(solution)/shard_map/sketch_cols/all_gather | solution.py:367
  18.0 0.0 copy-start.6
  18.0 0.0 copy-start.7
  18.0 0.7 pair.1
  18.7 3.4 %all-to-all-start = ((bf16[4,32,1024]{2,1,0:T(8,128)(2,1)}), bf16[4,32,1024]{2,1,0:T(8,128)(2,1)S(1)}, u32[]{:S(2)}, u32[]{:S(2)}) async-start(bf16[4,32,1024]{2,1,0:T(8,128)(2,1)} %pair.1), calls=%async_computation | async-start | bytes 524288 | tf_op jit(solution)/shard_map/sketch_cols/all_to_all | solution.py:335
  22.1 0.0 copy-done.8
  22.1 6.1 %all-to-all-done.parts_ref = bf16[4,32,1024]{2,1,0:T(8,128)(2,1)S(1)} async-done(((bf16[4,32,1024]{2,1,0:T(8,128)(2,1)}), bf16[4,32,1024]{2,1,0:T(8,128)(2,1)S(1)}, u32[]{:S(2)}, u32[]{:S(2)}) %all-to-all-start) | async-done | bytes 262176 | tf_op jit(solution)/shard_map/sketch_cols/all_to_all | solution.py:335
  28.2 3.0 %all-gather = bf16[64,1024]{1,0:T(8,128)(2,1)S(1)} all-gather(bf16[32,1024]{1,0:T(8,128)(2,1)S(1)} %scaled.1), channel_id=2, replica_groups=mesh['x'=4,'core'=2,'y'=4,'z'=16] {'core'}, dimensions={0}, use_global_device_ids=true | all-gather | bytes 196608 | tf_op jit(solution)/shard_map/scaled/all_gather | solution.py:376
  31.3 0.0 copy-done.10
  31.3 0.0 copy-done.12
  31.3 0.0 copy-start.1
  31.3 2.2 %copy-done.1 = bf16[8,512,512]{2,1,0:T(8,128)(2,1)S(1)} copy-done((bf16[8,512,512]{2,1,0:T(8,128)(2,1)S(1)}, bf16[8,512,512]{2,1,0:T(8,128)(2,1)}, u32[]{:S(2)}) %copy-start.1) | copy-done | bytes 4194328
  33.5 1.9 %ysketch.1 = f32[4,16,8,128]{3,2,1,0:T(8,128)S(1)} custom-call(s32[8]{0:T(128)S(1)} %bitcast.32, s32[8]{0:T(128)S(1)} %bitcast.36, bf16[2,32,1024]{2,1,0:T(8,128)(2,1)S(1)} %bitcast.25, bf16[8,512,512]{2,1,0:T(8,128)(2,1)S(1)} %copy-done.1), custom_call_target="tpu_custom_call" | custom-call | flops 134217728 | bytes 1048576 | tf_op jit(solution)/shard_map/ysketch/ysketch/pallas_call | solution.py:378
  35.3 8.8 %all_to_all.35 = f32[4,16,8,128]{3,2,1,0:T(8,128)S(1)} all-to-all(f32[4,16,8,128]{3,2,1,0:T(8,128)S(1)} %ysketch.1), channel_id=1, replica_groups=mesh['x'=4,'core'=2,'y'=4,'z'=16] {'y'}, dimensions={0} | all-to-all | bytes 524288 | tf_op jit(solution)/shard_map/ysketch/all_to_all | solution.py:335
  44.2 22.5 %all_to_all.36 = f32[16,8,128]{2,1,0:T(8,128)S(1)} all-to-all(f32[16,8,128]{2,1,0:T(8,128)S(1)} %reduce_sum.18), channel_id=1, replica_groups=mesh['x'=4,'core'=2,'y'=4,'z'=16] {'z'}, dimensions={0} | all-to-all | bytes 131072 | tf_op jit(solution)/shard_map/ysketch/all_to_all | solution.py:335
  66.8 14.4 %all_to_all.37 = f32[16,8,128]{2,1,0:T(8,128)S(1)} all-to-all(f32[16,8,128]{2,1,0:T(8,128)S(1)} %broadcast_in_dim.4), channel_id=1, replica_groups=mesh['x'=4,'core'=2,'y'=4,'z'=16] {'z'}, dimensions={0} | all-to-all | bytes 131072 | tf_op jit(solution)/shard_map/ysketch/all_to_all | solution.py:335
  81.2 7.9 %all_to_all.38.tiles_ref = f32[4,16,8,128]{3,2,1,0:T(8,128)S(1)} all-to-all(f32[4,16,8,128]{3,2,1,0:T(8,128)S(1)} %broadcast_in_dim.5), channel_id=1, replica_groups=mesh['x'=4,'core'=2,'y'=4,'z'=16] {'y'}, dimensions={0} | all-to-all | bytes 524288 | tf_op jit(solution)/shard_map/ysketch/all_to_all | solution.py:335
  89.1 0.0 copy-done.6
  89.1 0.0 copy-done.7
  89.1 0.0 copy-start.2
  89.1 2.2 %copy-done.2 = bf16[8,512,512]{2,1,0:T(8,128)(2,1)S(1)} copy-done((bf16[8,512,512]{2,1,0:T(8,128)(2,1)S(1)}, bf16[8,512,512]{2,1,0:T(8,128)(2,1)}, u32[]{:S(2)}) %copy-start.2) | copy-done | bytes 4194328
  91.3 0.0 copy-start.3
  91.3 2.0 %gram.1 = (f32[32,2048]{1,0:T(8,128)S(1)}, f32[69,8,128]{2,1,0:T(8,128)S(1)}) custom-call(s32[8]{0:T(128)S(1)} %bitcast.33, s32[8]{0:T(128)S(1)} %bitcast.37, f32[4,16,8,128]{3,2,1,0:T(8,128)S(1)} %all_to_all.38.tiles_ref, bf16[32,2048]{1,0:T(8,128)(2,1)S(1)} %bitcast.24, f32[1,2048]{1,0:T(1,128)S(1)} %bitcast.28, bf16[8,512,512]{2,1,0:T(8,128)(2,1)S(1)} %copy-done.2), custom_call_target="tpu_custom_call" | custom-call | flops 402653184 | bytes 1048576 | tf_op jit(solution)/shard_map/gram/gram/pallas_call | solution.py:390
  93.3 7.5 %all-gather.1 = f32[138,8,128]{2,1,0:T(8,128)S(1)} all-gather(f32[69,8,128]{2,1,0:T(8,128)S(1)} %get-tuple-element.11), channel_id=3, replica_groups=mesh['x'=4,'core'=2,'y'=4,'z'=16] {'core'}, dimensions={0}, use_global_device_ids=true | all-gather | bytes 847872 | tf_op jit(solution)/shard_map/gram/all_gather | solution.py:402
  100.8 12.0 %all_to_all.39.parts_ref = f32[4,36,8,128]{3,2,1,0:T(8,128)S(1)} all-to-all(f32[4,36,8,128]{3,2,1,0:T(8,128)S(1)} %pair_image.1), channel_id=1, replica_groups=mesh['x'=4,'core'=2,'y'=4,'z'=16] {'x'}, dimensions={0} | all-to-all | bytes 1179648 | tf_op jit(solution)/shard_map/gram/all_to_all | solution.py:335
  112.8 2.9 %image_scaled.1 = (f32[2,8,128]{2,1,0:T(8,128)S(1)}, f32[88,128]{1,0:T(8,128)S(1)}) custom-call(s32[1]{0:T(128)} %bitcast.3.core_ref, f32[4,36,8,128]{3,2,1,0:T(8,128)S(1)} %all_to_all.39.parts_ref, f32[2,8,128]{2,1,0:T(8,128)S(1)} %bitcast.30), custom_call_target="tpu_custom_call" | custom-call | bytes 1048576 | tf_op jit(solution)/shard_map/image_scaled/image_scaled/pallas_call | solution.py:411
  115.7 3.0 %all-gather.2 = f32[4,8,128]{2,1,0:T(8,128)S(1)} all-gather(f32[2,8,128]{2,1,0:T(8,128)S(1)} %get-tuple-element.12), channel_id=4, replica_groups=mesh['x'=4,'core'=2,'y'=4,'z'=16] {'core'}, dimensions={0}, use_global_device_ids=true | all-gather | bytes 24576 | tf_op jit(solution)/shard_map/image_scaled/all_gather | solution.py:418
  118.7 0.0 copy-done.3
  118.7 2.4 %image.1 = f32[128,128]{1,0:T(8,128)} custom-call(s32[8]{0:T(128)S(1)} %bitcast.34, s32[8]{0:T(128)S(1)} %bitcast.38, f32[2,2,8,128]{3,2,1,0:T(8,128)S(1)} %bitcast.27, bf16[8,512,512]{2,1,0:T(8,128)(2,1)S(1)} %copy-done.3), custom_call_target="tpu_custom_call" | custom-call | flops 4194304 | bytes 1048576 | tf_op jit(solution)/shard_map/image/image/pallas_call | solution.py:420
  121.1 4.6 %all-to-all-start.6 = ((f32[64,2,128]{2,1,0:T(2,128)}), f32[64,2,128]{2,1,0:T(2,128)S(1)}, u32[]{:S(2)}, u32[]{:S(2)}) async-start(f32[64,2,128]{2,1,0:T(2,128)} %bitcast.13), calls=%async_computation.6 | async-start | bytes 131072 | tf_op jit(solution)/shard_map/image/all_to_all | solution.py:335
  125.7 13.5 %all-to-all-done.6 = f32[64,2,128]{2,1,0:T(2,128)S(1)} async-done(((f32[64,2,128]{2,1,0:T(2,128)}), f32[64,2,128]{2,1,0:T(2,128)S(1)}, u32[]{:S(2)}, u32[]{:S(2)}) %all-to-all-start.6) | async-done | bytes 65568 | tf_op jit(solution)/shard_map/image/all_to_all | solution.py:335
  139.2 0.5 step.1
  139.8 0.5 slice_bitcast_fusion
  (7 shorter events, 0.2 us)
Async XLA Ops:
  0.6 30.7 %copy-start.10 = (s32[1,1,8]{2,1,0:T(1,128)S(1)}, s32[1,1,8]{2,1,0:T(1,128)}, u32[]{:S(2)}) copy-start(s32[1,1,8]{2,1,0:T(1,128)} %param.7) | copy-start | bytes 100
  0.6 30.7 %copy-start.12 = (s32[1,1,8]{2,1,0:T(1,128)S(1)}, s32[1,1,8]{2,1,0:T(1,128)}, u32[]{:S(2)}) copy-start(s32[1,1,8]{2,1,0:T(1,128)} %param.8) | copy-start | bytes 100
  0.7 21.5 %copy-start.8 = (f32[2048]{0:T(1024)S(1)}, f32[2048]{0:T(1024)}, u32[]{:S(2)}) copy-start(f32[2048]{0:T(1024)} %param.10) | copy-start | bytes 24580
  0.7 2.2 %copy-start.4 = (bf16[1,1,8,512,512]{4,3,2,1,0:T(8,128)(2,1)S(1)}, bf16[1,1,8,512,512]{4,3,2,1,0:T(8,128)(2,1)}, u32[]{:S(2)}) copy-start(bf16[1,1,8,512,512]{4,3,2,1,0:T(8,128)(2,1)} %param.6) | copy-start | bytes 12582916
  2.9 0.9 copy-start.5
  3.8 0.7 copy-start.9
  4.4 0.7 copy-start.11
  7.3 2.0 %copy-start = (bf16[8,512,512]{2,1,0:T(8,128)(2,1)}, bf16[8,512,512]{2,1,0:T(8,128)(2,1)S(1)}, u32[]{:S(2)}) copy-start(bf16[8,512,512]{2,1,0:T(8,128)(2,1)S(1)} %get-tuple-element.10.blocks_ref) | copy-start | bytes 12582916
  18.0 71.1 %copy-start.6 = (bf16[2048,32]{0,1:T(8,128)(2,1)S(1)}, bf16[2048,32]{0,1:T(8,128)(2,1)}, u32[]{:S(2)}) copy-start(bf16[2048,32]{0,1:T(8,128)(2,1)} %param.9) | copy-start | bytes 393220
  18.0 71.1 %copy-start.7 = (f32[2048]{0:T(1024)S(1)}, f32[2048]{0:T(1024)}, u32[]{:S(2)}) copy-start(f32[2048]{0:T(1024)} %param.11) | copy-start | bytes 24580
  18.7 9.5 %all-to-all-start = ((bf16[4,32,1024]{2,1,0:T(8,128)(2,1)}), bf16[4,32,1024]{2,1,0:T(8,128)(2,1)S(1)}, u32[]{:S(2)}, u32[]{:S(2)}) async-start(bf16[4,32,1024]{2,1,0:T(8,128)(2,1)} %pair.1), calls=%async_computation | async-start | bytes 524288 | tf_op jit(solution)/shard_map/sketch_cols/all_to_all | solution.py:335
  31.3 2.2 %copy-start.1 = (bf16[8,512,512]{2,1,0:T(8,128)(2,1)S(1)}, bf16[8,512,512]{2,1,0:T(8,128)(2,1)}, u32[]{:S(2)}) copy-start(bf16[8,512,512]{2,1,0:T(8,128)(2,1)} %copy-done) | copy-start | bytes 12582916
  89.1 2.2 %copy-start.2 = (bf16[8,512,512]{2,1,0:T(8,128)(2,1)S(1)}, bf16[8,512,512]{2,1,0:T(8,128)(2,1)}, u32[]{:S(2)}) copy-start(bf16[8,512,512]{2,1,0:T(8,128)(2,1)} %copy-done) | copy-start | bytes 12582916
  91.3 27.4 %copy-start.3 = (bf16[8,512,512]{2,1,0:T(8,128)(2,1)S(1)}, bf16[8,512,512]{2,1,0:T(8,128)(2,1)}, u32[]{:S(2)}) copy-start(bf16[8,512,512]{2,1,0:T(8,128)(2,1)} %copy-done) | copy-start | bytes 12582916
  121.1 18.1 %all-to-all-start.6 = ((f32[64,2,128]{2,1,0:T(2,128)}), f32[64,2,128]{2,1,0:T(2,128)S(1)}, u32[]{:S(2)}, u32[]{:S(2)}) async-start(f32[64,2,128]{2,1,0:T(2,128)} %bitcast.13), calls=%async_computation.6 | async-start | bytes 131072 | tf_op jit(solution)/shard_map/image/all_to_all | solution.py:335

commit v3 on v2

--- a/solution.py
+++ b/solution.py
@@ -28,6 +28,7 @@
 IMAGE_TILES = GROUPS * HALF_TILES + 1
 SENT_TILES = IMAGE_TILES + 3
 VMEM_LIMIT = 24 * 1024 * 1024
+FIRST_LIMIT = 64 * 1024 * 1024 - 64 * 1024
 
 NT = (((1,), (1,)), ((), ()))
 
@@ -48,7 +49,7 @@
     return lax.broadcasted_iota(jnp.int32, shape, axis)
 
 
-def call(body, in_specs, out_shape, scratch=(), flops=0, name=None):
+def call(body, in_specs, out_shape, scratch=(), flops=0, name=None, limit=VMEM_LIMIT):
     out_specs = jax.tree.map(lambda _: vmem(), out_shape)
     return pl.pallas_call(
         body,
@@ -56,29 +57,32 @@
         out_specs=out_specs,
         out_shape=out_shape,
         scratch_shapes=list(scratch),
-        compiler_params=pltpu.CompilerParams(vmem_limit_bytes=VMEM_LIMIT),
+        compiler_params=pltpu.CompilerParams(vmem_limit_bytes=limit),
         cost_estimate=pl.CostEstimate(flops=flops, bytes_accessed=1 << 20, transcendentals=0),
         name=name,
     )
 
 
 def sketch_body(
-    rows_hbm, cols_hbm, omega_hbm, blocks_hbm, out_ref, blocks_ref, rows_ref, cols_ref, omega_ref, sems
+    rows_hbm, cols_hbm, omega_hbm, blocks_hbm, out_ref, rows_ref, cols_ref, omega_ref, blocks_ref, sems
 ):
-    copies = [
-        pltpu.make_async_copy(rows_hbm, rows_ref, sems.at[0]),
-        pltpu.make_async_copy(cols_hbm, cols_ref, sems.at[1]),
-        pltpu.make_async_copy(omega_hbm, omega_ref, sems.at[2]),
+    first = [
+        pltpu.make_async_copy(rows_hbm, rows_ref, sems.at[BLOCKS]),
+        pltpu.make_async_copy(cols_hbm, cols_ref, sems.at[BLOCKS + 1]),
+        pltpu.make_async_copy(omega_hbm, omega_ref, sems.at[BLOCKS + 2]),
     ]
-    for n in range(BLOCKS):
-        copies.append(pltpu.make_async_copy(blocks_hbm.at[n], blocks_ref.at[n], sems.at[3 + n]))
-    for copy in copies:
+    for copy in first:
+        copy.start()
+    arrivals = [
+        pltpu.make_async_copy(blocks_hbm.at[n], blocks_ref.at[n], sems.at[n]) for n in range(BLOCKS)
+    ]
+    for copy in arrivals:
         copy.start()
     out_ref[...] = jnp.zeros(out_ref.shape, F32)
-    for copy in copies[:3]:
+    for copy in first:
         copy.wait()
     for n in range(BLOCKS):
-        copies[3 + n].wait()
+        arrivals[n].wait()
         start = pl.multiple_of(rows_ref[0, n] * ORDER, ORDER)
         place = pl.multiple_of(cols_ref[0, n] % 2 * ORDER, ORDER)
         out_ref[cols_ref[0, n] // 2, :, pl.ds(place, ORDER)] += jnp.dot(
@@ -88,16 +92,16 @@
 
 def pair_body(core_ref, parts_ref, out_ref):
     half = core_ref[0]
-    total = (parts_ref[half] + parts_ref[CORES + half]).astype(BF16)
+    total = parts_ref[0, half] + parts_ref[1, half]
     for i in range(X_PARTS):
         out_ref[i] = total
 
 
 def scale_body(core_ref, parts_ref, theta_ref, out_ref):
-    total = parts_ref[0].astype(F32)
-    for i in range(1, X_PARTS):
-        total += parts_ref[i].astype(F32)
-    out_ref[...] = (theta_ref[pl.ds(core_ref[0], 1), :] * total).astype(BF16)
+    total = (parts_ref[0] + parts_ref[1]) + (parts_ref[2] + parts_ref[3])
+    tile = theta_ref[core_ref[0]]
+    theta = jnp.concatenate([tile[t : t + 1, :] for t in range(HALF_TILES)], axis=1)
+    out_ref[...] = (theta * total).astype(BF16)
 
 
 def forward_body(rows_ref, cols_ref, scaled_ref, blocks_ref, out_ref):
@@ -112,6 +116,23 @@
                 out_ref[g, first + q] += product[8 * g : 8 * g + 8, LANES * q : LANES * (q + 1)]
 
 
+def gather_body(parts_ref, out_ref):
+    out_ref[...] = (parts_ref[0] + parts_ref[1]) + (parts_ref[2] + parts_ref[3])
+
+
+def copy_body(part_ref, out_ref):
+    for i in range(Y_PARTS):
+        out_ref[i] = part_ref[...]
+
+
+def spread_body(parts_ref, out_ref):
+    sums = [parts_ref[i] for i in range(Z_PARTS)]
+    while len(sums) > 1:
+        sums = [a + b for a, b in zip(sums[::2], sums[1::2])]
+    for i in range(Z_PARTS):
+        out_ref[i] = sums[0]
+
+
 def pack_square(square):
     packed = square[0:8]
     for g in range(1, GROUPS):
@@ -126,7 +147,17 @@
 
 
 def gram_body(
-    rows_ref, cols_ref, tiles_ref, omega_ref, rhs_ref, blocks_ref, y_ref, out_ref, all_ref, cut_ref, acc_ref
+    rows_ref,
+    cols_ref,
+    tiles_ref,
+    omega_ref,
+    rhs_ref,
+    blocks_ref,
+    y_ref,
+    out_ref,
+    all_ref,
+    cut_ref,
+    acc_ref,
 ):
     for g in range(GROUPS):
         for t in range(TILES):
@@ -215,6 +246,31 @@
     )
 
 
+def eliminate(work, panel):
+    spot = iota((WIDTH, LANES), 0)
+    for k in range(0, WIDTH, panel):
+        rows = [work[k + i : k + i + 1, :] for i in range(panel)]
+        columns = [jnp.broadcast_to(work[:, k + i : k + i + 1], work.shape) for i in range(panel)]
+        square = [
+            [jnp.broadcast_to(rows[i][:, k + j : k + j + 1], (1, LANES)) for j in range(panel)]
+            for i in range(panel)
+        ]
+        update = jnp.zeros(work.shape, F32)
+        for i in range(panel):
+            reciprocal = 1.0 / square[i][i]
+            for j in range(i + 1, panel):
+                factor = square[i][j] * reciprocal
+                rows[j] = rows[j] - factor * rows[i]
+                columns[j] = columns[j] - factor * columns[i]
+                for m in range(j, panel):
+                    square[j][m] = square[j][m] - factor * square[i][m]
+            update += columns[i] * (rows[i] * reciprocal)
+        work = jnp.where(spot >= k + panel, work - update, work)
+        for i in range(1, panel):
+            work = jnp.where(spot == k + i, rows[i], work)
+    return work
+
+
 def solve_gram(inverse, diagonal, row):
     half = jnp.sum(inverse * pltpu.roll(row, WIDTH, 1), axis=1, keepdims=True) / diagonal
     return jnp.sum(inverse * half, axis=0, keepdims=True)
@@ -227,11 +283,7 @@
     tail = sum_ref[IMAGE_TILES + 2]
     lane = iota((WIDTH, LANES), 1)
     spot = iota((WIDTH, LANES), 0)
-    work = jnp.where(lane == spot + WIDTH, 1.0, gram)
-    for k in range(WIDTH - 1):
-        pivot = work[k : k + 1, :]
-        scaled_pivot = pivot / pivot[:, k : k + 1]
-        work = work - jnp.where(spot > k, work[:, k : k + 1], 0.0) * scaled_pivot
+    work = eliminate(jnp.where(lane == spot + WIDTH, 1.0, gram), 4)
     diagonal = jnp.sum(jnp.where(lane == spot, work, 0.0), axis=1, keepdims=True)
     inverse = jnp.where((lane >= WIDTH) & (lane < 2 * WIDTH), work, 0.0)
 
@@ -282,21 +334,28 @@
             scaled_ref[cols_ref[n]], blocks_ref[n], NT, preferred_element_type=F32
         )
         acc_ref[rows_ref[n]] += product[0:8]
-    even = iota((8, LANES), 0) % 2 == 0
-    for t in range(TILES):
-        at = LANES * (t % per_block)
-        out_ref[8 * t : 8 * t + 8, :] = jnp.where(
-            even, acc_ref[t // per_block, :, at : at + LANES], sums
-        )
-
-
-def step_body(me_ref, parts_ref, keep_ref, y_ref, rhs_ref, out_ref):
+    lane = iota((8, LANES), 1)
+    shares = LANES // WIDTH
+    sums = jnp.broadcast_to(pltpu.roll(sums, WIDTH, 1), (8, LANES))
+    row = iota((8, LANES), 0)
+    for u in range(TILES // 2):
+        pack = sums
+        for v in range(2):
+            t = 2 * u + v
+            at = LANES * (t % per_block)
+            tile = acc_ref[t // per_block, :, at : at + LANES]
+            for q in range(shares):
+                turned = tile if q == 0 else pltpu.roll(tile, LANES - WIDTH * q, 1)
+                pack = jnp.where((lane < WIDTH) & (row == shares * v + q), turned, pack)
+        out_ref[8 * u : 8 * u + 8, :] = pack
+
+
+def step_body(me_ref, parts_ref, keep_ref, y_ref, rhs_ref, solution_ref, residual_ref, precond_ref):
     total = parts_ref[0:8, :]
-    for i in range(1, COL_PARTS // 4):
+    for i in range(1, COL_PARTS // 8):
         total += parts_ref[8 * i : 8 * i + 8, :]
-    even = iota((8, LANES), 0) % 2 == 0
-    image_rows = jnp.sum(jnp.where(even, total, 0.0), axis=0, keepdims=True)
-    sums = jnp.sum(jnp.where(even, 0.0, total), axis=0, keepdims=True)
+    image_rows = jnp.sum(total, axis=0, keepdims=True)
+    sums = pltpu.roll(image_rows, LANES - WIDTH, 1)
 
     lane = iota((1, LANES), 1)
     first = lane < WIDTH
@@ -313,8 +372,9 @@
     alpha = along / curvature
 
     start = pl.multiple_of((me_ref[0] // 4) * LANES, LANES)
-    ysketch = y_ref[:, pl.ds(start, LANES)]
-    rhs = rhs_ref[:, pl.ds(start, LANES)]
+    turn = ((4 - me_ref[0] % 4) % 4) * WIDTH
+    ysketch = pltpu.roll(y_ref[:, pl.ds(start, LANES)], turn, 1)
+    rhs = pltpu.roll(rhs_ref[:, pl.ds(start, LANES)], turn, 1)
     direction = (rhs - jnp.sum(ysketch * to_column(coeffs, WIDTH), axis=0, keepdims=True)) / precond_shift
     image = image_rows + regularize * direction
     residual = rhs - alpha * image
@@ -324,19 +384,13 @@
     precond_residual = (
         residual - jnp.sum(ysketch * to_column(res_coeffs, WIDTH), axis=0, keepdims=True)
     ) / precond_shift
-    which = iota((8, LANES), 0)
-    pack = jnp.where(
-        which == 0, alpha * direction, jnp.where(which == 1, residual, precond_residual)
-    )
-    out_ref[...] = pltpu.roll(pack, ((4 - me_ref[0] % 4) % 4) * WIDTH, 1)
+    solution_ref[...] = (alpha * direction)[0, :WIDTH]
+    residual_ref[...] = residual[0, :WIDTH]
+    precond_ref[...] = precond_residual[0, :WIDTH]
 
 
 def exchange(value, axis):
     return lax.all_to_all(value, axis, 0, 0, tiled=True)
-
-
-def copies(value, count):
-    return jnp.broadcast_to(value[None], (count,) + value.shape)
 
 
 def shards(blocks, block_rows, block_cols, sketch, theta, rhs):
@@ -345,34 +399,37 @@
     cols_idx = block_cols[0, 0]
     omega = sketch.T
     rhs_line = rhs.reshape(1, LOCAL)
+    theta_tiles = theta.reshape(CORES, HALF_TILES, LANES)
     my_core = lax.axis_index("core").astype(jnp.int32).reshape(1)
     my_col = lax.axis_index(("y", "z")).astype(jnp.int32).reshape(1)
     shape = jax.ShapeDtypeStruct
     work = 2 * BLOCKS * ORDER * ORDER
 
     with jax.named_scope("sketch_cols"):
-        terms, values = call(
+        terms = call(
             sketch_body,
             [hbm(), hbm(), hbm(), hbm()],
-            (shape((CORES, WIDTH, HALF), F32), shape(values.shape, BF16)),
+            shape((CORES, WIDTH, HALF), F32),
             scratch=[
                 pltpu.SMEM((1, BLOCKS), jnp.int32),
                 pltpu.SMEM((1, BLOCKS), jnp.int32),
                 pltpu.VMEM((WIDTH, LOCAL), BF16),
-                pltpu.SemaphoreType.DMA((3 + BLOCKS,)),
+                pltpu.VMEM(values.shape, BF16),
+                pltpu.SemaphoreType.DMA((BLOCKS + 3,)),
             ],
             flops=work * WIDTH,
             name="sketch_cols",
+            limit=FIRST_LIMIT,
         )(block_rows[0], block_cols[0], omega, values)
-        parts = lax.all_gather(terms, "core", tiled=True)
+        parts = lax.all_gather(terms, "core")
         parts = call(
-            pair_body, [smem(), vmem()], shape((X_PARTS, WIDTH, HALF), BF16), name="pair"
+            pair_body, [smem(), vmem()], shape((X_PARTS, WIDTH, HALF), F32), name="pair"
         )(my_core, parts)
         parts = exchange(parts, "x")
     with jax.named_scope("scaled"):
         scaled = call(
             scale_body, [smem(), vmem(), vmem()], shape((WIDTH, HALF), BF16), name="scaled"
-        )(my_core, parts, theta.reshape(CORES, HALF))
+        )(my_core, parts, theta_tiles)
         scaled = lax.all_gather(scaled, "core")
     with jax.named_scope("ysketch"):
         terms = call(
@@ -382,10 +439,19 @@
             flops=work * WIDTH,
             name="ysketch",
         )(rows_idx, cols_idx, scaled, values)
-        parts = jnp.sum(exchange(terms, "y"), axis=0)
-        parts = jnp.sum(exchange(parts, "z"), axis=0)
-        parts = exchange(copies(parts, Z_PARTS), "z")
-        tiles = exchange(copies(parts, Y_PARTS), "y")
+        parts = exchange(terms, "y")
+        parts = call(gather_body, [vmem()], shape((Z_PARTS, 8, LANES), F32), name="gather")(parts)
+        parts = call(
+            spread_body,
+            [vmem()],
+            shape((Z_PARTS, 8, LANES), F32),
+            name="spread",
+        )(exchange(parts, "z"))
+        parts = exchange(parts, "z")
+        tiles = call(
+            copy_body, [vmem()], shape((Y_PARTS, Z_PARTS, 8, LANES), F32), name="copies"
+        )(parts)
+        tiles = exchange(tiles, "y")
     with jax.named_scope("gram"):
         ysketch, terms = call(
             gram_body,
@@ -414,13 +480,13 @@
             (shape((2, 8, LANES), F32), shape((2 * WIDTH + 24, LANES), F32)),
             scratch=[pltpu.VMEM((SENT_TILES, 8, LANES), F32)],
             name="image_scaled",
-        )(my_core, parts, theta.reshape(CORES, HALF_TILES, LANES))
+        )(my_core, parts, theta_tiles)
         parts = lax.all_gather(terms, "core")
     with jax.named_scope("image"):
         terms = call(
             image_body,
             [smem(), smem(), vmem(), vmem()],
-            shape((2 * COL_PARTS, LANES), F32),
+            shape((COL_PARTS, LANES), F32),
             scratch=[
                 pltpu.VMEM((LOCAL // ORDER, 16, ORDER), BF16),
                 pltpu.VMEM((LOCAL // ORDER, 8, ORDER), F32),
@@ -428,16 +494,15 @@
             flops=work,
             name="image",
         )(rows_idx, cols_idx, parts, values)
-        parts = exchange(terms.reshape(COL_PARTS, 2, LANES), ("y", "z")).reshape(2 * COL_PARTS, LANES)
+        parts = exchange(terms, ("y", "z"))
     with jax.named_scope("step"):
-        out = call(
+        share = shape((LOCAL // COL_PARTS,), F32)
+        return call(
             step_body,
             [smem(), vmem(), vmem(), vmem(), vmem()],
-            shape((8, LANES), F32),
+            (share, share, share),
             name="step",
         )(my_col, parts, keep, ysketch, rhs_line)
-    share = LOCAL // COL_PARTS
-    return (out[0, :share], out[1, :share], out[2, :share])
 
 
 def solution(mesh):

time: 141 us -> 136 us (0.965)
  blocking collectives: 87.9 us -> 100 us
  local copies, waits for them, and re-layouts: 11.3 us -> 4.23 us
  waiting for transfers between devices: 19.6 us -> 13.1 us
  starting transfers between devices: 8 us -> 4.54 us
    all_to_all x5 -> x6, blocking collectives: 65.7 us -> 78.2 us  [exchange(): return lax.all_to_all(value, axis, 0, 0, tiled=True)]
    all_gather x2 -> x3, blocking collectives: 10.5 us -> 19.4 us  [shards(): parts = lax.all_gather(terms, 'core')]
    all_gather x1 -> x0, blocking collectives: 8.67 us -> none  [shards(): parts = lax.all_gather(terms, 'core', tiled=True)]
    unnamed x26 -> x20, local copies, waits for them, and re-layouts: 10.8 us -> 4.23 us
    all_to_all x2 -> x1, waiting for transfers between devices: 19.6 us -> 13.1 us  [exchange(): return lax.all_to_all(value, axis, 0, 0, tiled=True)]
    all_to_all x2 -> x1, starting transfers between devices: 8 us -> 4.54 us  [exchange(): return lax.all_to_all(value, axis, 0, 0, tiled=True)]
    pallas_call x1, Pallas kernels: 2.9 us -> 1.34 us  [shards(): call(factor_body, [smem(), vmem(), vmem()], (shape((2, 8, LANES), F32), s...]
    pallas_call x4 -> x7, Pallas kernels: 5.87 us -> 7.07 us  [the longest x1 3.51 us: shards(): call(sketch_body, [hbm(), hbm(), hbm(), hbm()], shape((CORES, WIDTH, HALF...]
  transfers between devices with their start and end apart: 2 -> 1, of which waited for: 2 -> 1; matrix products, arithmetic and copies ran while one was open for 0% -> 0% of each run, Pallas kernels for 0% -> 0%
where the time goes in v3:
time: 136 us; the launch traced here: 135 us
  blocking collectives  100 us (74%)
  waiting for transfers between devices  13.1 us (10%)
  Pallas kernels  12.4 us (9%)
  starting transfers between devices  4.54 us (3%)
  local copies, waits for them, and re-layouts  4.23 us (3%)
    all_to_all x6, blocking collectives, exchange(): return lax.all_to_all(value, axis, 0, 0, tiled=True)  78.2 us
    all_gather x3, blocking collectives, shards(): parts = lax.all_gather(terms, 'core')  19.4 us
    all_to_all x1, waiting for transfers between devices, exchange(): return lax.all_to_all(value, axis, 0, 0, tiled=True)  13.1 us
    all_to_all x1, starting transfers between devices, exchange(): return lax.all_to_all(value, axis, 0, 0, tiled=True)  4.54 us
    unnamed x20, local copies, waits for them, and re-layouts  4.23 us
    pallas_call x1, Pallas kernels, shards(): call(sketch_body, [hbm(), hbm(), hbm(), hbm()], shape((CORES, WIDTH, HALF...  3.51 us
    all_gather x1, blocking collectives, shards(): scaled = lax.all_gather(scaled, 'core')  2.75 us
  transfers between devices with their start and end apart: 1, of which 1 were waited for; matrix products, arithmetic and copies ran while one was open for 0% of the time, Pallas kernels for 0%

profile of v3, /device:TPU:1, one launch (start us, length us, event | category | flops | bytes accessed | tf_op | source)
XLA Modules:
  0.0 135.4 jit_solution(14510349525815232809)
XLA Ops:
  0.6 3.5 %sketch_cols.1 = f32[2,32,1024]{2,1,0:T(8,128)} custom-call(s32[1,8]{1,0:T(1,128)} %bitcast.33, s32[1,8]{1,0:T(1,128)} %bitcast.37, bf16[32,2048]{1,0:T(8,128)(2,1)} %bitcast.24, bf16[8,512,512]{2,1,0:T(8,128)(2,1)} %bitcast.18), custom_call_target="tpu_custom_call" | custom-call | flops 134217728 | bytes 1048576 | tf_op jit(solution)/shard_map/sketch_cols/sketch_cols/pallas_call | solution.py:409
  4.2 8.9 %all-gather = f32[4,32,1024]{2,1,0:T(8,128)S(1)} all-gather(f32[2,32,1024]{2,1,0:T(8,128)} %sketch_cols.1), channel_id=2, replica_groups=mesh['x'=4,'core'=2,'y'=4,'z'=16] {'core'}, dimensions={0}, use_global_device_ids=true | all-gather | bytes 786432 | tf_op jit(solution)/shard_map/sketch_cols/all_gather | solution.py:424
  13.1 0.0 copy-start.2
  13.1 0.0 copy-start.5
  13.1 0.0 copy-start.7
  13.1 0.0 copy-start.9
  13.1 11.8 %all_to_all.41.parts_ref = f32[4,32,1024]{2,1,0:T(8,128)S(1)} all-to-all(f32[4,32,1024]{2,1,0:T(8,128)S(1)} %pair.1), channel_id=1, replica_groups=mesh['x'=4,'core'=2,'y'=4,'z'=16] {'x'}, dimensions={0} | all-to-all | bytes 1048576 | tf_op jit(solution)/shard_map/sketch_cols/all_to_all | solution.py:393
  24.9 0.0 copy-start.3
  24.9 0.7 copy-done.3
  25.6 2.7 %all-gather.1 = bf16[64,1024]{1,0:T(8,128)(2,1)S(1)} all-gather(bf16[32,1024]{1,0:T(8,128)(2,1)S(1)} %scaled.1), channel_id=3, replica_groups=mesh['x'=4,'core'=2,'y'=4,'z'=16] {'core'}, dimensions={0}, use_global_device_ids=true | all-gather | bytes 196608 | tf_op jit(solution)/shard_map/scaled/all_gather | solution.py:433
  28.4 0.0 copy-start
  28.4 2.2 %copy-done = bf16[1,1,8,512,512]{4,3,2,1,0:T(8,128)(2,1)S(1)} copy-done((bf16[1,1,8,512,512]{4,3,2,1,0:T(8,128)(2,1)S(1)}, bf16[1,1,8,512,512]{4,3,2,1,0:T(8,128)(2,1)}, u32[]{:S(2)}) %copy-start) | copy-done | bytes 4194328
  30.6 0.0 copy-start.6
  30.6 0.7 copy-done.6
  31.2 0.0 copy-start.8
  31.2 0.7 copy-done.8
  31.9 0.0 copy-start.1
  31.9 1.9 %ysketch.1 = f32[4,16,8,128]{3,2,1,0:T(8,128)S(1)} custom-call(s32[8]{0:T(128)S(1)} %bitcast.34, s32[8]{0:T(128)S(1)} %bitcast.38, bf16[2,32,1024]{2,1,0:T(8,128)(2,1)S(1)} %bitcast.26, bf16[8,512,512]{2,1,0:T(8,128)(2,1)S(1)} %bitcast.19), custom_call_target="tpu_custom_call" | custom-call | flops 134217728 | bytes 1048576 | tf_op jit(solution)/shard_map/ysketch/ysketch/pallas_call | solution.py:435
  33.8 8.8 %all_to_all.42.parts_ref = f32[4,16,8,128]{3,2,1,0:T(8,128)S(1)} all-to-all(f32[4,16,8,128]{3,2,1,0:T(8,128)S(1)} %ysketch.1), channel_id=1, replica_groups=mesh['x'=4,'core'=2,'y'=4,'z'=16] {'y'}, dimensions={0} | all-to-all | bytes 524288 | tf_op jit(solution)/shard_map/ysketch/all_to_all | solution.py:393
  42.6 23.3 %all_to_all.43.parts_ref = f32[16,8,128]{2,1,0:T(8,128)S(1)} all-to-all(f32[16,8,128]{2,1,0:T(8,128)S(1)} %gather.1), channel_id=1, replica_groups=mesh['x'=4,'core'=2,'y'=4,'z'=16] {'z'}, dimensions={0} | all-to-all | bytes 131072 | tf_op jit(solution)/shard_map/ysketch/all_to_all | solution.py:393
  65.9 14.4 %all_to_all.44.part_ref = f32[16,8,128]{2,1,0:T(8,128)S(1)} all-to-all(f32[16,8,128]{2,1,0:T(8,128)S(1)} %spread.1), channel_id=1, replica_groups=mesh['x'=4,'core'=2,'y'=4,'z'=16] {'z'}, dimensions={0} | all-to-all | bytes 131072 | tf_op jit(solution)/shard_map/ysketch/all_to_all | solution.py:393
  80.3 0.0 copy-start.4
  80.4 7.9 %all_to_all.45.tiles_ref = f32[4,16,8,128]{3,2,1,0:T(8,128)S(1)} all-to-all(f32[4,16,8,128]{3,2,1,0:T(8,128)S(1)} %copies.1), channel_id=1, replica_groups=mesh['x'=4,'core'=2,'y'=4,'z'=16] {'y'}, dimensions={0} | all-to-all | bytes 524288 | tf_op jit(solution)/shard_map/ysketch/all_to_all | solution.py:393
  88.3 0.0 copy-done.2
  88.3 0.0 copy-done.5
  88.3 0.0 copy-done.7
  88.3 0.0 copy-done.9
  88.3 0.0 copy-done.1
  88.3 2.1 %gram.1 = (f32[32,2048]{1,0:T(8,128)S(1)}, f32[69,8,128]{2,1,0:T(8,128)S(1)}) custom-call(s32[8]{0:T(128)S(1)} %bitcast.35, s32[8]{0:T(128)S(1)} %bitcast.39, f32[4,16,8,128]{3,2,1,0:T(8,128)S(1)} %all_to_all.45.tiles_ref, bf16[32,2048]{1,0:T(8,128)(2,1)S(1)} %bitcast.25, f32[1,2048]{1,0:T(1,128)S(1)} %bitcast.31, bf16[8,512,512]{2,1,0:T(8,128)(2,1)S(1)} %bitcast.20), custom_call_target="tpu_custom_call" | custom-call | flops 402653184 | bytes 1048576 | tf_op jit(solution)/shard_map/gram/gram/pallas_call | solution.py:456
  90.4 7.5 %all-gather.2 = f32[138,8,128]{2,1,0:T(8,128)S(1)} all-gather(f32[69,8,128]{2,1,0:T(8,128)S(1)} %get-tuple-element.7), channel_id=4, replica_groups=mesh['x'=4,'core'=2,'y'=4,'z'=16] {'core'}, dimensions={0}, use_global_device_ids=true | all-gather | bytes 847872 | tf_op jit(solution)/shard_map/gram/all_gather | solution.py:468
  97.9 12.0 %all_to_all.46.parts_ref = f32[4,36,8,128]{3,2,1,0:T(8,128)S(1)} all-to-all(f32[4,36,8,128]{3,2,1,0:T(8,128)S(1)} %pair_image.1), channel_id=1, replica_groups=mesh['x'=4,'core'=2,'y'=4,'z'=16] {'x'}, dimensions={0} | all-to-all | bytes 1179648 | tf_op jit(solution)/shard_map/gram/all_to_all | solution.py:393
  109.9 0.0 copy-done.4
  109.9 1.3 image_scaled.1
  111.3 3.0 %all-gather.3 = f32[4,8,128]{2,1,0:T(8,128)S(1)} all-gather(f32[2,8,128]{2,1,0:T(8,128)S(1)} %get-tuple-element.8), channel_id=5, replica_groups=mesh['x'=4,'core'=2,'y'=4,'z'=16] {'core'}, dimensions={0}, use_global_device_ids=true | all-gather | bytes 24576 | tf_op jit(solution)/shard_map/image_scaled/all_gather | solution.py:484
  114.3 2.5 %image.1 = f32[64,128]{1,0:T(8,128)} custom-call(s32[8]{0:T(128)S(1)} %bitcast.36, s32[8]{0:T(128)S(1)} %bitcast.40, f32[2,2,8,128]{3,2,1,0:T(8,128)S(1)} %bitcast.28, bf16[8,512,512]{2,1,0:T(8,128)(2,1)S(1)} %bitcast.21), custom_call_target="tpu_custom_call" | custom-call | flops 4194304 | bytes 1048576 | tf_op jit(solution)/shard_map/image/image/pallas_call | solution.py:486
  116.7 4.5 %all-to-all-start.6 = ((f32[64,1,128]{2,1,0:T(1,128)}), f32[64,1,128]{2,1,0:T(1,128)S(1)}, u32[]{:S(2)}, u32[]{:S(2)}) async-start(f32[64,1,128]{2,1,0:T(1,128)} %bitcast.15), calls=%async_computation.6 | async-start | bytes 65536 | tf_op jit(solution)/shard_map/image/all_to_all | solution.py:393
  121.3 13.1 %all-to-all-done.6 = f32[64,1,128]{2,1,0:T(1,128)S(1)} async-done(((f32[64,1,128]{2,1,0:T(1,128)}), f32[64,1,128]{2,1,0:T(1,128)S(1)}, u32[]{:S(2)}, u32[]{:S(2)}) %all-to-all-start.6) | async-done | bytes 32800 | tf_op jit(solution)/shard_map/image/all_to_all | solution.py:393
  134.4 1.0 step.1
  (6 shorter events, 0.2 us)
Async XLA Ops:
  13.1 75.2 %copy-start.2 = (bf16[2048,32]{0,1:T(8,128)(2,1)S(1)}, bf16[2048,32]{0,1:T(8,128)(2,1)}, u32[]{:S(2)}) copy-start(bf16[2048,32]{0,1:T(8,128)(2,1)} %param.9) | copy-start | bytes 393220
  13.1 75.2 %copy-start.5 = (f32[2048]{0:T(1024)S(1)}, f32[2048]{0:T(1024)}, u32[]{:S(2)}) copy-start(f32[2048]{0:T(1024)} %param.11) | copy-start | bytes 24580
  13.1 75.2 %copy-start.7 = (s32[1,1,8]{2,1,0:T(1,128)S(1)}, s32[1,1,8]{2,1,0:T(1,128)}, u32[]{:S(2)}) copy-start(s32[1,1,8]{2,1,0:T(1,128)} %param.7) | copy-start | bytes 100
  13.1 75.2 %copy-start.9 = (s32[1,1,8]{2,1,0:T(1,128)S(1)}, s32[1,1,8]{2,1,0:T(1,128)}, u32[]{:S(2)}) copy-start(s32[1,1,8]{2,1,0:T(1,128)} %param.8) | copy-start | bytes 100
  24.9 0.7 copy-start.3
  28.4 2.2 %copy-start = (bf16[1,1,8,512,512]{4,3,2,1,0:T(8,128)(2,1)S(1)}, bf16[1,1,8,512,512]{4,3,2,1,0:T(8,128)(2,1)}, u32[]{:S(2)}) copy-start(bf16[1,1,8,512,512]{4,3,2,1,0:T(8,128)(2,1)} %param.6) | copy-start | bytes 12582916
  30.6 0.7 copy-start.6
  31.2 0.7 copy-start.8
  31.9 56.4 %copy-start.1 = (bf16[1,1,8,512,512]{4,3,2,1,0:T(8,128)(2,1)S(1)}, bf16[1,1,8,512,512]{4,3,2,1,0:T(8,128)(2,1)}, u32[]{:S(2)}) copy-start(bf16[1,1,8,512,512]{4,3,2,1,0:T(8,128)(2,1)} %param.6) | copy-start | bytes 12582916
  80.3 29.6 %copy-start.4 = (f32[2048]{0:T(1024)S(1)}, f32[2048]{0:T(1024)}, u32[]{:S(2)}) copy-start(f32[2048]{0:T(1024)} %param.10) | copy-start | bytes 24580
  116.7 17.7 %all-to-all-start.6 = ((f32[64,1,128]{2,1,0:T(1,128)}), f32[64,1,128]{2,1,0:T(1,128)S(1)}, u32[]{:S(2)}, u32[]{:S(2)}) async-start(f32[64,1,128]{2,1,0:T(1,128)} %bitcast.15), calls=%async_computation.6 | async-start | bytes 65536 | tf_op jit(solution)/shard_map/image/all_to_all | solution.py:393

commit v4 on v3

--- a/solution.py
+++ b/solution.py
@@ -15,8 +15,9 @@
 CORES = 2
 X_PARTS = 4
 Y_PARTS = 4
-Z_PARTS = 16
-COL_PARTS = Y_PARTS * Z_PARTS
+FAR_PARTS = 4
+NEAR_PARTS = 4
+COL_PARTS = Y_PARTS * FAR_PARTS * NEAR_PARTS
 BLOCKS = 8
 ORDER = 512
 LOCAL = 2048
@@ -25,10 +26,11 @@
 HALF_TILES = HALF // LANES
 TILES = LOCAL // LANES
 GROUPS = WIDTH // 8
+SHARES = Y_PARTS * NEAR_PARTS
+SHARE_TILES = GROUPS * TILES // SHARES
 IMAGE_TILES = GROUPS * HALF_TILES + 1
 SENT_TILES = IMAGE_TILES + 3
 VMEM_LIMIT = 24 * 1024 * 1024
-FIRST_LIMIT = 64 * 1024 * 1024 - 64 * 1024
 
 NT = (((1,), (1,)), ((), ()))
 
@@ -37,10 +39,6 @@
     return pl.BlockSpec(memory_space=pltpu.VMEM)
 
 
-def hbm():
-    return pl.BlockSpec(memory_space=pltpu.HBM)
-
-
 def smem():
     return pl.BlockSpec(memory_space=pltpu.SMEM)
 
@@ -49,7 +47,7 @@
     return lax.broadcasted_iota(jnp.int32, shape, axis)
 
 
-def call(body, in_specs, out_shape, scratch=(), flops=0, name=None, limit=VMEM_LIMIT):
+def call(body, in_specs, out_shape, scratch=(), flops=0, name=None):
     out_specs = jax.tree.map(lambda _: vmem(), out_shape)
     return pl.pallas_call(
         body,
@@ -57,35 +55,18 @@
         out_specs=out_specs,
         out_shape=out_shape,
         scratch_shapes=list(scratch),
-        compiler_params=pltpu.CompilerParams(vmem_limit_bytes=limit),
+        compiler_params=pltpu.CompilerParams(vmem_limit_bytes=VMEM_LIMIT),
         cost_estimate=pl.CostEstimate(flops=flops, bytes_accessed=1 << 20, transcendentals=0),
         name=name,
     )
 
 
-def sketch_body(
-    rows_hbm, cols_hbm, omega_hbm, blocks_hbm, out_ref, rows_ref, cols_ref, omega_ref, blocks_ref, sems
-):
-    first = [
-        pltpu.make_async_copy(rows_hbm, rows_ref, sems.at[BLOCKS]),
-        pltpu.make_async_copy(cols_hbm, cols_ref, sems.at[BLOCKS + 1]),
-        pltpu.make_async_copy(omega_hbm, omega_ref, sems.at[BLOCKS + 2]),
-    ]
-    for copy in first:
-        copy.start()
-    arrivals = [
-        pltpu.make_async_copy(blocks_hbm.at[n], blocks_ref.at[n], sems.at[n]) for n in range(BLOCKS)
-    ]
-    for copy in arrivals:
-        copy.start()
+def sketch_body(rows_ref, cols_ref, omega_ref, blocks_ref, out_ref):
     out_ref[...] = jnp.zeros(out_ref.shape, F32)
-    for copy in first:
-        copy.wait()
     for n in range(BLOCKS):
-        arrivals[n].wait()
-        start = pl.multiple_of(rows_ref[0, n] * ORDER, ORDER)
-        place = pl.multiple_of(cols_ref[0, n] % 2 * ORDER, ORDER)
-        out_ref[cols_ref[0, n] // 2, :, pl.ds(place, ORDER)] += jnp.dot(
+        start = pl.multiple_of(rows_ref[n] * ORDER, ORDER)
+        place = pl.multiple_of(cols_ref[n] % 2 * ORDER, ORDER)
+        out_ref[cols_ref[n] // 2, :, pl.ds(place, ORDER)] += jnp.dot(
             omega_ref[:, pl.ds(start, ORDER)], blocks_ref[n], preferred_element_type=F32
         )
 
@@ -110,26 +91,16 @@
         place = pl.multiple_of(cols_ref[n] % 2 * ORDER, ORDER)
         left = scaled_ref[cols_ref[n] // 2, :, pl.ds(place, ORDER)]
         product = lax.dot_general(left, blocks_ref[n], NT, preferred_element_type=F32)
-        first = rows_ref[n] * (ORDER // LANES)
         for g in range(GROUPS):
             for q in range(ORDER // LANES):
-                out_ref[g, first + q] += product[8 * g : 8 * g + 8, LANES * q : LANES * (q + 1)]
-
-
-def gather_body(parts_ref, out_ref):
-    out_ref[...] = (parts_ref[0] + parts_ref[1]) + (parts_ref[2] + parts_ref[3])
-
-
-def copy_body(part_ref, out_ref):
-    for i in range(Y_PARTS):
-        out_ref[i] = part_ref[...]
+                out_ref[g * (LOCAL // ORDER) + rows_ref[n], q] += product[8 * g : 8 * g + 8, LANES * q : LANES * (q + 1)]
 
 
 def spread_body(parts_ref, out_ref):
-    sums = [parts_ref[i] for i in range(Z_PARTS)]
+    sums = [parts_ref[i] for i in range(parts_ref.shape[0])]
     while len(sums) > 1:
         sums = [a + b for a, b in zip(sums[::2], sums[1::2])]
-    for i in range(Z_PARTS):
+    for i in range(out_ref.shape[0]):
         out_ref[i] = sums[0]
 
 
@@ -161,7 +132,7 @@
 ):
     for g in range(GROUPS):
         for t in range(TILES):
-            y_ref[8 * g : 8 * g + 8, LANES * t : LANES * (t + 1)] = tiles_ref[g, t]
+            y_ref[8 * g : 8 * g + 8, LANES * t : LANES * (t + 1)] = tiles_ref[(g * TILES + t) // SHARE_TILES, t % SHARE_TILES]
     omega = omega_ref[...].astype(F32)
     ysketch = y_ref[...] + regularize * omega
     y_ref[...] = ysketch
@@ -401,26 +372,18 @@
     rhs_line = rhs.reshape(1, LOCAL)
     theta_tiles = theta.reshape(CORES, HALF_TILES, LANES)
     my_core = lax.axis_index("core").astype(jnp.int32).reshape(1)
-    my_col = lax.axis_index(("y", "z")).astype(jnp.int32).reshape(1)
+    my_col = lax.axis_index(("y", "far", "near")).astype(jnp.int32).reshape(1)
     shape = jax.ShapeDtypeStruct
     work = 2 * BLOCKS * ORDER * ORDER
 
     with jax.named_scope("sketch_cols"):
         terms = call(
             sketch_body,
-            [hbm(), hbm(), hbm(), hbm()],
+            [smem(), smem(), vmem(), vmem()],
             shape((CORES, WIDTH, HALF), F32),
-            scratch=[
-                pltpu.SMEM((1, BLOCKS), jnp.int32),
-                pltpu.SMEM((1, BLOCKS), jnp.int32),
-                pltpu.VMEM((WIDTH, LOCAL), BF16),
-                pltpu.VMEM(values.shape, BF16),
-                pltpu.SemaphoreType.DMA((BLOCKS + 3,)),
-            ],
             flops=work * WIDTH,
             name="sketch_cols",
-            limit=FIRST_LIMIT,
-        )(block_rows[0], block_cols[0], omega, values)
+        )(rows_idx, cols_idx, omega, values)
         parts = lax.all_gather(terms, "core")
         parts = call(
             pair_body, [smem(), vmem()], shape((X_PARTS, WIDTH, HALF), F32), name="pair"
@@ -435,23 +398,20 @@
         terms = call(
             forward_body,
             [smem(), smem(), vmem(), vmem()],
-            shape((GROUPS, TILES, 8, LANES), F32),
+            shape((SHARES, SHARE_TILES, 8, LANES), F32),
             flops=work * WIDTH,
             name="ysketch",
         )(rows_idx, cols_idx, scaled, values)
-        parts = exchange(terms, "y")
-        parts = call(gather_body, [vmem()], shape((Z_PARTS, 8, LANES), F32), name="gather")(parts)
+        share = (SHARE_TILES, 8, LANES)
+        parts = exchange(terms, ("y", "near"))
         parts = call(
-            spread_body,
-            [vmem()],
-            shape((Z_PARTS, 8, LANES), F32),
-            name="spread",
-        )(exchange(parts, "z"))
-        parts = exchange(parts, "z")
-        tiles = call(
-            copy_body, [vmem()], shape((Y_PARTS, Z_PARTS, 8, LANES), F32), name="copies"
+            spread_body, [vmem()], shape((FAR_PARTS,) + share, F32), name="ysketch_near"
         )(parts)
-        tiles = exchange(tiles, "y")
+        parts = exchange(parts, "far")
+        parts = call(
+            spread_body, [vmem()], shape((SHARES,) + share, F32), name="ysketch_far"
+        )(parts)
+        tiles = exchange(parts, ("y", "near"))
     with jax.named_scope("gram"):
         ysketch, terms = call(
             gram_body,
@@ -494,7 +454,7 @@
             flops=work,
             name="image",
         )(rows_idx, cols_idx, parts, values)
-        parts = exchange(terms, ("y", "z"))
+        parts = exchange(terms, ("y", "far", "near"))
     with jax.named_scope("step"):
         share = shape((LOCAL // COL_PARTS,), F32)
         return call(
@@ -506,9 +466,10 @@
 
 
 def solution(mesh):
-    row, col = ("x", "core"), ("y", "z")
+    row, col = ("x", "core"), ("y", "far", "near")
     fine = jax.sharding.Mesh(
-        mesh.devices.reshape(X_PARTS, CORES, Y_PARTS, Z_PARTS), ("x", "core", "y", "z")
+        mesh.devices.reshape(X_PARTS, CORES, Y_PARTS, FAR_PARTS, NEAR_PARTS),
+        ("x", "core", "y", "far", "near"),
     )
     in_specs = (
         P(row, col, None, None, None),

time: 136 us -> 127 us (0.934)
  blocking collectives: 100 us -> 93.4 us
  Pallas kernels: 12.4 us -> 10.3 us
    all_to_all x6 -> x5, blocking collectives: 78.2 us -> 73.2 us  [exchange(): return lax.all_to_all(value, axis, 0, 0, tiled=True)]
    pallas_call x5 -> x4, Pallas kernels: 5.42 us -> 3.28 us  [the longest x1 1.87 us: shards(): call(forward_body, [smem(), smem(), vmem(), vmem()], shape((SHARES, SHARE...]
    all_gather x3, blocking collectives: 19.4 us -> 17.5 us  [shards(): parts = lax.all_gather(terms, 'core')]
where the time goes in v4:
time: 127 us
  blocking collectives  93.4 us (74%)
  waiting for transfers between devices  13.1 us (10%)
  Pallas kernels  10.3 us (8%)
  starting transfers between devices  4.54 us (4%)
  local copies, waits for them, and re-layouts  4.43 us (3%)
    all_to_all x5, blocking collectives, exchange(): return lax.all_to_all(value, axis, 0, 0, tiled=True)  73.2 us
    all_gather x3, blocking collectives, shards(): parts = lax.all_gather(terms, 'core')  17.5 us
    all_to_all x1, waiting for transfers between devices, exchange(): return lax.all_to_all(value, axis, 0, 0, tiled=True)  13.1 us
    all_to_all x1, starting transfers between devices, exchange(): return lax.all_to_all(value, axis, 0, 0, tiled=True)  4.54 us
    unnamed x20, local copies, waits for them, and re-layouts  4.43 us
    all_gather x1, blocking collectives, shards(): scaled = lax.all_gather(scaled, 'core')  2.75 us
  transfers between devices with their start and end apart: 1, of which 1 were waited for; matrix products, arithmetic and copies ran while one was open for 0% of the time, Pallas kernels for 0%

profile of v4, /device:TPU:1, one launch (start us, length us, event | category | flops | bytes accessed | tf_op | source)
XLA Modules:
  0.0 126.5 jit_solution(12503667506900103649)
XLA Ops:
  0.6 0.0 copy-start.9
  0.6 0.0 copy-start.7
  0.7 0.0 copy-start.4
  0.7 0.0 copy-start
  0.7 2.2 %copy-done = bf16[1,1,8,512,512]{4,3,2,1,0:T(8,128)(2,1)S(1)} copy-done((bf16[1,1,8,512,512]{4,3,2,1,0:T(8,128)(2,1)S(1)}, bf16[1,1,8,512,512]{4,3,2,1,0:T(8,128)(2,1)}, u32[]{:S(2)}) %copy-start) | copy-done | bytes 4194328
  2.9 0.0 copy-start.2
  2.9 0.9 copy-done.2
  3.8 0.0 copy-start.6
  3.8 0.7 copy-done.6
  4.4 0.0 copy-start.8
  4.4 0.7 copy-done.8
  5.1 0.0 copy-start.1
  5.1 1.4 %sketch_cols.1 = f32[2,32,1024]{2,1,0:T(8,128)S(1)} custom-call(s32[8]{0:T(128)S(1)} %bitcast.31, s32[8]{0:T(128)S(1)} %bitcast.35, bf16[32,2048]{1,0:T(8,128)(2,1)S(1)} %bitcast.22, bf16[8,512,512]{2,1,0:T(8,128)(2,1)S(1)} %bitcast.16), custom_call_target="tpu_custom_call" | custom-call | flops 134217728 | bytes 1048576 | tf_op jit(solution)/shard_map/sketch_cols/sketch_cols/pallas_call | solution.py:380
  6.5 8.7 %all-gather = f32[4,32,1024]{2,1,0:T(8,128)S(1)} all-gather(f32[2,32,1024]{2,1,0:T(8,128)S(1)} %sketch_cols.1), channel_id=2, replica_groups=mesh['x'=4,'core'=2,'y'=4,'far'=4,'near'=4] {'core'}, dimensions={0}, use_global_device_ids=true | all-gather | bytes 786432 | tf_op jit(solution)/shard_map/sketch_cols/all_gather | solution.py:387
  15.2 0.0 copy-start.3
  15.2 0.0 copy-start.5
  15.2 11.8 %all_to_all.36.parts_ref = f32[4,32,1024]{2,1,0:T(8,128)S(1)} all-to-all(f32[4,32,1024]{2,1,0:T(8,128)S(1)} %pair.1), channel_id=1, replica_groups=mesh['x'=4,'core'=2,'y'=4,'far'=4,'near'=4] {'x'}, dimensions={0} | all-to-all | bytes 1048576 | tf_op jit(solution)/shard_map/sketch_cols/all_to_all | solution.py:364
  27.0 0.0 copy-done.4
  27.0 2.8 %all-gather.1 = bf16[64,1024]{1,0:T(8,128)(2,1)S(1)} all-gather(bf16[32,1024]{1,0:T(8,128)(2,1)S(1)} %scaled.1), channel_id=3, replica_groups=mesh['x'=4,'core'=2,'y'=4,'far'=4,'near'=4] {'core'}, dimensions={0}, use_global_device_ids=true | all-gather | bytes 196608 | tf_op jit(solution)/shard_map/scaled/all_gather | solution.py:396
  29.7 0.0 copy-done.9
  29.7 0.0 copy-done.7
  29.7 0.0 copy-done.1
  29.8 1.9 %ysketch.1 = f32[16,4,8,128]{3,2,1,0:T(8,128)S(1)} custom-call(s32[8]{0:T(128)S(1)} %bitcast.32, s32[8]{0:T(128)S(1)} %bitcast.36, bf16[2,32,1024]{2,1,0:T(8,128)(2,1)S(1)} %bitcast.24, bf16[8,512,512]{2,1,0:T(8,128)(2,1)S(1)} %bitcast.17), custom_call_target="tpu_custom_call" | custom-call | flops 134217728 | bytes 1048576 | tf_op jit(solution)/shard_map/ysketch/ysketch/pallas_call | solution.py:398
  31.6 14.1 %all_to_all.37.parts_ref = f32[16,4,8,128]{3,2,1,0:T(8,128)S(1)} all-to-all(f32[16,4,8,128]{3,2,1,0:T(8,128)S(1)} %ysketch.1), channel_id=1, replica_groups=mesh['x'=4,'core'=2,'y'=4,'far'=4,'near'=4] {'y','near'}, dimensions={0} | all-to-all | bytes 524288 | tf_op jit(solution)/shard_map/ysketch/all_to_all | solution.py:364
  45.8 23.6 %all_to_all.38.parts_ref = f32[4,4,8,128]{3,2,1,0:T(8,128)S(1)} all-to-all(f32[4,4,8,128]{3,2,1,0:T(8,128)S(1)} %ysketch_near.1), channel_id=1, replica_groups=mesh['x'=4,'core'=2,'y'=4,'far'=4,'near'=4] {'far'}, dimensions={0} | all-to-all | bytes 131072 | tf_op jit(solution)/shard_map/ysketch/all_to_all | solution.py:364
  69.4 11.7 %all_to_all.39.tiles_ref = f32[16,4,8,128]{3,2,1,0:T(8,128)S(1)} all-to-all(f32[16,4,8,128]{3,2,1,0:T(8,128)S(1)} %ysketch_far.1), channel_id=1, replica_groups=mesh['x'=4,'core'=2,'y'=4,'far'=4,'near'=4] {'y','near'}, dimensions={0} | all-to-all | bytes 524288 | tf_op jit(solution)/shard_map/ysketch/all_to_all | solution.py:364
  81.1 0.0 copy-done.3
  81.1 0.0 copy-done.5
  81.1 2.1 %gram.1 = (f32[32,2048]{1,0:T(8,128)S(1)}, f32[69,8,128]{2,1,0:T(8,128)S(1)}) custom-call(s32[8]{0:T(128)S(1)} %bitcast.33, s32[8]{0:T(128)S(1)} %bitcast.37, f32[16,4,8,128]{3,2,1,0:T(8,128)S(1)} %all_to_all.39.tiles_ref, bf16[32,2048]{1,0:T(8,128)(2,1)S(1)} %bitcast.23, f32[1,2048]{1,0:T(1,128)S(1)} %bitcast.29, bf16[8,512,512]{2,1,0:T(8,128)(2,1)S(1)} %bitcast.18), custom_call_target="tpu_custom_call" | custom-call | flops 402653184 | bytes 1048576 | tf_op jit(solution)/shard_map/gram/gram/pallas_call | solution.py:416
  83.2 5.8 %all-gather.2 = f32[138,8,128]{2,1,0:T(8,128)S(1)} all-gather(f32[69,8,128]{2,1,0:T(8,128)S(1)} %get-tuple-element.7), channel_id=4, replica_groups=mesh['x'=4,'core'=2,'y'=4,'far'=4,'near'=4] {'core'}, dimensions={0}, use_global_device_ids=true | all-gather | bytes 847872 | tf_op jit(solution)/shard_map/gram/all_gather | solution.py:428
  89.0 12.0 %all_to_all.40.parts_ref = f32[4,36,8,128]{3,2,1,0:T(8,128)S(1)} all-to-all(f32[4,36,8,128]{3,2,1,0:T(8,128)S(1)} %pair_image.1), channel_id=1, replica_groups=mesh['x'=4,'core'=2,'y'=4,'far'=4,'near'=4] {'x'}, dimensions={0} | all-to-all | bytes 1179648 | tf_op jit(solution)/shard_map/gram/all_to_all | solution.py:364
  101.0 1.3 %image_scaled.1 = (f32[2,8,128]{2,1,0:T(8,128)S(1)}, f32[88,128]{1,0:T(8,128)S(1)}) custom-call(s32[1]{0:T(128)} %bitcast.3.core_ref, f32[4,36,8,128]{3,2,1,0:T(8,128)S(1)} %all_to_all.40.parts_ref, f32[2,8,128]{2,1,0:T(8,128)S(1)} %bitcast.28), custom_call_target="tpu_custom_call" | custom-call | bytes 1048576 | tf_op jit(solution)/shard_map/image_scaled/image_scaled/pallas_call | solution.py:437
  102.4 3.0 %all-gather.3 = f32[4,8,128]{2,1,0:T(8,128)S(1)} all-gather(f32[2,8,128]{2,1,0:T(8,128)S(1)} %get-tuple-element.8), channel_id=5, replica_groups=mesh['x'=4,'core'=2,'y'=4,'far'=4,'near'=4] {'core'}, dimensions={0}, use_global_device_ids=true | all-gather | bytes 24576 | tf_op jit(solution)/shard_map/image_scaled/all_gather | solution.py:444
  105.4 2.5 %image.1 = f32[64,128]{1,0:T(8,128)} custom-call(s32[8]{0:T(128)S(1)} %bitcast.34, s32[8]{0:T(128)S(1)} %bitcast.38, f32[2,2,8,128]{3,2,1,0:T(8,128)S(1)} %bitcast.26, bf16[8,512,512]{2,1,0:T(8,128)(2,1)S(1)} %bitcast.19), custom_call_target="tpu_custom_call" | custom-call | flops 4194304 | bytes 1048576 | tf_op jit(solution)/shard_map/image/image/pallas_call | solution.py:446
  107.8 4.5 %all-to-all-start.5 = ((f32[64,1,128]{2,1,0:T(1,128)}), f32[64,1,128]{2,1,0:T(1,128)S(1)}, u32[]{:S(2)}, u32[]{:S(2)}) async-start(f32[64,1,128]{2,1,0:T(1,128)} %bitcast.13), calls=%async_computation.5 | async-start | bytes 65536 | tf_op jit(solution)/shard_map/image/all_to_all | solution.py:364
  112.4 13.1 %all-to-all-done.5 = f32[64,1,128]{2,1,0:T(1,128)S(1)} async-done(((f32[64,1,128]{2,1,0:T(1,128)}), f32[64,1,128]{2,1,0:T(1,128)S(1)}, u32[]{:S(2)}, u32[]{:S(2)}) %all-to-all-start.5) | async-done | bytes 32800 | tf_op jit(solution)/shard_map/image/all_to_all | solution.py:364
  125.5 1.0 step.1
  (5 shorter events, 0.1 us)
Async XLA Ops:
  0.6 29.1 %copy-start.9 = (s32[1,1,8]{2,1,0:T(1,128)S(1)}, s32[1,1,8]{2,1,0:T(1,128)}, u32[]{:S(2)}) copy-start(s32[1,1,8]{2,1,0:T(1,128)} %param.8) | copy-start | bytes 100
  0.6 29.1 %copy-start.7 = (s32[1,1,8]{2,1,0:T(1,128)S(1)}, s32[1,1,8]{2,1,0:T(1,128)}, u32[]{:S(2)}) copy-start(s32[1,1,8]{2,1,0:T(1,128)} %param.7) | copy-start | bytes 100
  0.7 26.3 %copy-start.4 = (f32[2048]{0:T(1024)S(1)}, f32[2048]{0:T(1024)}, u32[]{:S(2)}) copy-start(f32[2048]{0:T(1024)} %param.10) | copy-start | bytes 24580
  0.7 2.2 %copy-start = (bf16[1,1,8,512,512]{4,3,2,1,0:T(8,128)(2,1)S(1)}, bf16[1,1,8,512,512]{4,3,2,1,0:T(8,128)(2,1)}, u32[]{:S(2)}) copy-start(bf16[1,1,8,512,512]{4,3,2,1,0:T(8,128)(2,1)} %param.6) | copy-start | bytes 12582916
  2.9 0.9 copy-start.2
  3.8 0.7 copy-start.6
  4.4 0.7 copy-start.8
  5.1 24.7 %copy-start.1 = (bf16[1,1,8,512,512]{4,3,2,1,0:T(8,128)(2,1)S(1)}, bf16[1,1,8,512,512]{4,3,2,1,0:T(8,128)(2,1)}, u32[]{:S(2)}) copy-start(bf16[1,1,8,512,512]{4,3,2,1,0:T(8,128)(2,1)} %param.6) | copy-start | bytes 12582916
  15.2 65.9 %copy-start.3 = (bf16[2048,32]{0,1:T(8,128)(2,1)S(1)}, bf16[2048,32]{0,1:T(8,128)(2,1)}, u32[]{:S(2)}) copy-start(bf16[2048,32]{0,1:T(8,128)(2,1)} %param.9) | copy-start | bytes 393220
  15.2 65.9 %copy-start.5 = (f32[2048]{0:T(1024)S(1)}, f32[2048]{0:T(1024)}, u32[]{:S(2)}) copy-start(f32[2048]{0:T(1024)} %param.11) | copy-start | bytes 24580
  107.8 17.7 %all-to-all-start.5 = ((f32[64,1,128]{2,1,0:T(1,128)}), f32[64,1,128]{2,1,0:T(1,128)S(1)}, u32[]{:S(2)}, u32[]{:S(2)}) async-start(f32[64,1,128]{2,1,0:T(1,128)} %bitcast.13), calls=%async_computation.5 | async-start | bytes 65536 | tf_op jit(solution)/shard_map/image/all_to_all | solution.py:364

commit v5 on v4

v5 whole, which is shorter than its diff:
```python
import jax
import jax.numpy as jnp
from jax import lax
from jax.experimental import pallas as pl
from jax.experimental.pallas import tpu as pltpu
from jax.sharding import PartitionSpec as P

precond_shift = 1.0
regularize = 0.5

F32 = jnp.float32
BF16 = jnp.bfloat16
HIGHEST = lax.Precision.HIGHEST
LANES = 128
CORES = 2
X_PARTS = 4
Y_PARTS = 4
ROW_PARTS = X_PARTS * CORES
FAR_PARTS = 4
NEAR_PARTS = 4
COL_PARTS = Y_PARTS * FAR_PARTS * NEAR_PARTS
BLOCKS = 8
ORDER = 512
LOCAL = 2048
WIDTH = 32
HALF = LOCAL // CORES
HALF_TILES = HALF // LANES
TILES = LOCAL // LANES
GROUPS = WIDTH // 8
SHARES = Y_PARTS * NEAR_PARTS
SHARE_TILES = GROUPS * TILES // SHARES
VMEM_LIMIT = 24 * 1024 * 1024

NT = (((1,), (1,)), ((), ()))


def vmem():
    return pl.BlockSpec(memory_space=pltpu.VMEM)


def smem():
    return pl.BlockSpec(memory_space=pltpu.SMEM)


def iota(shape, axis):
    return lax.broadcasted_iota(jnp.int32, shape, axis)


def call(body, in_specs, out_shape, scratch=(), flops=0, name=None):
    out_specs = jax.tree.map(lambda _: vmem(), out_shape)
    return pl.pallas_call(
        body,
        in_specs=in_specs,
        out_specs=out_specs,
        out_shape=out_shape,
        scratch_shapes=list(scratch),
        compiler_params=pltpu.CompilerParams(vmem_limit_bytes=VMEM_LIMIT),
        cost_estimate=pl.CostEstimate(flops=flops, bytes_accessed=1 << 20, transcendentals=0),
        name=name,
    )


def sketch_body(rows_ref, cols_ref, omega_ref, blocks_ref, out_ref):
    out_ref[...] = jnp.zeros(out_ref.shape, F32)
    for n in range(BLOCKS):
        start = pl.multiple_of(rows_ref[n] * ORDER, ORDER)
        place = pl.multiple_of(cols_ref[n] % 2 * ORDER, ORDER)
        out_ref[cols_ref[n] // 2, :, pl.ds(place, ORDER)] += jnp.dot(
            omega_ref[:, pl.ds(start, ORDER)], blocks_ref[n], preferred_element_type=F32
        )


def pair_body(core_ref, parts_ref, out_ref):
    half = core_ref[0]
    total = parts_ref[0, half] + parts_ref[1, half]
    for i in range(X_PARTS):
        out_ref[i] = total


def scale_body(core_ref, parts_ref, theta_ref, out_ref):
    total = (parts_ref[0] + parts_ref[1]) + (parts_ref[2] + parts_ref[3])
    tile = theta_ref[core_ref[0]]
    theta = jnp.concatenate([tile[t : t + 1, :] for t in range(HALF_TILES)], axis=1)
    out_ref[...] = (theta * total).astype(BF16)


def forward_body(rows_ref, cols_ref, scaled_ref, blocks_ref, out_ref):
    out_ref[...] = jnp.zeros(out_ref.shape, F32)
    for n in range(BLOCKS):
        place = pl.multiple_of(cols_ref[n] % 2 * ORDER, ORDER)
        left = scaled_ref[cols_ref[n] // 2, :, pl.ds(place, ORDER)]
        product = lax.dot_general(left, blocks_ref[n], NT, preferred_element_type=F32)
        for g in range(GROUPS):
            for q in range(ORDER // LANES):
                out_ref[g * (LOCAL // ORDER) + rows_ref[n], q] += product[8 * g : 8 * g + 8, LANES * q : LANES * (q + 1)]


def spread_body(parts_ref, out_ref):
    sums = [parts_ref[i] for i in range(parts_ref.shape[0])]
    while len(sums) > 1:
        sums = [a + b for a, b in zip(sums[::2], sums[1::2])]
    for i in range(out_ref.shape[0]):
        out_ref[i] = sums[0]


def pack_square(square):
    packed = square[0:8]
    for g in range(1, GROUPS):
        packed += pltpu.roll(square[8 * g : 8 * g + 8], WIDTH * g, 1)
    return packed


def unpack_square(packed):
    lane = iota((8, LANES), 1)
    parts = [packed] + [pltpu.roll(packed, LANES - WIDTH * g, 1) for g in range(1, GROUPS)]
    return jnp.concatenate([jnp.where(lane < WIDTH, part, 0.0) for part in parts], axis=0)


def gram_body(tiles_ref, omega_ref, rhs_ref, y_ref, out_ref, all_ref):
    for g in range(GROUPS):
        for t in range(TILES):
            y_ref[8 * g : 8 * g + 8, LANES * t : LANES * (t + 1)] = tiles_ref[
                (g * TILES + t) // SHARE_TILES, t % SHARE_TILES
            ]
    omega = omega_ref[...].astype(F32)
    ysketch = y_ref[...] + regularize * omega
    y_ref[...] = ysketch
    all_ref[0:WIDTH, :] = ysketch
    all_ref[WIDTH : 2 * WIDTH, :] = omega
    all_ref[2 * WIDTH :, :] = jnp.where(
        iota((LANES - 2 * WIDTH, LOCAL), 0) == 0, rhs_ref[...], 0.0
    )
    products = lax.dot_general(
        all_ref[0 : 2 * WIDTH + 8, :], all_ref[...], NT, precision=HIGHEST, preferred_element_type=F32
    )
    lane = iota((WIDTH, LANES), 1)
    upper = products[0:WIDTH]
    cross = 0.5 * (products[WIDTH : 2 * WIDTH] + pltpu.roll(upper, LANES - WIDTH, 1))
    gram = pack_square(jnp.where(lane < WIDTH, upper + precond_shift * cross, 0.0))
    for i in range(ROW_PARTS):
        out_ref[i, 0] = gram
        out_ref[i, 1] = products[2 * WIDTH :]


def to_column(row, shift):
    lane = iota((WIDTH, LANES), 1)
    return jnp.sum(
        jnp.where(lane == iota((WIDTH, LANES), 0) + shift, row, 0.0), axis=1, keepdims=True
    )


def to_row(column, shift):
    lane = iota((WIDTH, LANES), 1)
    return jnp.sum(
        jnp.where(lane == iota((WIDTH, LANES), 0) + shift, column, 0.0), axis=0, keepdims=True
    )


def eliminate(work, panel):
    spot = iota((WIDTH, LANES), 0)
    for k in range(0, WIDTH, panel):
        rows = [work[k + i : k + i + 1, :] for i in range(panel)]
        columns = [jnp.broadcast_to(work[:, k + i : k + i + 1], work.shape) for i in range(panel)]
        square = [
            [jnp.broadcast_to(rows[i][:, k + j : k + j + 1], (1, LANES)) for j in range(panel)]
            for i in range(panel)
        ]
        update = jnp.zeros(work.shape, F32)
        for i in range(panel):
            reciprocal = 1.0 / square[i][i]
            for j in range(i + 1, panel):
                factor = square[i][j] * reciprocal
                rows[j] = rows[j] - factor * rows[i]
                columns[j] = columns[j] - factor * columns[i]
                for m in range(j, panel):
                    square[j][m] = square[j][m] - factor * square[i][m]
            update += columns[i] * (rows[i] * reciprocal)
        work = jnp.where(spot >= k + panel, work - update, work)
        for i in range(1, panel):
            work = jnp.where(spot == k + i, rows[i], work)
    return work


def solve_gram(inverse, diagonal, row):
    half = jnp.sum(inverse * pltpu.roll(row, WIDTH, 1), axis=1, keepdims=True) / diagonal
    return jnp.sum(inverse * half, axis=0, keepdims=True)


def factor_body(
    rows_ref, cols_ref, parts_ref, y_ref, rhs_ref, blocks_ref, out_ref, keep_ref, direction_ref, low_ref, acc_ref
):
    total = parts_ref[0]
    for i in range(1, ROW_PARTS):
        total += parts_ref[i]
    lane = iota((WIDTH, LANES), 1)
    spot = iota((WIDTH, LANES), 0)
    work = eliminate(jnp.where(lane == spot + WIDTH, 1.0, unpack_square(total[0])), 4)
    diagonal = jnp.sum(jnp.where(lane == spot, work, 0.0), axis=1, keepdims=True)
    inverse = jnp.where((lane >= WIDTH) & (lane < 2 * WIDTH), work, 0.0)
    sketched_rhs = jnp.where(iota((1, LANES), 1) < WIDTH, total[1, 0:1], 0.0)
    coeffs = solve_gram(inverse, diagonal, sketched_rhs)

    ysketch = y_ref[...]
    rhs = rhs_ref[...]
    direction = (
        rhs - jnp.sum(ysketch * to_column(coeffs, WIDTH), axis=0, keepdims=True)
    ) / precond_shift
    direction_ref[...] = direction
    low_ref[...] = jnp.broadcast_to(direction, low_ref.shape).astype(BF16)

    acc_ref[...] = jnp.zeros(acc_ref.shape, F32)
    for n in range(BLOCKS):
        start = pl.multiple_of(rows_ref[n] * ORDER, ORDER)
        product = jnp.dot(
            low_ref[:, pl.ds(start, ORDER)], blocks_ref[n], preferred_element_type=F32
        )
        acc_ref[cols_ref[n]] += product[0:8]
    row = iota((8, LANES), 0)
    per_block = ORDER // LANES
    for h in range(CORES):
        tile = jnp.zeros((8, LANES), F32)
        for t in range(HALF_TILES):
            j = h * (HALF_TILES // per_block) + t // per_block
            at = LANES * (t % per_block)
            tile = jnp.where(row == t, acc_ref[j, :, at : at + LANES], tile)
        for i in range(ROW_PARTS):
            out_ref[i, h] = tile

    sketched = to_row(jnp.sum(ysketch * direction, axis=1, keepdims=True), WIDTH)
    length = jnp.sum(direction * direction, axis=1, keepdims=True)
    along = jnp.sum(rhs * direction, axis=1, keepdims=True)
    line = iota((1, LANES), 1)
    sums = regularize * jnp.where(line == 2 * WIDTH, length, sketched)
    sums = jnp.where(line == 2 * WIDTH + 1, along, sums)
    keep_ref[0:WIDTH, :] = inverse
    keep_ref[WIDTH : 2 * WIDTH, :] = jnp.broadcast_to(diagonal, (WIDTH, LANES))
    keep_ref[2 * WIDTH : 2 * WIDTH + 8, :] = jnp.broadcast_to(sketched_rhs, (8, LANES))
    keep_ref[2 * WIDTH + 8 :, :] = jnp.broadcast_to(sums, (8, LANES))


def image_body(
    rows_ref, cols_ref, parts_ref, theta_ref, y_ref, direction_ref, blocks_ref, out_ref, scaled_ref, acc_ref
):
    total = parts_ref[0]
    for i in range(1, ROW_PARTS):
        total += parts_ref[i]
    scaled = theta_ref[...] * total
    per_block = ORDER // LANES
    for j in range(LOCAL // ORDER):
        h, first = j // 2, j % 2 * per_block
        line = jnp.concatenate(
            [scaled[h, first + q : first + q + 1, :] for q in range(per_block)], axis=1
        )
        scaled_ref[j] = jnp.broadcast_to(line, (16, ORDER)).astype(BF16)
    acc_ref[...] = jnp.zeros(acc_ref.shape, F32)
    for n in range(BLOCKS):
        product = lax.dot_general(
            scaled_ref[cols_ref[n]], blocks_ref[n], NT, preferred_element_type=F32
        )
        acc_ref[rows_ref[n]] += product[0:8]

    whole = jnp.concatenate([acc_ref[r, 0:1, :] for r in range(LOCAL // ORDER)], axis=1)
    sketched = to_row(jnp.sum(y_ref[...] * whole, axis=1, keepdims=True), WIDTH)
    curvature = jnp.sum(direction_ref[...] * whole, axis=1, keepdims=True)
    sums = jnp.where(iota((1, LANES), 1) == 2 * WIDTH, curvature, sketched)
    sums = jnp.broadcast_to(sums, (8, LANES))
    lane = iota((8, LANES), 1)
    row = iota((8, LANES), 0)
    shares = LANES // WIDTH
    for u in range(TILES // 2):
        pack = sums
        for v in range(2):
            t = 2 * u + v
            at = LANES * (t % per_block)
            tile = acc_ref[t // per_block, :, at : at + LANES]
            for q in range(shares):
                turned = tile if q == 0 else pltpu.roll(tile, LANES - WIDTH * q, 1)
                pack = jnp.where((lane < WIDTH) & (row == shares * v + q), turned, pack)
        out_ref[8 * u : 8 * u + 8, :] = pack


def sums_body(parts_ref, keep_ref, out_ref):
    total = parts_ref[0:8, :]
    for i in range(1, COL_PARTS // 8):
        total += parts_ref[8 * i : 8 * i + 8, :]
    line = jnp.sum(total, axis=0, keepdims=True)
    out_ref[...] = jnp.broadcast_to(line + keep_ref[2 * WIDTH + 8 : 2 * WIDTH + 9, :], (8, LANES))


def step_body(
    me_ref, mine_ref, parts_ref, keep_ref, y_ref, rhs_ref, direction_ref, solution_ref, residual_ref, precond_ref
):
    sums = jnp.sum(parts_ref[...], axis=0, keepdims=True)
    lane = iota((1, LANES), 1)
    inverse = keep_ref[0:WIDTH, :]
    diagonal = keep_ref[WIDTH : 2 * WIDTH, 0:1]
    sketched_rhs = keep_ref[2 * WIDTH : 2 * WIDTH + 1, :]
    curvature = jnp.sum(jnp.where(lane == 2 * WIDTH, sums, 0.0), axis=1, keepdims=True)
    along = jnp.sum(jnp.where(lane == 2 * WIDTH + 1, sums, 0.0), axis=1, keepdims=True)
    alpha = along / curvature

    start = pl.multiple_of((me_ref[0] // 4) * LANES, LANES)
    turn = ((4 - me_ref[0] % 4) % 4) * WIDTH
    ysketch = pltpu.roll(y_ref[:, pl.ds(start, LANES)], turn, 1)
    rhs = pltpu.roll(rhs_ref[:, pl.ds(start, LANES)], turn, 1)
    direction = pltpu.roll(direction_ref[:, pl.ds(start, LANES)], turn, 1)
    image = mine_ref[0:1, :] + regularize * direction
    residual = rhs - alpha * image
    sketched_image = jnp.where(lane < WIDTH, pltpu.roll(sums, LANES - WIDTH, 1), 0.0)
    res_coeffs = solve_gram(inverse, diagonal, sketched_rhs - alpha * sketched_image)
    precond_residual = (
        residual - jnp.sum(ysketch * to_column(res_coeffs, WIDTH), axis=0, keepdims=True)
    ) / precond_shift
    solution_ref[...] = (alpha * direction)[0, :WIDTH]
    residual_ref[...] = residual[0, :WIDTH]
    precond_ref[...] = precond_residual[0, :WIDTH]


def exchange(value, axis):
    return lax.all_to_all(value, axis, 0, 0, tiled=True)


def shards(blocks, block_rows, block_cols, sketch, theta, rhs):
    values = blocks[0, 0]
    rows_idx = block_rows[0, 0]
    cols_idx = block_cols[0, 0]
    omega = sketch.T
    rhs_line = rhs.reshape(1, LOCAL)
    theta_tiles = theta.reshape(CORES, HALF_TILES, LANES)
    my_core = lax.axis_index("core").astype(jnp.int32).reshape(1)
    my_col = lax.axis_index(("y", "far", "near")).astype(jnp.int32).reshape(1)
    shape = jax.ShapeDtypeStruct
    work = 2 * BLOCKS * ORDER * ORDER

    with jax.named_scope("sketch_cols"):
        terms = call(
            sketch_body,
            [smem(), smem(), vmem(), vmem()],
            shape((CORES, WIDTH, HALF), F32),
            flops=work * WIDTH,
            name="sketch_cols",
        )(rows_idx, cols_idx, omega, values)
        parts = lax.all_gather(terms, "core")
        parts = call(
            pair_body, [smem(), vmem()], shape((X_PARTS, WIDTH, HALF), F32), name="pair"
        )(my_core, parts)
        parts = exchange(parts, "x")
    with jax.named_scope("scaled"):
        scaled = call(
            scale_body, [smem(), vmem(), vmem()], shape((WIDTH, HALF), BF16), name="scaled"
        )(my_core, parts, theta_tiles)
        scaled = lax.all_gather(scaled, "core")
    with jax.named_scope("ysketch"):
        terms = call(
            forward_body,
            [smem(), smem(), vmem(), vmem()],
            shape((SHARES, SHARE_TILES, 8, LANES), F32),
            flops=work * WIDTH,
            name="ysketch",
        )(rows_idx, cols_idx, scaled, values)
        share = (SHARE_TILES, 8, LANES)
        parts = exchange(terms, ("y", "near"))
        parts = call(
            spread_body, [vmem()], shape((FAR_PARTS,) + share, F32), name="ysketch_near"
        )(parts)
        parts = exchange(parts, "far")
        parts = call(
            spread_body, [vmem()], shape((SHARES,) + share, F32), name="ysketch_far"
        )(parts)
        tiles = exchange(parts, ("y", "near"))
    with jax.named_scope("gram"):
        ysketch, terms = call(
            gram_body,
            [vmem(), vmem(), vmem()],
            (shape((WIDTH, LOCAL), F32), shape((ROW_PARTS, 2, 8, LANES), F32)),
            scratch=[pltpu.VMEM((LANES, LOCAL), F32)],
            name="gram",
        )(tiles, omega, rhs_line)
        parts = exchange(terms, ("x", "core"))
    with jax.named_scope("direction"):
        terms, keep, direction = call(
            factor_body,
            [smem(), smem(), vmem(), vmem(), vmem(), vmem()],
            (
                shape((ROW_PARTS, CORES, HALF_TILES, LANES), F32),
                shape((2 * WIDTH + 16, LANES), F32),
                shape((1, LOCAL), F32),
            ),
            scratch=[
                pltpu.VMEM((16, LOCAL), BF16),
                pltpu.VMEM((LOCAL // ORDER, 8, ORDER), F32),
            ],
            flops=work,
            name="direction",
        )(rows_idx, cols_idx, parts, ysketch, rhs_line, values)
        parts = exchange(terms, ("x", "core"))
    with jax.named_scope("image"):
        terms = call(
            image_body,
            [smem(), smem(), vmem(), vmem(), vmem(), vmem(), vmem()],
            shape((COL_PARTS, LANES), F32),
            scratch=[
                pltpu.VMEM((LOCAL // ORDER, 16, ORDER), BF16),
                pltpu.VMEM((LOCAL // ORDER, 8, ORDER), F32),
            ],
            flops=work,
            name="image",
        )(rows_idx, cols_idx, parts, theta_tiles, ysketch, direction, values)
        parts = exchange(terms, ("y", "far", "near"))
        terms = call(sums_body, [vmem(), vmem()], shape((ROW_PARTS, LANES), F32), name="sums")(
            parts, keep
        )
        parts = exchange(terms, ("x", "core"))
    with jax.named_scope("step"):
        share = shape((LOCAL // COL_PARTS,), F32)
        return call(
            step_body,
            [smem(), vmem(), vmem(), vmem(), vmem(), vmem(), vmem()],
            (share, share, share),
            name="step",
        )(my_col, terms, parts, keep, ysketch, rhs_line, direction)


def solution(mesh):
    row, col = ("x", "core"), ("y", "far", "near")
    fine = jax.sharding.Mesh(
        mesh.devices.reshape(X_PARTS, CORES, Y_PARTS, FAR_PARTS, NEAR_PARTS),
        ("x", "core", "y", "far", "near"),
    )
    in_specs = (
        P(row, col, None, None, None),
        P(row, col, None),
        P(row, col, None),
        P(row, None),
        P(col),
        P(row),
    )
    out_specs = (P(row + col), P(row + col), P(row + col))
    return jax.shard_map(shards, mesh=fine, in_specs=in_specs, out_specs=out_specs, check_vma=False)
```

time: 127 us -> 135 us (1.063)
  blocking collectives: 93.4 us -> 109 us
  waiting for transfers between devices: 13.1 us -> 4.44 us
    all_to_all x5 -> x7, blocking collectives: 73.2 us -> 97.7 us  [exchange(): return lax.all_to_all(value, axis, 0, 0, tiled=True)]
    all_gather x3 -> x1, blocking collectives: 17.5 us -> 8.68 us  [shards(): parts = lax.all_gather(terms, 'core')]
    all_to_all x1, waiting for transfers between devices: 13.1 us -> 4.44 us  [exchange(): return lax.all_to_all(value, axis, 0, 0, tiled=True)]
where the time goes in v5:
time: 135 us
  blocking collectives  109 us (81%)
  Pallas kernels  10.6 us (8%)
  starting transfers between devices  5.35 us (4%)
  waiting for transfers between devices  4.44 us (3%)
  local copies, waits for them, and re-layouts  4.43 us (3%)
    all_to_all x7, blocking collectives, exchange(): return lax.all_to_all(value, axis, 0, 0, tiled=True)  97.7 us
    all_gather x1, blocking collectives, shards(): parts = lax.all_gather(terms, 'core')  8.68 us
    all_to_all x1, starting transfers between devices, exchange(): return lax.all_to_all(value, axis, 0, 0, tiled=True)  5.35 us
    all_to_all x1, waiting for transfers between devices, exchange(): return lax.all_to_all(value, axis, 0, 0, tiled=True)  4.44 us
    unnamed x20, local copies, waits for them, and re-layouts  4.43 us
    all_gather x1, blocking collectives, shards(): scaled = lax.all_gather(scaled, 'core')  2.75 us
  transfers between devices with their start and end apart: 1, of which 1 were waited for; matrix products, arithmetic and copies ran while one was open for 0% of the time, Pallas kernels for 0%

profile of v5, /device:TPU:1, one launch (start us, length us, event | category | flops | bytes accessed | tf_op | source)
XLA Modules:
  0.0 134.7 jit_solution(14094365262392440915)
XLA Ops:
  0.6 0.0 copy-start.9
  0.6 0.0 copy-start.7
  0.7 0.0 copy-start.5
  0.7 0.0 copy-start
  0.7 2.2 %copy-done = bf16[1,1,8,512,512]{4,3,2,1,0:T(8,128)(2,1)S(1)} copy-done((bf16[1,1,8,512,512]{4,3,2,1,0:T(8,128)(2,1)S(1)}, bf16[1,1,8,512,512]{4,3,2,1,0:T(8,128)(2,1)}, u32[]{:S(2)}) %copy-start) | copy-done | bytes 4194328
  2.9 0.0 copy-start.2
  2.9 0.9 copy-done.2
  3.8 0.0 copy-start.6
  3.8 0.7 copy-done.6
  4.4 0.0 copy-start.8
  4.4 0.7 copy-done.8
  5.1 0.0 copy-start.1
  5.1 1.4 %sketch_cols.1 = f32[2,32,1024]{2,1,0:T(8,128)S(1)} custom-call(s32[8]{0:T(128)S(1)} %bitcast.34, s32[8]{0:T(128)S(1)} %bitcast.38, bf16[32,2048]{1,0:T(8,128)(2,1)S(1)} %bitcast.23, bf16[8,512,512]{2,1,0:T(8,128)(2,1)S(1)} %bitcast.18), custom_call_target="tpu_custom_call" | custom-call | flops 134217728 | bytes 1048576 | tf_op jit(solution)/shard_map/sketch_cols/sketch_cols/pallas_call | solution.py:336
  6.5 8.7 %all-gather = f32[4,32,1024]{2,1,0:T(8,128)S(1)} all-gather(f32[2,32,1024]{2,1,0:T(8,128)S(1)} %sketch_cols.1), channel_id=2, replica_groups=mesh['x'=4,'core'=2,'y'=4,'far'=4,'near'=4] {'core'}, dimensions={0}, use_global_device_ids=true | all-gather | bytes 786432 | tf_op jit(solution)/shard_map/sketch_cols/all_gather | solution.py:343
  15.2 0.0 copy-start.3
  15.2 0.0 copy-start.4
  15.2 11.8 %all_to_all.52.parts_ref = f32[4,32,1024]{2,1,0:T(8,128)S(1)} all-to-all(f32[4,32,1024]{2,1,0:T(8,128)S(1)} %pair.1), channel_id=1, replica_groups=mesh['x'=4,'core'=2,'y'=4,'far'=4,'near'=4] {'x'}, dimensions={0} | all-to-all | bytes 1048576 | tf_op jit(solution)/shard_map/sketch_cols/all_to_all | solution.py:320
  27.0 0.0 copy-done.5
  27.0 2.8 %all-gather.1 = bf16[64,1024]{1,0:T(8,128)(2,1)S(1)} all-gather(bf16[32,1024]{1,0:T(8,128)(2,1)S(1)} %scaled.1), channel_id=3, replica_groups=mesh['x'=4,'core'=2,'y'=4,'far'=4,'near'=4] {'core'}, dimensions={0}, use_global_device_ids=true | all-gather | bytes 196608 | tf_op jit(solution)/shard_map/scaled/all_gather | solution.py:352
  29.7 0.0 copy-done.9
  29.7 0.0 copy-done.7
  29.7 0.0 copy-done.1
  29.8 1.9 %ysketch.1 = f32[16,4,8,128]{3,2,1,0:T(8,128)S(1)} custom-call(s32[8]{0:T(128)S(1)} %bitcast.35, s32[8]{0:T(128)S(1)} %bitcast.39, bf16[2,32,1024]{2,1,0:T(8,128)(2,1)S(1)} %bitcast.25, bf16[8,512,512]{2,1,0:T(8,128)(2,1)S(1)} %bitcast.19), custom_call_target="tpu_custom_call" | custom-call | flops 134217728 | bytes 1048576 | tf_op jit(solution)/shard_map/ysketch/ysketch/pallas_call | solution.py:354
  31.6 14.1 %all_to_all.53.parts_ref = f32[16,4,8,128]{3,2,1,0:T(8,128)S(1)} all-to-all(f32[16,4,8,128]{3,2,1,0:T(8,128)S(1)} %ysketch.1), channel_id=1, replica_groups=mesh['x'=4,'core'=2,'y'=4,'far'=4,'near'=4] {'y','near'}, dimensions={0} | all-to-all | bytes 524288 | tf_op jit(solution)/shard_map/ysketch/all_to_all | solution.py:320
  45.8 23.6 %all_to_all.54.parts_ref = f32[4,4,8,128]{3,2,1,0:T(8,128)S(1)} all-to-all(f32[4,4,8,128]{3,2,1,0:T(8,128)S(1)} %ysketch_near.1), channel_id=1, replica_groups=mesh['x'=4,'core'=2,'y'=4,'far'=4,'near'=4] {'far'}, dimensions={0} | all-to-all | bytes 131072 | tf_op jit(solution)/shard_map/ysketch/all_to_all | solution.py:320
  69.4 11.7 %all_to_all.55.tiles_ref = f32[16,4,8,128]{3,2,1,0:T(8,128)S(1)} all-to-all(f32[16,4,8,128]{3,2,1,0:T(8,128)S(1)} %ysketch_far.1), channel_id=1, replica_groups=mesh['x'=4,'core'=2,'y'=4,'far'=4,'near'=4] {'y','near'}, dimensions={0} | all-to-all | bytes 524288 | tf_op jit(solution)/shard_map/ysketch/all_to_all | solution.py:320
  81.1 0.0 copy-done.3
  81.1 0.0 copy-done.4
  81.1 0.7 gram.1
  81.8 11.2 %all_to_all.56.parts_ref = f32[8,2,8,128]{3,2,1,0:T(8,128)S(1)} all-to-all(f32[8,2,8,128]{3,2,1,0:T(8,128)S(1)} %get-tuple-element.8), channel_id=1, replica_groups=mesh['x'=4,'core'=2,'y'=4,'far'=4,'near'=4] {'x','core'}, dimensions={0} | all-to-all | bytes 131072 | tf_op jit(solution)/shard_map/gram/all_to_all | solution.py:320
  93.0 2.4 %direction.1 = (f32[8,2,8,128]{3,2,1,0:T(8,128)S(1)}, f32[80,128]{1,0:T(8,128)S(1)}, f32[1,2048]{1,0:T(1,128)S(1)}) custom-call(s32[8]{0:T(128)S(1)} %bitcast.36, s32[8]{0:T(128)S(1)} %bitcast.40, f32[8,2,8,128]{3,2,1,0:T(8,128)S(1)} %all_to_all.56.parts_ref, f32[32,2048]{1,0:T(8,128)S(1)} %get-tuple-element.9.y_ref, f32[1,2048]{1,0:T(1,128)S(1)} %bitcast.29, ...), custom_call_target="tpu_custom_call" | custom-call | flops 4194304 | bytes 1048576 | tf_op jit(solution)/shard_map/direction/direction/pallas_call | solution.py:381
  95.4 8.0 %all_to_all.57.parts_ref = f32[8,2,8,128]{3,2,1,0:T(8,128)S(1)} all-to-all(f32[8,2,8,128]{3,2,1,0:T(8,128)S(1)} %get-tuple-element.10), channel_id=1, replica_groups=mesh['x'=4,'core'=2,'y'=4,'far'=4,'near'=4] {'x','core'}, dimensions={0} | all-to-all | bytes 131072 | tf_op jit(solution)/shard_map/direction/all_to_all | solution.py:320
  103.4 1.9 %image.1 = f32[64,128]{1,0:T(8,128)S(1)} custom-call(s32[8]{0:T(128)S(1)} %bitcast.37, s32[8]{0:T(128)S(1)} %bitcast.41, f32[8,2,8,128]{3,2,1,0:T(8,128)S(1)} %all_to_all.57.parts_ref, f32[2,8,128]{2,1,0:T(8,128)S(1)} %bitcast.32, f32[32,2048]{1,0:T(8,128)S(1)} %get-tuple-element.9.y_ref, f32[1,2048]{1,0:T(1,128)S(1)} %get-tuple-element.11.direction_ref, ...), custom_call_target="tpu_custom_call" | custom-call | flops 4194304 | bytes 1048576 | tf_op jit(solution)/shard_map/image/image/pallas_call | solution.py:398
  105.3 17.4 %all_to_all.58 = f32[64,1,128]{2,1,0:T(1,128)S(1)} all-to-all(f32[64,1,128]{2,1,0:T(1,128)S(1)} %bitcast.26), channel_id=1, replica_groups=mesh['x'=4,'core'=2,'y'=4,'far'=4,'near'=4] {'y','far','near'}, dimensions={0} | all-to-all | bytes 65536 | tf_op jit(solution)/shard_map/image/all_to_all | solution.py:320
  122.7 0.6 sums.1.mine_ref
  123.3 5.3 %all-to-all-start.7 = ((f32[8,1,128]{2,1,0:T(1,128)}), f32[8,1,128]{2,1,0:T(1,128)S(1)}, u32[]{:S(2)}, u32[]{:S(2)}) async-start(f32[8,1,128]{2,1,0:T(1,128)} %bitcast.14), calls=%async_computation.7 | async-start | bytes 8192 | tf_op jit(solution)/shard_map/image/all_to_all | solution.py:320
  128.7 4.4 %all-to-all-done.7 = f32[8,1,128]{2,1,0:T(1,128)S(1)} async-done(((f32[8,1,128]{2,1,0:T(1,128)}), f32[8,1,128]{2,1,0:T(1,128)S(1)}, u32[]{:S(2)}, u32[]{:S(2)}) %all-to-all-start.7) | async-done | bytes 4128 | tf_op jit(solution)/shard_map/image/all_to_all | solution.py:320
  133.1 1.6 %step.1 = (f32[32]{0:T(128)}, f32[32]{0:T(128)}, f32[32]{0:T(128)}) custom-call(s32[1]{0:T(128)} %bitcast.me_ref, f32[8,128]{1,0:T(8,128)} %sums.1.mine_ref, f32[8,128]{1,0:T(8,128)S(1)} %bitcast.33, f32[80,128]{1,0:T(8,128)S(1)} %get-tuple-element.12.keep_ref, f32[32,2048]{1,0:T(8,128)S(1)} %get-tuple-element.9.y_ref, f32[1,2048]{1,0:T(1,128)S(1)} %bitcast.30, ...), custom_call_target="tpu_custom_call" | custom-call | bytes 1048576 | tf_op jit(solution)/shard_map/step/step/pallas_call | solution.py:416
  (4 shorter events, 0.1 us)
Async XLA Ops:
  0.6 29.1 %copy-start.9 = (s32[1,1,8]{2,1,0:T(1,128)S(1)}, s32[1,1,8]{2,1,0:T(1,128)}, u32[]{:S(2)}) copy-start(s32[1,1,8]{2,1,0:T(1,128)} %param.8) | copy-start | bytes 100
  0.6 29.1 %copy-start.7 = (s32[1,1,8]{2,1,0:T(1,128)S(1)}, s32[1,1,8]{2,1,0:T(1,128)}, u32[]{:S(2)}) copy-start(s32[1,1,8]{2,1,0:T(1,128)} %param.7) | copy-start | bytes 100
  0.7 26.3 %copy-start.5 = (f32[2048]{0:T(1024)S(1)}, f32[2048]{0:T(1024)}, u32[]{:S(2)}) copy-start(f32[2048]{0:T(1024)} %param.10) | copy-start | bytes 24580
  0.7 2.2 %copy-start = (bf16[1,1,8,512,512]{4,3,2,1,0:T(8,128)(2,1)S(1)}, bf16[1,1,8,512,512]{4,3,2,1,0:T(8,128)(2,1)}, u32[]{:S(2)}) copy-start(bf16[1,1,8,512,512]{4,3,2,1,0:T(8,128)(2,1)} %param.6) | copy-start | bytes 12582916
  2.9 0.9 copy-start.2
  3.8 0.7 copy-start.6
  4.4 0.7 copy-start.8
  5.1 24.7 %copy-start.1 = (bf16[1,1,8,512,512]{4,3,2,1,0:T(8,128)(2,1)S(1)}, bf16[1,1,8,512,512]{4,3,2,1,0:T(8,128)(2,1)}, u32[]{:S(2)}) copy-start(bf16[1,1,8,512,512]{4,3,2,1,0:T(8,128)(2,1)} %param.6) | copy-start | bytes 12582916
  15.2 65.9 %copy-start.3 = (bf16[2048,32]{0,1:T(8,128)(2,1)S(1)}, bf16[2048,32]{0,1:T(8,128)(2,1)}, u32[]{:S(2)}) copy-start(bf16[2048,32]{0,1:T(8,128)(2,1)} %param.9) | copy-start | bytes 393220
  15.2 65.9 %copy-start.4 = (f32[2048]{0:T(1024)S(1)}, f32[2048]{0:T(1024)}, u32[]{:S(2)}) copy-start(f32[2048]{0:T(1024)} %param.11) | copy-start | bytes 24580
  123.3 9.8 %all-to-all-start.7 = ((f32[8,1,128]{2,1,0:T(1,128)}), f32[8,1,128]{2,1,0:T(1,128)S(1)}, u32[]{:S(2)}, u32[]{:S(2)}) async-start(f32[8,1,128]{2,1,0:T(1,128)} %bitcast.14), calls=%async_computation.7 | async-start | bytes 8192 | tf_op jit(solution)/shard_map/image/all_to_all | solution.py:320

commit v6 on v5

--- a/solution.py
+++ b/solution.py
@@ -10,6 +10,7 @@
 
 F32 = jnp.float32
 BF16 = jnp.bfloat16
+I16 = jnp.int16
 HIGHEST = lax.Precision.HIGHEST
 LANES = 128
 CORES = 2
@@ -23,6 +24,7 @@
 ORDER = 512
 LOCAL = 2048
 WIDTH = 32
+TINY = 2.0**-100
 HALF = LOCAL // CORES
 HALF_TILES = HALF // LANES
 TILES = LOCAL // LANES
@@ -60,39 +62,53 @@
     )
 
 
-def sketch_body(rows_ref, cols_ref, omega_ref, blocks_ref, out_ref):
+def sketch_body(places_ref, omega_ref, blocks_ref, out_ref):
     out_ref[...] = jnp.zeros(out_ref.shape, F32)
     for n in range(BLOCKS):
-        start = pl.multiple_of(rows_ref[n] * ORDER, ORDER)
-        place = pl.multiple_of(cols_ref[n] % 2 * ORDER, ORDER)
-        out_ref[cols_ref[n] // 2, :, pl.ds(place, ORDER)] += jnp.dot(
+        start = pl.multiple_of(places_ref[n] * ORDER, ORDER)
+        place = pl.multiple_of(places_ref[BLOCKS + n] % 2 * ORDER, ORDER)
+        out_ref[places_ref[BLOCKS + n] // 2, :, pl.ds(place, ORDER)] += jnp.dot(
             omega_ref[:, pl.ds(start, ORDER)], blocks_ref[n], preferred_element_type=F32
         )
+
+
+def scale_of(mantissa, power):
+    return mantissa * jnp.exp2(power - 14.0)
 
 
 def pair_body(core_ref, parts_ref, out_ref):
     half = core_ref[0]
     total = parts_ref[0, half] + parts_ref[1, half]
+    largest = jnp.maximum(jnp.max(jnp.abs(total), axis=1, keepdims=True), TINY)
+    power = jnp.ceil(jnp.log2(largest))
+    mantissa = jnp.ceil(largest * jnp.exp2(14.0 - power))
+    coded = jnp.round(total * (32000.0 / scale_of(mantissa, power))).astype(jnp.int32).astype(I16)
+    unit = jnp.where(iota((WIDTH, LANES), 1) == 0, power, mantissa).astype(jnp.int32).astype(I16)
     for i in range(X_PARTS):
-        out_ref[i] = total
+        out_ref[i, :, :HALF] = coded
+        out_ref[i, :, HALF:] = unit
 
 
 def scale_body(core_ref, parts_ref, theta_ref, out_ref):
-    total = (parts_ref[0] + parts_ref[1]) + (parts_ref[2] + parts_ref[3])
+    total = jnp.zeros(out_ref.shape, F32)
+    for i in range(X_PARTS):
+        unit = parts_ref[i, :, HALF:].astype(jnp.int32).astype(F32)
+        coded = parts_ref[i, :, :HALF].astype(jnp.int32).astype(F32)
+        total += coded * (scale_of(unit[:, 1:2], unit[:, 0:1]) / 32000.0)
     tile = theta_ref[core_ref[0]]
     theta = jnp.concatenate([tile[t : t + 1, :] for t in range(HALF_TILES)], axis=1)
     out_ref[...] = (theta * total).astype(BF16)
 
 
-def forward_body(rows_ref, cols_ref, scaled_ref, blocks_ref, out_ref):
+def forward_body(places_ref, scaled_ref, blocks_ref, out_ref):
     out_ref[...] = jnp.zeros(out_ref.shape, F32)
     for n in range(BLOCKS):
-        place = pl.multiple_of(cols_ref[n] % 2 * ORDER, ORDER)
-        left = scaled_ref[cols_ref[n] // 2, :, pl.ds(place, ORDER)]
+        place = pl.multiple_of(places_ref[BLOCKS + n] % 2 * ORDER, ORDER)
+        left = scaled_ref[places_ref[BLOCKS + n] // 2, :, pl.ds(place, ORDER)]
         product = lax.dot_general(left, blocks_ref[n], NT, preferred_element_type=F32)
         for g in range(GROUPS):
             for q in range(ORDER // LANES):
-                out_ref[g * (LOCAL // ORDER) + rows_ref[n], q] += product[8 * g : 8 * g + 8, LANES * q : LANES * (q + 1)]
+                out_ref[g * (LOCAL // ORDER) + places_ref[n], q] += product[8 * g : 8 * g + 8, LANES * q : LANES * (q + 1)]
 
 
 def spread_body(parts_ref, out_ref):
@@ -187,7 +203,7 @@
 
 
 def factor_body(
-    rows_ref, cols_ref, parts_ref, y_ref, rhs_ref, blocks_ref, out_ref, keep_ref, direction_ref, low_ref, acc_ref
+    places_ref, parts_ref, y_ref, rhs_ref, blocks_ref, out_ref, keep_ref, direction_ref, low_ref, acc_ref
 ):
     total = parts_ref[0]
     for i in range(1, ROW_PARTS):
@@ -210,11 +226,11 @@
 
     acc_ref[...] = jnp.zeros(acc_ref.shape, F32)
     for n in range(BLOCKS):
-        start = pl.multiple_of(rows_ref[n] * ORDER, ORDER)
+        start = pl.multiple_of(places_ref[n] * ORDER, ORDER)
         product = jnp.dot(
             low_ref[:, pl.ds(start, ORDER)], blocks_ref[n], preferred_element_type=F32
         )
-        acc_ref[cols_ref[n]] += product[0:8]
+        acc_ref[places_ref[BLOCKS + n]] += product[0:8]
     row = iota((8, LANES), 0)
     per_block = ORDER // LANES
     for h in range(CORES):
@@ -226,12 +242,12 @@
         for i in range(ROW_PARTS):
             out_ref[i, h] = tile
 
-    sketched = to_row(jnp.sum(ysketch * direction, axis=1, keepdims=True), WIDTH)
+    sketched = to_row(jnp.sum(ysketch * direction, axis=1, keepdims=True), 3 * WIDTH)
     length = jnp.sum(direction * direction, axis=1, keepdims=True)
     along = jnp.sum(rhs * direction, axis=1, keepdims=True)
     line = iota((1, LANES), 1)
-    sums = regularize * jnp.where(line == 2 * WIDTH, length, sketched)
-    sums = jnp.where(line == 2 * WIDTH + 1, along, sums)
+    sums = jnp.where(line == 2 * WIDTH + 1, length, sketched)
+    sums = jnp.where(line == 2 * WIDTH + 2, along, sums)
     keep_ref[0:WIDTH, :] = inverse
     keep_ref[WIDTH : 2 * WIDTH, :] = jnp.broadcast_to(diagonal, (WIDTH, LANES))
     keep_ref[2 * WIDTH : 2 * WIDTH + 8, :] = jnp.broadcast_to(sketched_rhs, (8, LANES))
@@ -239,7 +255,17 @@
 
 
 def image_body(
-    rows_ref, cols_ref, parts_ref, theta_ref, y_ref, direction_ref, blocks_ref, out_ref, scaled_ref, acc_ref
+    places_ref,
+    parts_ref,
+    theta_ref,
+    y_ref,
+    direction_ref,
+    keep_ref,
+    blocks_ref,
+    out_ref,
+    sums_ref,
+    scaled_ref,
+    acc_ref,
 ):
     total = parts_ref[0]
     for i in range(1, ROW_PARTS):
@@ -255,48 +281,72 @@
     acc_ref[...] = jnp.zeros(acc_ref.shape, F32)
     for n in range(BLOCKS):
         product = lax.dot_general(
-            scaled_ref[cols_ref[n]], blocks_ref[n], NT, preferred_element_type=F32
+            scaled_ref[places_ref[BLOCKS + n]], blocks_ref[n], NT, preferred_element_type=F32
         )
-        acc_ref[rows_ref[n]] += product[0:8]
+        acc_ref[places_ref[n]] += product[0:8]
 
     whole = jnp.concatenate([acc_ref[r, 0:1, :] for r in range(LOCAL // ORDER)], axis=1)
     sketched = to_row(jnp.sum(y_ref[...] * whole, axis=1, keepdims=True), WIDTH)
     curvature = jnp.sum(direction_ref[...] * whole, axis=1, keepdims=True)
     sums = jnp.where(iota((1, LANES), 1) == 2 * WIDTH, curvature, sketched)
-    sums = jnp.broadcast_to(sums, (8, LANES))
+    sums += keep_ref[2 * WIDTH + 8 : 2 * WIDTH + 9, :]
+    sums_ref[...] = jnp.broadcast_to(sums, sums_ref.shape)
+    row = iota((8, LANES), 0)
+    for h in range(CORES):
+        tile = jnp.zeros((8, LANES), F32)
+        for t in range(HALF_TILES):
+            r, at = (h * HALF_TILES + t) // per_block, LANES * (t % per_block)
+            tile = jnp.where(row == t, acc_ref[r, :, at : at + LANES], tile)
+        out_ref[h] = tile
+
+
+def lines_body(image_ref, parts_ref, out_ref, sums_ref):
+    sums = jnp.sum(parts_ref[...], axis=0, keepdims=True)
+    sums_ref[...] = jnp.broadcast_to(sums, sums_ref.shape)
     lane = iota((8, LANES), 1)
     row = iota((8, LANES), 0)
     shares = LANES // WIDTH
+    added = jnp.broadcast_to(
+        jnp.where(iota((1, LANES), 1) <= 2 * WIDTH, sums, 0.0), (8, LANES)
+    )
     for u in range(TILES // 2):
-        pack = sums
+        pack = added
         for v in range(2):
             t = 2 * u + v
-            at = LANES * (t % per_block)
-            tile = acc_ref[t // per_block, :, at : at + LANES]
+            line = image_ref[t // HALF_TILES, t % HALF_TILES : t % HALF_TILES + 1, :]
             for q in range(shares):
-                turned = tile if q == 0 else pltpu.roll(tile, LANES - WIDTH * q, 1)
+                turned = line if q == 0 else pltpu.roll(line, LANES - WIDTH * q, 1)
                 pack = jnp.where((lane < WIDTH) & (row == shares * v + q), turned, pack)
         out_ref[8 * u : 8 * u + 8, :] = pack
 
 
-def sums_body(parts_ref, keep_ref, out_ref):
+def step_body(
+    me_ref,
+    parts_ref,
+    sums_ref,
+    keep_ref,
+    y_ref,
+    rhs_ref,
+    direction_ref,
+    solution_ref,
+    residual_ref,
+    precond_ref,
+):
     total = parts_ref[0:8, :]
     for i in range(1, COL_PARTS // 8):
         total += parts_ref[8 * i : 8 * i + 8, :]
-    line = jnp.sum(total, axis=0, keepdims=True)
-    out_ref[...] = jnp.broadcast_to(line + keep_ref[2 * WIDTH + 8 : 2 * WIDTH + 9, :], (8, LANES))
-
-
-def step_body(
-    me_ref, mine_ref, parts_ref, keep_ref, y_ref, rhs_ref, direction_ref, solution_ref, residual_ref, precond_ref
-):
-    sums = jnp.sum(parts_ref[...], axis=0, keepdims=True)
+    total = jnp.sum(total, axis=0, keepdims=True)
+    sums = sums_ref[0:1, :]
     lane = iota((1, LANES), 1)
     inverse = keep_ref[0:WIDTH, :]
     diagonal = keep_ref[WIDTH : 2 * WIDTH, 0:1]
     sketched_rhs = keep_ref[2 * WIDTH : 2 * WIDTH + 1, :]
-    curvature = jnp.sum(jnp.where(lane == 2 * WIDTH, sums, 0.0), axis=1, keepdims=True)
-    along = jnp.sum(jnp.where(lane == 2 * WIDTH + 1, sums, 0.0), axis=1, keepdims=True)
+
+    def pick(line, at):
+        return jnp.sum(jnp.where(lane == at, line, 0.0), axis=1, keepdims=True)
+
+    along = pick(sums, 2 * WIDTH + 2)
+    curvature = pick(total, 2 * WIDTH) + regularize * pick(sums, 2 * WIDTH + 1)
     alpha = along / curvature
 
     start = pl.multiple_of((me_ref[0] // 4) * LANES, LANES)
@@ -304,9 +354,10 @@
     ysketch = pltpu.roll(y_ref[:, pl.ds(start, LANES)], turn, 1)
     rhs = pltpu.roll(rhs_ref[:, pl.ds(start, LANES)], turn, 1)
     direction = pltpu.roll(direction_ref[:, pl.ds(start, LANES)], turn, 1)
-    image = mine_ref[0:1, :] + regularize * direction
+    image = total + regularize * direction
     residual = rhs - alpha * image
-    sketched_image = jnp.where(lane < WIDTH, pltpu.roll(sums, LANES - WIDTH, 1), 0.0)
+    sketched_image = pltpu.roll(total, LANES - WIDTH, 1) + regularize * pltpu.roll(sums, WIDTH, 1)
+    sketched_image = jnp.where(lane < WIDTH, sketched_image, 0.0)
     res_coeffs = solve_gram(inverse, diagonal, sketched_rhs - alpha * sketched_image)
     precond_residual = (
         residual - jnp.sum(ysketch * to_column(res_coeffs, WIDTH), axis=0, keepdims=True)
@@ -322,8 +373,7 @@
 
 def shards(blocks, block_rows, block_cols, sketch, theta, rhs):
     values = blocks[0, 0]
-    rows_idx = block_rows[0, 0]
-    cols_idx = block_cols[0, 0]
+    places = jnp.concatenate([block_rows[0, 0], block_cols[0, 0]])
     omega = sketch.T
     rhs_line = rhs.reshape(1, LOCAL)
     theta_tiles = theta.reshape(CORES, HALF_TILES, LANES)
@@ -335,14 +385,14 @@
     with jax.named_scope("sketch_cols"):
         terms = call(
             sketch_body,
-            [smem(), smem(), vmem(), vmem()],
+            [smem(), vmem(), vmem()],
             shape((CORES, WIDTH, HALF), F32),
             flops=work * WIDTH,
             name="sketch_cols",
-        )(rows_idx, cols_idx, omega, values)
+        )(places, omega, values)
         parts = lax.all_gather(terms, "core")
         parts = call(
-            pair_body, [smem(), vmem()], shape((X_PARTS, WIDTH, HALF), F32), name="pair"
+            pair_body, [smem(), vmem()], shape((X_PARTS, WIDTH, HALF + LANES), I16), name="pair"
         )(my_core, parts)
         parts = exchange(parts, "x")
     with jax.named_scope("scaled"):
@@ -353,11 +403,11 @@
     with jax.named_scope("ysketch"):
         terms = call(
             forward_body,
-            [smem(), smem(), vmem(), vmem()],
+            [smem(), vmem(), vmem()],
             shape((SHARES, SHARE_TILES, 8, LANES), F32),
             flops=work * WIDTH,
             name="ysketch",
-        )(rows_idx, cols_idx, scaled, values)
+        )(places, scaled, values)
         share = (SHARE_TILES, 8, LANES)
         parts = exchange(terms, ("y", "near"))
         parts = call(
@@ -380,7 +430,7 @@
     with jax.named_scope("direction"):
         terms, keep, direction = call(
             factor_body,
-            [smem(), smem(), vmem(), vmem(), vmem(), vmem()],
+            [smem(), vmem(), vmem(), vmem(), vmem()],
             (
                 shape((ROW_PARTS, CORES, HALF_TILES, LANES), F32),
                 shape((2 * WIDTH + 16, LANES), F32),
@@ -392,25 +442,28 @@
             ],
             flops=work,
             name="direction",
-        )(rows_idx, cols_idx, parts, ysketch, rhs_line, values)
+        )(places, parts, ysketch, rhs_line, values)
         parts = exchange(terms, ("x", "core"))
     with jax.named_scope("image"):
-        terms = call(
+        image, terms = call(
             image_body,
-            [smem(), smem(), vmem(), vmem(), vmem(), vmem(), vmem()],
-            shape((COL_PARTS, LANES), F32),
+            [smem()] + [vmem()] * 6,
+            (shape((CORES, HALF_TILES, LANES), F32), shape((ROW_PARTS, LANES), F32)),
             scratch=[
                 pltpu.VMEM((LOCAL // ORDER, 16, ORDER), BF16),
                 pltpu.VMEM((LOCAL // ORDER, 8, ORDER), F32),
             ],
             flops=work,
             name="image",
-        )(rows_idx, cols_idx, parts, theta_tiles, ysketch, direction, values)
+        )(places, parts, theta_tiles, ysketch, direction, keep, values)
+        parts = exchange(terms, ("x", "core"))
+        terms, sums = call(
+            lines_body,
+            [vmem(), vmem()],
+            (shape((COL_PARTS, LANES), F32), shape((8, LANES), F32)),
+            name="lines",
+        )(image, parts)
         parts = exchange(terms, ("y", "far", "near"))
-        terms = call(sums_body, [vmem(), vmem()], shape((ROW_PARTS, LANES), F32), name="sums")(
-            parts, keep
-        )
-        parts = exchange(terms, ("x", "core"))
     with jax.named_scope("step"):
         share = shape((LOCAL // COL_PARTS,), F32)
         return call(
@@ -418,7 +471,7 @@
             [smem(), vmem(), vmem(), vmem(), vmem(), vmem(), vmem()],
             (share, share, share),
             name="step",
-        )(my_col, terms, parts, keep, ysketch, rhs_line, direction)
+        )(my_col, parts, sums, keep, ysketch, rhs_line, direction)
 
 
 def solution(mesh):

time: 135 us -> 130 us (0.963)
  blocking collectives: 109 us -> 96.9 us
  waiting for transfers between devices: 4.44 us -> 13.3 us
    all_to_all x7, blocking collectives: 97.7 us -> 85.3 us  [exchange(): return lax.all_to_all(value, axis, 0, 0, tiled=True)]
    all_to_all x1, waiting for transfers between devices: 4.44 us -> 13.3 us  [exchange(): return lax.all_to_all(value, axis, 0, 0, tiled=True)]
    unnamed x20 -> x12, local copies, waits for them, and re-layouts: 4.43 us -> 3.11 us
where the time goes in v6:
time: 130 us
  blocking collectives  96.9 us (75%)
  waiting for transfers between devices  13.3 us (10%)
  Pallas kernels  10.2 us (8%)
  starting transfers between devices  4.6 us (4%)
  local copies, waits for them, and re-layouts  3.11 us (2%)
    all_to_all x7, blocking collectives, exchange(): return lax.all_to_all(value, axis, 0, 0, tiled=True)  85.3 us
    all_to_all x1, waiting for transfers between devices, exchange(): return lax.all_to_all(value, axis, 0, 0, tiled=True)  13.3 us
    all_gather x1, blocking collectives, shards(): parts = lax.all_gather(terms, 'core')  8.68 us
    all_to_all x1, starting transfers between devices, exchange(): return lax.all_to_all(value, axis, 0, 0, tiled=True)  4.6 us
    unnamed x12, local copies, waits for them, and re-layouts  3.11 us
    all_gather x1, blocking collectives, shards(): scaled = lax.all_gather(scaled, 'core')  2.9 us
  transfers between devices with their start and end apart: 1, of which 1 were waited for; matrix products, arithmetic and copies ran while one was open for 0% of the time, Pallas kernels for 0%

profile of v6, /device:TPU:1, one launch (start us, length us, event | category | flops | bytes accessed | tf_op | source)
XLA Modules:
  0.0 129.6 jit_solution(6531336465218451451)
XLA Ops:
  0.6 0.0 copy-start.5
  0.6 0.7 pad_add_fusion.places_ref
  1.4 0.0 copy-start
  1.4 2.2 %copy-done = bf16[1,1,8,512,512]{4,3,2,1,0:T(8,128)(2,1)S(1)} copy-done((bf16[1,1,8,512,512]{4,3,2,1,0:T(8,128)(2,1)S(1)}, bf16[1,1,8,512,512]{4,3,2,1,0:T(8,128)(2,1)}, u32[]{:S(2)}) %copy-start) | copy-done | bytes 4194328
  3.6 0.0 copy-start.2
  3.6 0.9 copy-done.2
  4.5 0.0 copy-start.1
  4.5 1.4 %sketch_cols.1 = f32[2,32,1024]{2,1,0:T(8,128)S(1)} custom-call(s32[16]{0:T(128)S(1)} %pad_add_fusion.places_ref, bf16[32,2048]{1,0:T(8,128)(2,1)S(1)} %bitcast.23, bf16[8,512,512]{2,1,0:T(8,128)(2,1)S(1)} %bitcast.18), custom_call_target="tpu_custom_call" | custom-call | flops 134217728 | bytes 1048576 | tf_op jit(solution)/shard_map/sketch_cols/sketch_cols/pallas_call | solution.py:386
  5.8 8.7 %all-gather = f32[4,32,1024]{2,1,0:T(8,128)S(1)} all-gather(f32[2,32,1024]{2,1,0:T(8,128)S(1)} %sketch_cols.1), channel_id=2, replica_groups=mesh['x'=4,'core'=2,'y'=4,'far'=4,'near'=4] {'core'}, dimensions={0}, use_global_device_ids=true | all-gather | bytes 786432 | tf_op jit(solution)/shard_map/sketch_cols/all_gather | solution.py:393
  14.5 0.0 copy-start.3
  14.5 0.0 copy-start.4
  14.5 0.1 pair.1
  14.7 9.0 %all_to_all.52.parts_ref = s16[4,32,1152]{2,1,0:T(8,128)(2,1)S(1)} all-to-all(s16[4,32,1152]{2,1,0:T(8,128)(2,1)S(1)} %pair.1), channel_id=1, replica_groups=mesh['x'=4,'core'=2,'y'=4,'far'=4,'near'=4] {'x'}, dimensions={0} | all-to-all | bytes 589824 | tf_op jit(solution)/shard_map/sketch_cols/all_to_all | solution.py:371
  23.7 0.0 copy-done.5
  23.7 0.2 scaled.1
  23.9 2.9 %all-gather.1 = bf16[64,1024]{1,0:T(8,128)(2,1)S(1)} all-gather(bf16[32,1024]{1,0:T(8,128)(2,1)S(1)} %scaled.1), channel_id=3, replica_groups=mesh['x'=4,'core'=2,'y'=4,'far'=4,'near'=4] {'core'}, dimensions={0}, use_global_device_ids=true | all-gather | bytes 196608 | tf_op jit(solution)/shard_map/scaled/all_gather | solution.py:402
  26.8 0.0 copy-done.1
  26.8 1.9 %ysketch.1 = f32[16,4,8,128]{3,2,1,0:T(8,128)S(1)} custom-call(s32[16]{0:T(128)S(1)} %pad_add_fusion.places_ref, bf16[2,32,1024]{2,1,0:T(8,128)(2,1)S(1)} %bitcast.25, bf16[8,512,512]{2,1,0:T(8,128)(2,1)S(1)} %bitcast.19), custom_call_target="tpu_custom_call" | custom-call | flops 134217728 | bytes 1048576 | tf_op jit(solution)/shard_map/ysketch/ysketch/pallas_call | solution.py:404
  28.6 14.2 %all_to_all.53.parts_ref = f32[16,4,8,128]{3,2,1,0:T(8,128)S(1)} all-to-all(f32[16,4,8,128]{3,2,1,0:T(8,128)S(1)} %ysketch.1), channel_id=1, replica_groups=mesh['x'=4,'core'=2,'y'=4,'far'=4,'near'=4] {'y','near'}, dimensions={0} | all-to-all | bytes 524288 | tf_op jit(solution)/shard_map/ysketch/all_to_all | solution.py:371
  42.8 23.6 %all_to_all.54.parts_ref = f32[4,4,8,128]{3,2,1,0:T(8,128)S(1)} all-to-all(f32[4,4,8,128]{3,2,1,0:T(8,128)S(1)} %ysketch_near.1), channel_id=1, replica_groups=mesh['x'=4,'core'=2,'y'=4,'far'=4,'near'=4] {'far'}, dimensions={0} | all-to-all | bytes 131072 | tf_op jit(solution)/shard_map/ysketch/all_to_all | solution.py:371
  66.4 11.7 %all_to_all.55.tiles_ref = f32[16,4,8,128]{3,2,1,0:T(8,128)S(1)} all-to-all(f32[16,4,8,128]{3,2,1,0:T(8,128)S(1)} %ysketch_far.1), channel_id=1, replica_groups=mesh['x'=4,'core'=2,'y'=4,'far'=4,'near'=4] {'y','near'}, dimensions={0} | all-to-all | bytes 524288 | tf_op jit(solution)/shard_map/ysketch/all_to_all | solution.py:371
  78.1 0.0 copy-done.3
  78.1 0.0 copy-done.4
  78.1 0.7 gram.1
  78.9 11.2 %all_to_all.56.parts_ref = f32[8,2,8,128]{3,2,1,0:T(8,128)S(1)} all-to-all(f32[8,2,8,128]{3,2,1,0:T(8,128)S(1)} %get-tuple-element.12), channel_id=1, replica_groups=mesh['x'=4,'core'=2,'y'=4,'far'=4,'near'=4] {'x','core'}, dimensions={0} | all-to-all | bytes 131072 | tf_op jit(solution)/shard_map/gram/all_to_all | solution.py:371
  90.1 2.4 %direction.1 = (f32[8,2,8,128]{3,2,1,0:T(8,128)S(1)}, f32[80,128]{1,0:T(8,128)S(1)}, f32[1,2048]{1,0:T(1,128)S(1)}) custom-call(s32[16]{0:T(128)S(1)} %pad_add_fusion.places_ref, f32[8,2,8,128]{3,2,1,0:T(8,128)S(1)} %all_to_all.56.parts_ref, f32[32,2048]{1,0:T(8,128)S(1)} %get-tuple-element.13.y_ref, f32[1,2048]{1,0:T(1,128)S(1)} %bitcast.28, ...), custom_call_target="tpu_custom_call" | custom-call | flops 4194304 | bytes 1048576 | tf_op jit(solution)/shard_map/direction/direction/pallas_call | solution.py:431
  92.5 8.0 %all_to_all.57.parts_ref = f32[8,2,8,128]{3,2,1,0:T(8,128)S(1)} all-to-all(f32[8,2,8,128]{3,2,1,0:T(8,128)S(1)} %get-tuple-element.14), channel_id=1, replica_groups=mesh['x'=4,'core'=2,'y'=4,'far'=4,'near'=4] {'x','core'}, dimensions={0} | all-to-all | bytes 131072 | tf_op jit(solution)/shard_map/direction/all_to_all | solution.py:371
  100.4 1.9 %image.1 = (f32[2,8,128]{2,1,0:T(8,128)S(1)}, f32[8,128]{1,0:T(8,128)S(1)}) custom-call(s32[16]{0:T(128)S(1)} %pad_add_fusion.places_ref, f32[8,2,8,128]{3,2,1,0:T(8,128)S(1)} %all_to_all.57.parts_ref, f32[2,8,128]{2,1,0:T(8,128)S(1)} %bitcast.31, f32[32,2048]{1,0:T(8,128)S(1)} %get-tuple-element.13.y_ref, f32[1,2048]{1,0:T(1,128)S(1)} %get-tuple-element.15.direction_ref, ...), custom_call_target="tpu_custom_call" | custom-call | flops 4194304 | bytes 1048576 | tf_op jit(solution)/shard_map/image/image/pallas_call | solution.py:448
  102.3 7.7 %all_to_all.58 = f32[8,1,128]{2,1,0:T(1,128)S(1)} all-to-all(f32[8,1,128]{2,1,0:T(1,128)S(1)} %bitcast.33), channel_id=1, replica_groups=mesh['x'=4,'core'=2,'y'=4,'far'=4,'near'=4] {'x','core'}, dimensions={0} | all-to-all | bytes 8192 | tf_op jit(solution)/shard_map/image/all_to_all | solution.py:371
  110.0 0.7 lines.1
  110.7 4.6 %all-to-all-start.7 = ((f32[64,1,128]{2,1,0:T(1,128)}), f32[64,1,128]{2,1,0:T(1,128)S(1)}, u32[]{:S(2)}, u32[]{:S(2)}) async-start(f32[64,1,128]{2,1,0:T(1,128)} %bitcast.14), calls=%async_computation.7 | async-start | bytes 65536 | tf_op jit(solution)/shard_map/image/all_to_all | solution.py:371
  115.4 13.3 %all-to-all-done.7 = f32[64,1,128]{2,1,0:T(1,128)S(1)} async-done(((f32[64,1,128]{2,1,0:T(1,128)}), f32[64,1,128]{2,1,0:T(1,128)S(1)}, u32[]{:S(2)}, u32[]{:S(2)}) %all-to-all-start.7) | async-done | bytes 32800 | tf_op jit(solution)/shard_map/image/all_to_all | solution.py:371
  128.6 0.9 step.1
  (2 shorter events, 0.0 us)
Async XLA Ops:
  0.6 23.0 %copy-start.5 = (f32[2048]{0:T(1024)S(1)}, f32[2048]{0:T(1024)}, u32[]{:S(2)}) copy-start(f32[2048]{0:T(1024)} %param.10) | copy-start | bytes 24580
  1.4 2.2 %copy-start = (bf16[1,1,8,512,512]{4,3,2,1,0:T(8,128)(2,1)S(1)}, bf16[1,1,8,512,512]{4,3,2,1,0:T(8,128)(2,1)}, u32[]{:S(2)}) copy-start(bf16[1,1,8,512,512]{4,3,2,1,0:T(8,128)(2,1)} %param.6) | copy-start | bytes 12582916
  3.6 0.9 copy-start.2
  4.5 22.3 %copy-start.1 = (bf16[1,1,8,512,512]{4,3,2,1,0:T(8,128)(2,1)S(1)}, bf16[1,1,8,512,512]{4,3,2,1,0:T(8,128)(2,1)}, u32[]{:S(2)}) copy-start(bf16[1,1,8,512,512]{4,3,2,1,0:T(8,128)(2,1)} %param.6) | copy-start | bytes 12582916
  14.5 63.6 %copy-start.3 = (bf16[2048,32]{0,1:T(8,128)(2,1)S(1)}, bf16[2048,32]{0,1:T(8,128)(2,1)}, u32[]{:S(2)}) copy-start(bf16[2048,32]{0,1:T(8,128)(2,1)} %param.9) | copy-start | bytes 393220
  14.5 63.6 %copy-start.4 = (f32[2048]{0:T(1024)S(1)}, f32[2048]{0:T(1024)}, u32[]{:S(2)}) copy-start(f32[2048]{0:T(1024)} %param.11) | copy-start | bytes 24580
  110.7 17.9 %all-to-all-start.7 = ((f32[64,1,128]{2,1,0:T(1,128)}), f32[64,1,128]{2,1,0:T(1,128)S(1)}, u32[]{:S(2)}, u32[]{:S(2)}) async-start(f32[64,1,128]{2,1,0:T(1,128)} %bitcast.14), calls=%async_computation.7 | async-start | bytes 65536 | tf_op jit(solution)/shard_map/image/all_to_all | solution.py:371

commit v7 on v6

--- a/solution.py
+++ b/solution.py
@@ -62,7 +62,8 @@
     )
 
 
-def sketch_body(places_ref, omega_ref, blocks_ref, out_ref):
+def sketch_body(me_ref, places_ref, omega_ref, blocks_ref, out_ref):
+    del me_ref
     out_ref[...] = jnp.zeros(out_ref.shape, F32)
     for n in range(BLOCKS):
         start = pl.multiple_of(places_ref[n] * ORDER, ORDER)
@@ -76,12 +77,30 @@
     return mantissa * jnp.exp2(power - 14.0)
 
 
-def pair_body(core_ref, parts_ref, out_ref):
-    half = core_ref[0]
+def unit_of(largest):
+    largest = jnp.maximum(largest, TINY)
+    power = jnp.ceil(jnp.log2(largest))
+    return power, jnp.ceil(largest * jnp.exp2(14.0 - power))
+
+
+def encode(tiles, power, mantissa):
+    factor = 32000.0 / scale_of(mantissa, power)
+    unit = jnp.where(iota((8, LANES), 1) == 0, power, mantissa)
+    rows = jnp.concatenate([tile * factor for tile in tiles] + [unit], axis=0)
+    return jnp.round(rows).astype(jnp.int32).astype(I16)
+
+
+def decode(coded):
+    rows = coded.astype(jnp.int32).astype(F32)
+    unit = rows[8 * SHARE_TILES :]
+    factor = scale_of(unit[:, 1:2], unit[:, 0:1]) / 32000.0
+    return [rows[8 * q : 8 * q + 8] * factor for q in range(SHARE_TILES)]
+
+
+def pair_body(me_ref, parts_ref, out_ref):
+    half = lax.rem(me_ref[0], CORES)
     total = parts_ref[0, half] + parts_ref[1, half]
-    largest = jnp.maximum(jnp.max(jnp.abs(total), axis=1, keepdims=True), TINY)
-    power = jnp.ceil(jnp.log2(largest))
-    mantissa = jnp.ceil(largest * jnp.exp2(14.0 - power))
+    power, mantissa = unit_of(jnp.max(jnp.abs(total), axis=1, keepdims=True))
     coded = jnp.round(total * (32000.0 / scale_of(mantissa, power))).astype(jnp.int32).astype(I16)
     unit = jnp.where(iota((WIDTH, LANES), 1) == 0, power, mantissa).astype(jnp.int32).astype(I16)
     for i in range(X_PARTS):
@@ -89,34 +108,52 @@
         out_ref[i, :, HALF:] = unit
 
 
-def scale_body(core_ref, parts_ref, theta_ref, out_ref):
+def scale_body(me_ref, parts_ref, theta_ref, out_ref):
     total = jnp.zeros(out_ref.shape, F32)
     for i in range(X_PARTS):
         unit = parts_ref[i, :, HALF:].astype(jnp.int32).astype(F32)
         coded = parts_ref[i, :, :HALF].astype(jnp.int32).astype(F32)
         total += coded * (scale_of(unit[:, 1:2], unit[:, 0:1]) / 32000.0)
-    tile = theta_ref[core_ref[0]]
+    tile = theta_ref[lax.rem(me_ref[0], CORES)]
     theta = jnp.concatenate([tile[t : t + 1, :] for t in range(HALF_TILES)], axis=1)
     out_ref[...] = (theta * total).astype(BF16)
 
 
-def forward_body(places_ref, scaled_ref, blocks_ref, out_ref):
-    out_ref[...] = jnp.zeros(out_ref.shape, F32)
+def forward_body(places_ref, scaled_ref, blocks_ref, out_ref, acc_ref):
+    acc_ref[...] = jnp.zeros(acc_ref.shape, F32)
     for n in range(BLOCKS):
         place = pl.multiple_of(places_ref[BLOCKS + n] % 2 * ORDER, ORDER)
         left = scaled_ref[places_ref[BLOCKS + n] // 2, :, pl.ds(place, ORDER)]
         product = lax.dot_general(left, blocks_ref[n], NT, preferred_element_type=F32)
         for g in range(GROUPS):
             for q in range(ORDER // LANES):
-                out_ref[g * (LOCAL // ORDER) + places_ref[n], q] += product[8 * g : 8 * g + 8, LANES * q : LANES * (q + 1)]
-
-
-def spread_body(parts_ref, out_ref):
-    sums = [parts_ref[i] for i in range(parts_ref.shape[0])]
+                acc_ref[g * (LOCAL // ORDER) + places_ref[n], q] += product[
+                    8 * g : 8 * g + 8, LANES * q : LANES * (q + 1)
+                ]
+    per_group = SHARES // GROUPS
+    for g in range(GROUPS):
+        part = acc_ref[per_group * g : per_group * (g + 1)]
+        largest = jnp.max(jnp.max(jnp.max(jnp.abs(part), axis=0), axis=0), axis=1, keepdims=True)
+        power, mantissa = unit_of(largest)
+        for u in range(per_group):
+            out_ref[per_group * g + u] = encode(
+                [part[u, q] for q in range(SHARE_TILES)], power, mantissa
+            )
+
+
+def near_body(parts_ref, out_ref):
+    sums = [decode(parts_ref[i]) for i in range(SHARES)]
     while len(sums) > 1:
-        sums = [a + b for a, b in zip(sums[::2], sums[1::2])]
-    for i in range(out_ref.shape[0]):
-        out_ref[i] = sums[0]
+        sums = [[a + b for a, b in zip(*pair)] for pair in zip(sums[::2], sums[1::2])]
+    for i in range(FAR_PARTS):
+        for q in range(SHARE_TILES):
+            out_ref[i, q] = sums[0][q]
+
+
+def far_body(parts_ref, out_ref):
+    total = (parts_ref[0] + parts_ref[1]) + (parts_ref[2] + parts_ref[3])
+    for i in range(SHARES):
+        out_ref[i] = total
 
 
 def pack_square(square):
@@ -133,11 +170,11 @@
 
 
 def gram_body(tiles_ref, omega_ref, rhs_ref, y_ref, out_ref, all_ref):
-    for g in range(GROUPS):
-        for t in range(TILES):
-            y_ref[8 * g : 8 * g + 8, LANES * t : LANES * (t + 1)] = tiles_ref[
-                (g * TILES + t) // SHARE_TILES, t % SHARE_TILES
-            ]
+    for i in range(SHARES):
+        g, first = i // (SHARES // GROUPS), i % (SHARES // GROUPS) * SHARE_TILES
+        for q in range(SHARE_TILES):
+            at = LANES * (first + q)
+            y_ref[8 * g : 8 * g + 8, at : at + LANES] = tiles_ref[i, q]
     omega = omega_ref[...].astype(F32)
     ysketch = y_ref[...] + regularize * omega
     y_ref[...] = ysketch
@@ -300,7 +337,18 @@
         out_ref[h] = tile
 
 
-def lines_body(image_ref, parts_ref, out_ref, sums_ref):
+def lines_body(
+    me_ref, image_ref, parts_ref, y_ref, rhs_ref, direction_ref, out_ref, sums_ref, mine_ref
+):
+    shares = LANES // WIDTH
+    column = lax.div(me_ref[0], CORES)
+    start = pl.multiple_of(lax.div(column, shares) * LANES, LANES)
+    turn = lax.rem(shares - lax.rem(column, shares), shares) * WIDTH
+    mine_ref[0:WIDTH, :] = pltpu.roll(y_ref[:, pl.ds(start, LANES)], turn, 1)
+    rhs = jnp.broadcast_to(rhs_ref[:, pl.ds(start, LANES)], (8, LANES))
+    mine_ref[WIDTH : WIDTH + 8, :] = pltpu.roll(rhs, turn, 1)
+    direction = jnp.broadcast_to(direction_ref[:, pl.ds(start, LANES)], (8, LANES))
+    mine_ref[WIDTH + 8 :, :] = pltpu.roll(direction, turn, 1)
     sums = jnp.sum(parts_ref[...], axis=0, keepdims=True)
     sums_ref[...] = jnp.broadcast_to(sums, sums_ref.shape)
     lane = iota((8, LANES), 1)
@@ -321,16 +369,7 @@
 
 
 def step_body(
-    me_ref,
-    parts_ref,
-    sums_ref,
-    keep_ref,
-    y_ref,
-    rhs_ref,
-    direction_ref,
-    solution_ref,
-    residual_ref,
-    precond_ref,
+    parts_ref, sums_ref, keep_ref, mine_ref, solution_ref, residual_ref, precond_ref
 ):
     total = parts_ref[0:8, :]
     for i in range(1, COL_PARTS // 8):
@@ -349,11 +388,9 @@
     curvature = pick(total, 2 * WIDTH) + regularize * pick(sums, 2 * WIDTH + 1)
     alpha = along / curvature
 
-    start = pl.multiple_of((me_ref[0] // 4) * LANES, LANES)
-    turn = ((4 - me_ref[0] % 4) % 4) * WIDTH
-    ysketch = pltpu.roll(y_ref[:, pl.ds(start, LANES)], turn, 1)
-    rhs = pltpu.roll(rhs_ref[:, pl.ds(start, LANES)], turn, 1)
-    direction = pltpu.roll(direction_ref[:, pl.ds(start, LANES)], turn, 1)
+    ysketch = mine_ref[0:WIDTH, :]
+    rhs = mine_ref[WIDTH : WIDTH + 1, :]
+    direction = mine_ref[WIDTH + 8 : WIDTH + 9, :]
     image = total + regularize * direction
     residual = rhs - alpha * image
     sketched_image = pltpu.roll(total, LANES - WIDTH, 1) + regularize * pltpu.roll(sums, WIDTH, 1)
@@ -373,49 +410,55 @@
 
 def shards(blocks, block_rows, block_cols, sketch, theta, rhs):
     values = blocks[0, 0]
-    places = jnp.concatenate([block_rows[0, 0], block_cols[0, 0]])
     omega = sketch.T
     rhs_line = rhs.reshape(1, LOCAL)
     theta_tiles = theta.reshape(CORES, HALF_TILES, LANES)
-    my_core = lax.axis_index("core").astype(jnp.int32).reshape(1)
-    my_col = lax.axis_index(("y", "far", "near")).astype(jnp.int32).reshape(1)
+    places = jnp.concatenate([block_rows[0, 0], block_cols[0, 0]])
+    me = lax.axis_index("core") + CORES * lax.axis_index(("y", "far", "near"))
+    me = me.astype(jnp.int32).reshape(1)
     shape = jax.ShapeDtypeStruct
     work = 2 * BLOCKS * ORDER * ORDER
 
     with jax.named_scope("sketch_cols"):
         terms = call(
             sketch_body,
-            [smem(), vmem(), vmem()],
+            [smem(), smem(), vmem(), vmem()],
             shape((CORES, WIDTH, HALF), F32),
             flops=work * WIDTH,
             name="sketch_cols",
-        )(places, omega, values)
+        )(me, places, omega, values)
         parts = lax.all_gather(terms, "core")
         parts = call(
             pair_body, [smem(), vmem()], shape((X_PARTS, WIDTH, HALF + LANES), I16), name="pair"
-        )(my_core, parts)
+        )(me, parts)
         parts = exchange(parts, "x")
     with jax.named_scope("scaled"):
         scaled = call(
             scale_body, [smem(), vmem(), vmem()], shape((WIDTH, HALF), BF16), name="scaled"
-        )(my_core, parts, theta_tiles)
+        )(me, parts, theta_tiles)
         scaled = lax.all_gather(scaled, "core")
     with jax.named_scope("ysketch"):
         terms = call(
             forward_body,
             [smem(), vmem(), vmem()],
-            shape((SHARES, SHARE_TILES, 8, LANES), F32),
+            shape((SHARES, 8 * SHARE_TILES + 8, LANES), I16),
+            scratch=[pltpu.VMEM((SHARES, SHARE_TILES, 8, LANES), F32)],
             flops=work * WIDTH,
             name="ysketch",
         )(places, scaled, values)
-        share = (SHARE_TILES, 8, LANES)
         parts = exchange(terms, ("y", "near"))
         parts = call(
-            spread_body, [vmem()], shape((FAR_PARTS,) + share, F32), name="ysketch_near"
+            near_body,
+            [vmem()],
+            shape((FAR_PARTS, SHARE_TILES, 8, LANES), F32),
+            name="ysketch_near",
         )(parts)
         parts = exchange(parts, "far")
         parts = call(
-            spread_body, [vmem()], shape((SHARES,) + share, F32), name="ysketch_far"
+            far_body,
+            [vmem()],
+            shape((SHARES, SHARE_TILES, 8, LANES), F32),
+            name="ysketch_far",
         )(parts)
         tiles = exchange(parts, ("y", "near"))
     with jax.named_scope("gram"):
@@ -457,21 +500,25 @@
             name="image",
         )(places, parts, theta_tiles, ysketch, direction, keep, values)
         parts = exchange(terms, ("x", "core"))
-        terms, sums = call(
+        terms, sums, mine = call(
             lines_body,
-            [vmem(), vmem()],
-            (shape((COL_PARTS, LANES), F32), shape((8, LANES), F32)),
+            [smem()] + [vmem()] * 5,
+            (
+                shape((COL_PARTS, LANES), F32),
+                shape((8, LANES), F32),
+                shape((WIDTH + 16, LANES), F32),
+            ),
             name="lines",
-        )(image, parts)
+        )(me, image, parts, ysketch, rhs_line, direction)
         parts = exchange(terms, ("y", "far", "near"))
     with jax.named_scope("step"):
         share = shape((LOCAL // COL_PARTS,), F32)
         return call(
             step_body,
-            [smem(), vmem(), vmem(), vmem(), vmem(), vmem(), vmem()],
+            [vmem()] * 4,
             (share, share, share),
             name="step",
-        )(my_col, parts, sums, keep, ysketch, rhs_line, direction)
+        )(parts, sums, keep, mine)
 
 
 def solution(mesh):

time: 130 us -> 128 us (0.985)
  blocking collectives: 96.9 us -> 112 us
  waiting for transfers between devices: 13.3 us -> 0 us
  starting transfers between devices: 4.6 us -> 0 us
    all_to_all x7 -> x8, blocking collectives: 85.3 us -> 101 us  [exchange(): return lax.all_to_all(value, axis, 0, 0, tiled=True)]
    all_to_all x1 -> x0, waiting for transfers between devices: 13.3 us -> none  [exchange(): return lax.all_to_all(value, axis, 0, 0, tiled=True)]
    all_to_all x1 -> x0, starting transfers between devices: 4.6 us -> none  [exchange(): return lax.all_to_all(value, axis, 0, 0, tiled=True)]
  transfers between devices with their start and end apart: 1 -> 0, of which waited for: 1 -> 0; matrix products, arithmetic and copies ran while one was open for 0% -> 0% of each run, Pallas kernels for 0% -> 0%
where the time goes in v7:
time: 128 us; the launch traced here: 127 us
  blocking collectives  112 us (88%)
  Pallas kernels  9.97 us (8%)
  local copies, waits for them, and re-layouts  3.11 us (2%)
    all_to_all x8, blocking collectives, exchange(): return lax.all_to_all(value, axis, 0, 0, tiled=True)  101 us
    all_gather x1, blocking collectives, shards(): parts = lax.all_gather(terms, 'core')  8.68 us
    unnamed x12, local copies, waits for them, and re-layouts  3.11 us
    all_gather x1, blocking collectives, shards(): scaled = lax.all_gather(scaled, 'core')  2.9 us

profile of v7, /device:TPU:1, one launch (start us, length us, event | category | flops | bytes accessed | tf_op | source)
XLA Modules:
  0.0 127.0 jit_solution(4274706814950726715)
XLA Ops:
  0.6 0.0 copy-start.5
  0.7 0.7 pad_add_fusion.places_ref
  1.4 0.0 copy-start
  1.4 2.2 %copy-done = bf16[1,1,8,512,512]{4,3,2,1,0:T(8,128)(2,1)S(1)} copy-done((bf16[1,1,8,512,512]{4,3,2,1,0:T(8,128)(2,1)S(1)}, bf16[1,1,8,512,512]{4,3,2,1,0:T(8,128)(2,1)}, u32[]{:S(2)}) %copy-start) | copy-done | bytes 4194328
  3.6 0.0 copy-start.2
  3.6 0.9 copy-done.2
  4.5 0.0 copy-start.1
  4.5 1.4 %sketch_cols.1 = f32[2,32,1024]{2,1,0:T(8,128)S(1)} custom-call(s32[1]{0:T(128)} %bitcast.me_ref, s32[16]{0:T(128)S(1)} %pad_add_fusion.places_ref, bf16[32,2048]{1,0:T(8,128)(2,1)S(1)} %bitcast.22, bf16[8,512,512]{2,1,0:T(8,128)(2,1)S(1)} %bitcast.17), custom_call_target="tpu_custom_call" | custom-call | flops 134217728 | bytes 1048576 | tf_op jit(solution)/shard_map/sketch_cols/sketch_cols/pallas_call | solution.py:423
  5.9 8.7 %all-gather = f32[4,32,1024]{2,1,0:T(8,128)S(1)} all-gather(f32[2,32,1024]{2,1,0:T(8,128)S(1)} %sketch_cols.1), channel_id=2, replica_groups=mesh['x'=4,'core'=2,'y'=4,'far'=4,'near'=4] {'core'}, dimensions={0}, use_global_device_ids=true | all-gather | bytes 786432 | tf_op jit(solution)/shard_map/sketch_cols/all_gather | solution.py:430
  14.5 0.0 copy-start.3
  14.5 0.0 copy-start.4
  14.5 0.1 pair.1
  14.7 9.0 %all_to_all.52.parts_ref = s16[4,32,1152]{2,1,0:T(8,128)(2,1)S(1)} all-to-all(s16[4,32,1152]{2,1,0:T(8,128)(2,1)S(1)} %pair.1), channel_id=1, replica_groups=mesh['x'=4,'core'=2,'y'=4,'far'=4,'near'=4] {'x'}, dimensions={0} | all-to-all | bytes 589824 | tf_op jit(solution)/shard_map/sketch_cols/all_to_all | solution.py:408
  23.7 0.0 copy-done.5
  23.7 0.2 scaled.1
  23.9 2.9 %all-gather.1 = bf16[64,1024]{1,0:T(8,128)(2,1)S(1)} all-gather(bf16[32,1024]{1,0:T(8,128)(2,1)S(1)} %scaled.1), channel_id=3, replica_groups=mesh['x'=4,'core'=2,'y'=4,'far'=4,'near'=4] {'core'}, dimensions={0}, use_global_device_ids=true | all-gather | bytes 196608 | tf_op jit(solution)/shard_map/scaled/all_gather | solution.py:439
  26.8 0.0 copy-done.1
  26.8 2.0 %ysketch.1 = s16[16,40,128]{2,1,0:T(8,128)(2,1)S(1)} custom-call(s32[16]{0:T(128)S(1)} %pad_add_fusion.places_ref, bf16[2,32,1024]{2,1,0:T(8,128)(2,1)S(1)} %bitcast.24, bf16[8,512,512]{2,1,0:T(8,128)(2,1)S(1)} %bitcast.18), custom_call_target="tpu_custom_call" | custom-call | flops 134217728 | bytes 1048576 | tf_op jit(solution)/shard_map/ysketch/ysketch/pallas_call | solution.py:441
  28.8 11.6 %all_to_all.53.parts_ref = s16[16,40,128]{2,1,0:T(8,128)(2,1)S(1)} all-to-all(s16[16,40,128]{2,1,0:T(8,128)(2,1)S(1)} %ysketch.1), channel_id=1, replica_groups=mesh['x'=4,'core'=2,'y'=4,'far'=4,'near'=4] {'y','near'}, dimensions={0} | all-to-all | bytes 327680 | tf_op jit(solution)/shard_map/ysketch/all_to_all | solution.py:408
  40.4 0.2 ysketch_near.1
  40.6 23.7 %all_to_all.54.parts_ref = f32[4,4,8,128]{3,2,1,0:T(8,128)S(1)} all-to-all(f32[4,4,8,128]{3,2,1,0:T(8,128)S(1)} %ysketch_near.1), channel_id=1, replica_groups=mesh['x'=4,'core'=2,'y'=4,'far'=4,'near'=4] {'far'}, dimensions={0} | all-to-all | bytes 131072 | tf_op jit(solution)/shard_map/ysketch/all_to_all | solution.py:408
  64.3 12.1 %all_to_all.55.tiles_ref = f32[16,4,8,128]{3,2,1,0:T(8,128)S(1)} all-to-all(f32[16,4,8,128]{3,2,1,0:T(8,128)S(1)} %ysketch_far.1), channel_id=1, replica_groups=mesh['x'=4,'core'=2,'y'=4,'far'=4,'near'=4] {'y','near'}, dimensions={0} | all-to-all | bytes 524288 | tf_op jit(solution)/shard_map/ysketch/all_to_all | solution.py:408
  76.5 0.0 copy-done.3
  76.5 0.0 copy-done.4
  76.5 0.8 gram.1
  77.2 11.3 %all_to_all.56.parts_ref = f32[8,2,8,128]{3,2,1,0:T(8,128)S(1)} all-to-all(f32[8,2,8,128]{3,2,1,0:T(8,128)S(1)} %get-tuple-element.13), channel_id=1, replica_groups=mesh['x'=4,'core'=2,'y'=4,'far'=4,'near'=4] {'x','core'}, dimensions={0} | all-to-all | bytes 131072 | tf_op jit(solution)/shard_map/gram/all_to_all | solution.py:408
  88.5 2.4 %direction.1 = (f32[8,2,8,128]{3,2,1,0:T(8,128)S(1)}, f32[80,128]{1,0:T(8,128)S(1)}, f32[1,2048]{1,0:T(1,128)S(1)}) custom-call(s32[16]{0:T(128)S(1)} %pad_add_fusion.places_ref, f32[8,2,8,128]{3,2,1,0:T(8,128)S(1)} %all_to_all.56.parts_ref, f32[32,2048]{1,0:T(8,128)S(1)} %get-tuple-element.14.y_ref, f32[1,2048]{1,0:T(1,128)S(1)} %bitcast.27, ...), custom_call_target="tpu_custom_call" | custom-call | flops 4194304 | bytes 1048576 | tf_op jit(solution)/shard_map/direction/direction/pallas_call | solution.py:474
  90.9 8.0 %all_to_all.57.parts_ref = f32[8,2,8,128]{3,2,1,0:T(8,128)S(1)} all-to-all(f32[8,2,8,128]{3,2,1,0:T(8,128)S(1)} %get-tuple-element.15), channel_id=1, replica_groups=mesh['x'=4,'core'=2,'y'=4,'far'=4,'near'=4] {'x','core'}, dimensions={0} | all-to-all | bytes 131072 | tf_op jit(solution)/shard_map/direction/all_to_all | solution.py:408
  98.9 1.9 %image.1 = (f32[2,8,128]{2,1,0:T(8,128)S(1)}, f32[8,128]{1,0:T(8,128)S(1)}) custom-call(s32[16]{0:T(128)S(1)} %pad_add_fusion.places_ref, f32[8,2,8,128]{3,2,1,0:T(8,128)S(1)} %all_to_all.57.parts_ref, f32[2,8,128]{2,1,0:T(8,128)S(1)} %bitcast.30, f32[32,2048]{1,0:T(8,128)S(1)} %get-tuple-element.14.y_ref, f32[1,2048]{1,0:T(1,128)S(1)} %get-tuple-element.16.direction_ref, ...), custom_call_target="tpu_custom_call" | custom-call | flops 4194304 | bytes 1048576 | tf_op jit(solution)/shard_map/image/image/pallas_call | solution.py:491
  100.8 7.7 %all_to_all.58 = f32[8,1,128]{2,1,0:T(1,128)S(1)} all-to-all(f32[8,1,128]{2,1,0:T(1,128)S(1)} %bitcast.33), channel_id=1, replica_groups=mesh['x'=4,'core'=2,'y'=4,'far'=4,'near'=4] {'x','core'}, dimensions={0} | all-to-all | bytes 8192 | tf_op jit(solution)/shard_map/image/all_to_all | solution.py:408
  108.5 0.1 lines.1
  108.6 17.5 %all_to_all.59 = f32[64,1,128]{2,1,0:T(1,128)S(1)} all-to-all(f32[64,1,128]{2,1,0:T(1,128)S(1)} %bitcast.31), channel_id=1, replica_groups=mesh['x'=4,'core'=2,'y'=4,'far'=4,'near'=4] {'y','far','near'}, dimensions={0} | all-to-all | bytes 65536 | tf_op jit(solution)/shard_map/image/all_to_all | solution.py:408
  126.1 0.9 step.1
  (1 shorter events, 0.0 us)
Async XLA Ops:
  0.6 23.0 %copy-start.5 = (f32[2048]{0:T(1024)S(1)}, f32[2048]{0:T(1024)}, u32[]{:S(2)}) copy-start(f32[2048]{0:T(1024)} %param.10) | copy-start | bytes 24580
  1.4 2.2 %copy-start = (bf16[1,1,8,512,512]{4,3,2,1,0:T(8,128)(2,1)S(1)}, bf16[1,1,8,512,512]{4,3,2,1,0:T(8,128)(2,1)}, u32[]{:S(2)}) copy-start(bf16[1,1,8,512,512]{4,3,2,1,0:T(8,128)(2,1)} %param.6) | copy-start | bytes 12582916
  3.6 0.9 copy-start.2
  4.5 22.3 %copy-start.1 = (bf16[1,1,8,512,512]{4,3,2,1,0:T(8,128)(2,1)S(1)}, bf16[1,1,8,512,512]{4,3,2,1,0:T(8,128)(2,1)}, u32[]{:S(2)}) copy-start(bf16[1,1,8,512,512]{4,3,2,1,0:T(8,128)(2,1)} %param.6) | copy-start | bytes 12582916
  14.5 61.9 %copy-start.3 = (bf16[2048,32]{0,1:T(8,128)(2,1)S(1)}, bf16[2048,32]{0,1:T(8,128)(2,1)}, u32[]{:S(2)}) copy-start(bf16[2048,32]{0,1:T(8,128)(2,1)} %param.9) | copy-start | bytes 393220
  14.5 61.9 %copy-start.4 = (f32[2048]{0:T(1024)S(1)}, f32[2048]{0:T(1024)}, u32[]{:S(2)}) copy-start(f32[2048]{0:T(1024)} %param.11) | copy-start | bytes 24580

commit v8 on v7

--- a/solution.py
+++ b/solution.py
@@ -62,13 +62,17 @@
     )
 
 
+def place_of(places_ref, n):
+    return lax.bitwise_and(lax.shift_right_logical(places_ref[0], 2 * n), 3)
+
+
 def sketch_body(me_ref, places_ref, omega_ref, blocks_ref, out_ref):
     del me_ref
     out_ref[...] = jnp.zeros(out_ref.shape, F32)
     for n in range(BLOCKS):
-        start = pl.multiple_of(places_ref[n] * ORDER, ORDER)
-        place = pl.multiple_of(places_ref[BLOCKS + n] % 2 * ORDER, ORDER)
-        out_ref[places_ref[BLOCKS + n] // 2, :, pl.ds(place, ORDER)] += jnp.dot(
+        start = pl.multiple_of(place_of(places_ref, n) * ORDER, ORDER)
+        place = pl.multiple_of(place_of(places_ref, BLOCKS + n) % 2 * ORDER, ORDER)
+        out_ref[place_of(places_ref, BLOCKS + n) // 2, :, pl.ds(place, ORDER)] += jnp.dot(
             omega_ref[:, pl.ds(start, ORDER)], blocks_ref[n], preferred_element_type=F32
         )
 
@@ -122,12 +126,12 @@
 def forward_body(places_ref, scaled_ref, blocks_ref, out_ref, acc_ref):
     acc_ref[...] = jnp.zeros(acc_ref.shape, F32)
     for n in range(BLOCKS):
-        place = pl.multiple_of(places_ref[BLOCKS + n] % 2 * ORDER, ORDER)
-        left = scaled_ref[places_ref[BLOCKS + n] // 2, :, pl.ds(place, ORDER)]
+        place = pl.multiple_of(place_of(places_ref, BLOCKS + n) % 2 * ORDER, ORDER)
+        left = scaled_ref[place_of(places_ref, BLOCKS + n) // 2, :, pl.ds(place, ORDER)]
         product = lax.dot_general(left, blocks_ref[n], NT, preferred_element_type=F32)
         for g in range(GROUPS):
             for q in range(ORDER // LANES):
-                acc_ref[g * (LOCAL // ORDER) + places_ref[n], q] += product[
+                acc_ref[g * (LOCAL // ORDER) + place_of(places_ref, n), q] += product[
                     8 * g : 8 * g + 8, LANES * q : LANES * (q + 1)
                 ]
     per_group = SHARES // GROUPS
@@ -247,7 +251,7 @@
         total += parts_ref[i]
     lane = iota((WIDTH, LANES), 1)
     spot = iota((WIDTH, LANES), 0)
-    work = eliminate(jnp.where(lane == spot + WIDTH, 1.0, unpack_square(total[0])), 4)
+    work = eliminate(jnp.where(lane == spot + WIDTH, 1.0, unpack_square(total[0])), 8)
     diagonal = jnp.sum(jnp.where(lane == spot, work, 0.0), axis=1, keepdims=True)
     inverse = jnp.where((lane >= WIDTH) & (lane < 2 * WIDTH), work, 0.0)
     sketched_rhs = jnp.where(iota((1, LANES), 1) < WIDTH, total[1, 0:1], 0.0)
@@ -263,11 +267,11 @@
 
     acc_ref[...] = jnp.zeros(acc_ref.shape, F32)
     for n in range(BLOCKS):
-        start = pl.multiple_of(places_ref[n] * ORDER, ORDER)
+        start = pl.multiple_of(place_of(places_ref, n) * ORDER, ORDER)
         product = jnp.dot(
             low_ref[:, pl.ds(start, ORDER)], blocks_ref[n], preferred_element_type=F32
         )
-        acc_ref[places_ref[BLOCKS + n]] += product[0:8]
+        acc_ref[place_of(places_ref, BLOCKS + n)] += product[0:8]
     row = iota((8, LANES), 0)
     per_block = ORDER // LANES
     for h in range(CORES):
@@ -318,9 +322,9 @@
     acc_ref[...] = jnp.zeros(acc_ref.shape, F32)
     for n in range(BLOCKS):
         product = lax.dot_general(
-            scaled_ref[places_ref[BLOCKS + n]], blocks_ref[n], NT, preferred_element_type=F32
+            scaled_ref[place_of(places_ref, BLOCKS + n)], blocks_ref[n], NT, preferred_element_type=F32
         )
-        acc_ref[places_ref[n]] += product[0:8]
+        acc_ref[place_of(places_ref, n)] += product[0:8]
 
     whole = jnp.concatenate([acc_ref[r, 0:1, :] for r in range(LOCAL // ORDER)], axis=1)
     sketched = to_row(jnp.sum(y_ref[...] * whole, axis=1, keepdims=True), WIDTH)
@@ -414,8 +418,11 @@
     rhs_line = rhs.reshape(1, LOCAL)
     theta_tiles = theta.reshape(CORES, HALF_TILES, LANES)
     places = jnp.concatenate([block_rows[0, 0], block_cols[0, 0]])
+    places = jnp.sum(jnp.left_shift(places, 2 * jnp.arange(2 * BLOCKS, dtype=jnp.int32)))
     me = lax.axis_index("core") + CORES * lax.axis_index(("y", "far", "near"))
-    me = me.astype(jnp.int32).reshape(1)
+    me = me.astype(jnp.int32)
+    places = (places + lax.shift_right_arithmetic(me, 30)).reshape(1)
+    me = me.reshape(1)
     shape = jax.ShapeDtypeStruct
     work = 2 * BLOCKS * ORDER * ORDER
 

time: 128 us -> 126 us (0.984)
  Pallas kernels: 9.97 us -> 7.51 us
    reduce_sum x0 -> x1, other arithmetic: none -> 1.38 us  [shards(): jnp.sum(jnp.left_shift(places, 2 * jnp.arange(2 * BLOCKS, dtype=jnp.int32)))]
where the time goes in v8:
time: 126 us
  blocking collectives  113 us (90%)
  Pallas kernels  7.51 us (6%)
  local copies, waits for them, and re-layouts  3.1 us (2%)
  other arithmetic  1.38 us (1%)
  between operations  1.37 us (1%)
    all_to_all x8, blocking collectives, exchange(): return lax.all_to_all(value, axis, 0, 0, tiled=True)  101 us
    all_gather x1, blocking collectives, shards(): parts = lax.all_gather(terms, 'core')  8.81 us
    unnamed x12, local copies, waits for them, and re-layouts  3.1 us
    all_gather x1, blocking collectives, shards(): scaled = lax.all_gather(scaled, 'core')  2.9 us

profile of v8, /device:TPU:1, one launch (start us, length us, event | category | flops | bytes accessed | tf_op | source)
XLA Modules:
  0.0 126.0 jit_solution(10605452672612116792)
XLA Ops:
  0.6 0.0 copy-start.5
  0.7 1.4 %fusion = s32[]{:T(128)} fusion(s32[8]{0:T(128)} %bitcast.35, s32[8]{0:T(128)} %bitcast.36), kind=kLoop, calls=%fused_computation.1 | loop fusion | flops 63 | bytes 68 | tf_op jit(solution)/shard_map/reduce_sum | solution.py:421
  2.7 0.0 copy-start
  2.7 2.2 %copy-done = bf16[1,1,8,512,512]{4,3,2,1,0:T(8,128)(2,1)S(1)} copy-done((bf16[1,1,8,512,512]{4,3,2,1,0:T(8,128)(2,1)S(1)}, bf16[1,1,8,512,512]{4,3,2,1,0:T(8,128)(2,1)}, u32[]{:S(2)}) %copy-start) | copy-done | bytes 4194328
  4.9 0.0 copy-start.2
  4.9 0.9 copy-done.2
  5.8 0.0 copy-start.1
  5.8 0.8 sketch_cols.1
  6.6 8.8 %all-gather = f32[4,32,1024]{2,1,0:T(8,128)S(1)} all-gather(f32[2,32,1024]{2,1,0:T(8,128)S(1)} %sketch_cols.1), channel_id=2, replica_groups=mesh['x'=4,'core'=2,'y'=4,'far'=4,'near'=4] {'core'}, dimensions={0}, use_global_device_ids=true | all-gather | bytes 786432 | tf_op jit(solution)/shard_map/sketch_cols/all_gather | solution.py:437
  15.4 0.0 copy-start.3
  15.4 0.0 copy-start.4
  15.4 0.1 pair.1
  15.6 9.0 %all_to_all.52.parts_ref = s16[4,32,1152]{2,1,0:T(8,128)(2,1)S(1)} all-to-all(s16[4,32,1152]{2,1,0:T(8,128)(2,1)S(1)} %pair.1), channel_id=1, replica_groups=mesh['x'=4,'core'=2,'y'=4,'far'=4,'near'=4] {'x'}, dimensions={0} | all-to-all | bytes 589824 | tf_op jit(solution)/shard_map/sketch_cols/all_to_all | solution.py:412
  24.5 0.0 copy-done.5
  24.5 0.2 scaled.1
  24.7 2.9 %all-gather.1 = bf16[64,1024]{1,0:T(8,128)(2,1)S(1)} all-gather(bf16[32,1024]{1,0:T(8,128)(2,1)S(1)} %scaled.1), channel_id=3, replica_groups=mesh['x'=4,'core'=2,'y'=4,'far'=4,'near'=4] {'core'}, dimensions={0}, use_global_device_ids=true | all-gather | bytes 196608 | tf_op jit(solution)/shard_map/scaled/all_gather | solution.py:446
  27.6 0.0 copy-done.1
  27.6 1.5 %ysketch.1 = s16[16,40,128]{2,1,0:T(8,128)(2,1)S(1)} custom-call(s32[1]{0:T(128)} %bitcast.3.places_ref, bf16[2,32,1024]{2,1,0:T(8,128)(2,1)S(1)} %bitcast.25, bf16[8,512,512]{2,1,0:T(8,128)(2,1)S(1)} %bitcast.19), custom_call_target="tpu_custom_call" | custom-call | flops 134217728 | bytes 1048576 | tf_op jit(solution)/shard_map/ysketch/ysketch/pallas_call | solution.py:448
  29.1 11.6 %all_to_all.53.parts_ref = s16[16,40,128]{2,1,0:T(8,128)(2,1)S(1)} all-to-all(s16[16,40,128]{2,1,0:T(8,128)(2,1)S(1)} %ysketch.1), channel_id=1, replica_groups=mesh['x'=4,'core'=2,'y'=4,'far'=4,'near'=4] {'y','near'}, dimensions={0} | all-to-all | bytes 327680 | tf_op jit(solution)/shard_map/ysketch/all_to_all | solution.py:412
  40.7 0.2 ysketch_near.1
  40.9 23.7 %all_to_all.54.parts_ref = f32[4,4,8,128]{3,2,1,0:T(8,128)S(1)} all-to-all(f32[4,4,8,128]{3,2,1,0:T(8,128)S(1)} %ysketch_near.1), channel_id=1, replica_groups=mesh['x'=4,'core'=2,'y'=4,'far'=4,'near'=4] {'far'}, dimensions={0} | all-to-all | bytes 131072 | tf_op jit(solution)/shard_map/ysketch/all_to_all | solution.py:412
  64.6 12.1 %all_to_all.55.tiles_ref = f32[16,4,8,128]{3,2,1,0:T(8,128)S(1)} all-to-all(f32[16,4,8,128]{3,2,1,0:T(8,128)S(1)} %ysketch_far.1), channel_id=1, replica_groups=mesh['x'=4,'core'=2,'y'=4,'far'=4,'near'=4] {'y','near'}, dimensions={0} | all-to-all | bytes 524288 | tf_op jit(solution)/shard_map/ysketch/all_to_all | solution.py:412
  76.8 0.0 copy-done.3
  76.8 0.0 copy-done.4
  76.8 0.8 gram.1
  77.5 11.3 %all_to_all.56.parts_ref = f32[8,2,8,128]{3,2,1,0:T(8,128)S(1)} all-to-all(f32[8,2,8,128]{3,2,1,0:T(8,128)S(1)} %get-tuple-element.13), channel_id=1, replica_groups=mesh['x'=4,'core'=2,'y'=4,'far'=4,'near'=4] {'x','core'}, dimensions={0} | all-to-all | bytes 131072 | tf_op jit(solution)/shard_map/gram/all_to_all | solution.py:412
  88.8 1.6 %direction.1 = (f32[8,2,8,128]{3,2,1,0:T(8,128)S(1)}, f32[80,128]{1,0:T(8,128)S(1)}, f32[1,2048]{1,0:T(1,128)S(1)}) custom-call(s32[1]{0:T(128)} %bitcast.3.places_ref, f32[8,2,8,128]{3,2,1,0:T(8,128)S(1)} %all_to_all.56.parts_ref, f32[32,2048]{1,0:T(8,128)S(1)} %get-tuple-element.14.y_ref, f32[1,2048]{1,0:T(1,128)S(1)} %bitcast.28, ...), custom_call_target="tpu_custom_call" | custom-call | flops 4194304 | bytes 1048576 | tf_op jit(solution)/shard_map/direction/direction/pallas_call | solution.py:481
  90.4 8.0 %all_to_all.57.parts_ref = f32[8,2,8,128]{3,2,1,0:T(8,128)S(1)} all-to-all(f32[8,2,8,128]{3,2,1,0:T(8,128)S(1)} %get-tuple-element.15), channel_id=1, replica_groups=mesh['x'=4,'core'=2,'y'=4,'far'=4,'near'=4] {'x','core'}, dimensions={0} | all-to-all | bytes 131072 | tf_op jit(solution)/shard_map/direction/all_to_all | solution.py:412
  98.4 1.3 %image.1 = (f32[2,8,128]{2,1,0:T(8,128)S(1)}, f32[8,128]{1,0:T(8,128)S(1)}) custom-call(s32[1]{0:T(128)} %bitcast.3.places_ref, f32[8,2,8,128]{3,2,1,0:T(8,128)S(1)} %all_to_all.57.parts_ref, f32[2,8,128]{2,1,0:T(8,128)S(1)} %bitcast.31, f32[32,2048]{1,0:T(8,128)S(1)} %get-tuple-element.14.y_ref, f32[1,2048]{1,0:T(1,128)S(1)} %get-tuple-element.16.direction_ref, ...), custom_call_target="tpu_custom_call" | custom-call | flops 4194304 | bytes 1048576 | tf_op jit(solution)/shard_map/image/image/pallas_call | solution.py:498
  99.7 7.7 %all_to_all.58 = f32[8,1,128]{2,1,0:T(1,128)S(1)} all-to-all(f32[8,1,128]{2,1,0:T(1,128)S(1)} %bitcast.34), channel_id=1, replica_groups=mesh['x'=4,'core'=2,'y'=4,'far'=4,'near'=4] {'x','core'}, dimensions={0} | all-to-all | bytes 8192 | tf_op jit(solution)/shard_map/image/all_to_all | solution.py:412
  107.4 0.1 lines.1
  107.5 17.5 %all_to_all.59 = f32[64,1,128]{2,1,0:T(1,128)S(1)} all-to-all(f32[64,1,128]{2,1,0:T(1,128)S(1)} %bitcast.32), channel_id=1, replica_groups=mesh['x'=4,'core'=2,'y'=4,'far'=4,'near'=4] {'y','far','near'}, dimensions={0} | all-to-all | bytes 65536 | tf_op jit(solution)/shard_map/image/all_to_all | solution.py:412
  125.0 0.9 step.1
  (1 shorter events, 0.0 us)
Async XLA Ops:
  0.6 23.9 %copy-start.5 = (f32[2048]{0:T(1024)S(1)}, f32[2048]{0:T(1024)}, u32[]{:S(2)}) copy-start(f32[2048]{0:T(1024)} %param.10) | copy-start | bytes 24580
  2.7 2.2 %copy-start = (bf16[1,1,8,512,512]{4,3,2,1,0:T(8,128)(2,1)S(1)}, bf16[1,1,8,512,512]{4,3,2,1,0:T(8,128)(2,1)}, u32[]{:S(2)}) copy-start(bf16[1,1,8,512,512]{4,3,2,1,0:T(8,128)(2,1)} %param.6) | copy-start | bytes 12582916
  4.9 0.9 copy-start.2
  5.8 21.9 %copy-start.1 = (bf16[1,1,8,512,512]{4,3,2,1,0:T(8,128)(2,1)S(1)}, bf16[1,1,8,512,512]{4,3,2,1,0:T(8,128)(2,1)}, u32[]{:S(2)}) copy-start(bf16[1,1,8,512,512]{4,3,2,1,0:T(8,128)(2,1)} %param.6) | copy-start | bytes 12582916
  15.4 61.4 %copy-start.3 = (bf16[2048,32]{0,1:T(8,128)(2,1)S(1)}, bf16[2048,32]{0,1:T(8,128)(2,1)}, u32[]{:S(2)}) copy-start(bf16[2048,32]{0,1:T(8,128)(2,1)} %param.9) | copy-start | bytes 393220
  15.4 61.4 %copy-start.4 = (f32[2048]{0:T(1024)S(1)}, f32[2048]{0:T(1024)}, u32[]{:S(2)}) copy-start(f32[2048]{0:T(1024)} %param.11) | copy-start | bytes 24580

commit v9 on v8

--- a/solution.py
+++ b/solution.py
@@ -149,15 +149,22 @@
     sums = [decode(parts_ref[i]) for i in range(SHARES)]
     while len(sums) > 1:
         sums = [[a + b for a, b in zip(*pair)] for pair in zip(sums[::2], sums[1::2])]
+    total = sums[0]
+    largest = jnp.abs(total[0])
+    for tile in total[1:]:
+        largest = jnp.maximum(largest, jnp.abs(tile))
+    power, mantissa = unit_of(jnp.max(largest, axis=1, keepdims=True))
+    coded = encode(total, power, mantissa)
     for i in range(FAR_PARTS):
+        out_ref[i] = coded
+
+
+def far_body(parts_ref, out_ref):
+    parts = [decode(parts_ref[i]) for i in range(FAR_PARTS)]
+    total = [(a + b) + (c + d) for a, b, c, d in zip(*parts)]
+    for i in range(SHARES):
         for q in range(SHARE_TILES):
-            out_ref[i, q] = sums[0][q]
-
-
-def far_body(parts_ref, out_ref):
-    total = (parts_ref[0] + parts_ref[1]) + (parts_ref[2] + parts_ref[3])
-    for i in range(SHARES):
-        out_ref[i] = total
+            out_ref[i, q] = total[q]
 
 
 def pack_square(square):
@@ -457,7 +464,7 @@
         parts = call(
             near_body,
             [vmem()],
-            shape((FAR_PARTS, SHARE_TILES, 8, LANES), F32),
+            shape((FAR_PARTS, 8 * SHARE_TILES + 8, LANES), I16),
             name="ysketch_near",
         )(parts)
         parts = exchange(parts, "far")

time: 126 us -> 126 us (level)
  no operation moved by 1% of the time
where the time goes in v9:
time: 126 us; the launch traced here: 125 us
  blocking collectives  112 us (89%)
  Pallas kernels  7.74 us (6%)
  local copies, waits for them, and re-layouts  3.11 us (2%)
  other arithmetic  1.38 us (1%)
  between operations  1.38 us (1%)
    all_to_all x8, blocking collectives, exchange(): return lax.all_to_all(value, axis, 0, 0, tiled=True)  100 us
    all_gather x1, blocking collectives, shards(): parts = lax.all_gather(terms, 'core')  8.82 us
    unnamed x12, local copies, waits for them, and re-layouts  3.11 us
    all_gather x1, blocking collectives, shards(): scaled = lax.all_gather(scaled, 'core')  2.9 us

profile of v9, /device:TPU:1, one launch (start us, length us, event | category | flops | bytes accessed | tf_op | source)
XLA Modules:
  0.0 125.5 jit_solution(17055905406508475444)
XLA Ops:
  0.6 0.0 copy-start.5
  0.7 1.4 %fusion = s32[]{:T(128)} fusion(s32[8]{0:T(128)} %bitcast.35, s32[8]{0:T(128)} %bitcast.36), kind=kLoop, calls=%fused_computation.1 | loop fusion | flops 63 | bytes 68 | tf_op jit(solution)/shard_map/reduce_sum | solution.py:428
  2.7 0.0 copy-start
  2.7 2.2 %copy-done = bf16[1,1,8,512,512]{4,3,2,1,0:T(8,128)(2,1)S(1)} copy-done((bf16[1,1,8,512,512]{4,3,2,1,0:T(8,128)(2,1)S(1)}, bf16[1,1,8,512,512]{4,3,2,1,0:T(8,128)(2,1)}, u32[]{:S(2)}) %copy-start) | copy-done | bytes 4194328
  4.9 0.0 copy-start.2
  4.9 0.9 copy-done.2
  5.8 0.0 copy-start.1
  5.8 0.8 sketch_cols.1
  6.6 0.0 copy-start.3
  6.6 0.0 copy-start.4
  6.6 8.8 %all-gather = f32[4,32,1024]{2,1,0:T(8,128)S(1)} all-gather(f32[2,32,1024]{2,1,0:T(8,128)S(1)} %sketch_cols.1), channel_id=2, replica_groups=mesh['x'=4,'core'=2,'y'=4,'far'=4,'near'=4] {'core'}, dimensions={0}, use_global_device_ids=true | all-gather | bytes 786432 | tf_op jit(solution)/shard_map/sketch_cols/all_gather | solution.py:444
  15.4 0.1 pair.1
  15.6 9.0 %all_to_all.52.parts_ref = s16[4,32,1152]{2,1,0:T(8,128)(2,1)S(1)} all-to-all(s16[4,32,1152]{2,1,0:T(8,128)(2,1)S(1)} %pair.1), channel_id=1, replica_groups=mesh['x'=4,'core'=2,'y'=4,'far'=4,'near'=4] {'x'}, dimensions={0} | all-to-all | bytes 589824 | tf_op jit(solution)/shard_map/sketch_cols/all_to_all | solution.py:419
  24.6 0.0 copy-done.5
  24.6 0.2 scaled.1
  24.8 2.9 %all-gather.1 = bf16[64,1024]{1,0:T(8,128)(2,1)S(1)} all-gather(bf16[32,1024]{1,0:T(8,128)(2,1)S(1)} %scaled.1), channel_id=3, replica_groups=mesh['x'=4,'core'=2,'y'=4,'far'=4,'near'=4] {'core'}, dimensions={0}, use_global_device_ids=true | all-gather | bytes 196608 | tf_op jit(solution)/shard_map/scaled/all_gather | solution.py:453
  27.7 0.0 copy-done.1
  27.7 1.5 %ysketch.1 = s16[16,40,128]{2,1,0:T(8,128)(2,1)S(1)} custom-call(s32[1]{0:T(128)} %bitcast.3.places_ref, bf16[2,32,1024]{2,1,0:T(8,128)(2,1)S(1)} %bitcast.25, bf16[8,512,512]{2,1,0:T(8,128)(2,1)S(1)} %bitcast.19), custom_call_target="tpu_custom_call" | custom-call | flops 134217728 | bytes 1048576 | tf_op jit(solution)/shard_map/ysketch/ysketch/pallas_call | solution.py:455
  29.1 11.6 %all_to_all.53.parts_ref = s16[16,40,128]{2,1,0:T(8,128)(2,1)S(1)} all-to-all(s16[16,40,128]{2,1,0:T(8,128)(2,1)S(1)} %ysketch.1), channel_id=1, replica_groups=mesh['x'=4,'core'=2,'y'=4,'far'=4,'near'=4] {'y','near'}, dimensions={0} | all-to-all | bytes 327680 | tf_op jit(solution)/shard_map/ysketch/all_to_all | solution.py:419
  40.8 0.3 ysketch_near.1
  41.0 23.6 %all_to_all.54.parts_ref = s16[4,40,128]{2,1,0:T(8,128)(2,1)S(1)} all-to-all(s16[4,40,128]{2,1,0:T(8,128)(2,1)S(1)} %ysketch_near.1), channel_id=1, replica_groups=mesh['x'=4,'core'=2,'y'=4,'far'=4,'near'=4] {'far'}, dimensions={0} | all-to-all | bytes 81920 | tf_op jit(solution)/shard_map/ysketch/all_to_all | solution.py:419
  64.6 0.2 ysketch_far.1
  64.8 12.2 %all_to_all.55.tiles_ref = f32[16,4,8,128]{3,2,1,0:T(8,128)S(1)} all-to-all(f32[16,4,8,128]{3,2,1,0:T(8,128)S(1)} %ysketch_far.1), channel_id=1, replica_groups=mesh['x'=4,'core'=2,'y'=4,'far'=4,'near'=4] {'y','near'}, dimensions={0} | all-to-all | bytes 524288 | tf_op jit(solution)/shard_map/ysketch/all_to_all | solution.py:419
  77.0 0.0 copy-done.3
  77.0 0.0 copy-done.4
  77.0 0.7 gram.1
  77.7 10.9 %all_to_all.56.parts_ref = f32[8,2,8,128]{3,2,1,0:T(8,128)S(1)} all-to-all(f32[8,2,8,128]{3,2,1,0:T(8,128)S(1)} %get-tuple-element.13), channel_id=1, replica_groups=mesh['x'=4,'core'=2,'y'=4,'far'=4,'near'=4] {'x','core'}, dimensions={0} | all-to-all | bytes 131072 | tf_op jit(solution)/shard_map/gram/all_to_all | solution.py:419
  88.6 1.6 %direction.1 = (f32[8,2,8,128]{3,2,1,0:T(8,128)S(1)}, f32[80,128]{1,0:T(8,128)S(1)}, f32[1,2048]{1,0:T(1,128)S(1)}) custom-call(s32[1]{0:T(128)} %bitcast.3.places_ref, f32[8,2,8,128]{3,2,1,0:T(8,128)S(1)} %all_to_all.56.parts_ref, f32[32,2048]{1,0:T(8,128)S(1)} %get-tuple-element.14.y_ref, f32[1,2048]{1,0:T(1,128)S(1)} %bitcast.28, ...), custom_call_target="tpu_custom_call" | custom-call | flops 4194304 | bytes 1048576 | tf_op jit(solution)/shard_map/direction/direction/pallas_call | solution.py:488
  90.2 8.0 %all_to_all.57.parts_ref = f32[8,2,8,128]{3,2,1,0:T(8,128)S(1)} all-to-all(f32[8,2,8,128]{3,2,1,0:T(8,128)S(1)} %get-tuple-element.15), channel_id=1, replica_groups=mesh['x'=4,'core'=2,'y'=4,'far'=4,'near'=4] {'x','core'}, dimensions={0} | all-to-all | bytes 131072 | tf_op jit(solution)/shard_map/direction/all_to_all | solution.py:419
  98.2 1.3 %image.1 = (f32[2,8,128]{2,1,0:T(8,128)S(1)}, f32[8,128]{1,0:T(8,128)S(1)}) custom-call(s32[1]{0:T(128)} %bitcast.3.places_ref, f32[8,2,8,128]{3,2,1,0:T(8,128)S(1)} %all_to_all.57.parts_ref, f32[2,8,128]{2,1,0:T(8,128)S(1)} %bitcast.31, f32[32,2048]{1,0:T(8,128)S(1)} %get-tuple-element.14.y_ref, f32[1,2048]{1,0:T(1,128)S(1)} %get-tuple-element.16.direction_ref, ...), custom_call_target="tpu_custom_call" | custom-call | flops 4194304 | bytes 1048576 | tf_op jit(solution)/shard_map/image/image/pallas_call | solution.py:505
  99.5 7.7 %all_to_all.58 = f32[8,1,128]{2,1,0:T(1,128)S(1)} all-to-all(f32[8,1,128]{2,1,0:T(1,128)S(1)} %bitcast.34), channel_id=1, replica_groups=mesh['x'=4,'core'=2,'y'=4,'far'=4,'near'=4] {'x','core'}, dimensions={0} | all-to-all | bytes 8192 | tf_op jit(solution)/shard_map/image/all_to_all | solution.py:419
  107.2 0.1 lines.1
  107.3 17.2 %all_to_all.59 = f32[64,1,128]{2,1,0:T(1,128)S(1)} all-to-all(f32[64,1,128]{2,1,0:T(1,128)S(1)} %bitcast.32), channel_id=1, replica_groups=mesh['x'=4,'core'=2,'y'=4,'far'=4,'near'=4] {'y','far','near'}, dimensions={0} | all-to-all | bytes 65536 | tf_op jit(solution)/shard_map/image/all_to_all | solution.py:419
  124.5 0.9 step.1
Async XLA Ops:
  0.6 23.9 %copy-start.5 = (f32[2048]{0:T(1024)S(1)}, f32[2048]{0:T(1024)}, u32[]{:S(2)}) copy-start(f32[2048]{0:T(1024)} %param.10) | copy-start | bytes 24580
  2.7 2.2 %copy-start = (bf16[1,1,8,512,512]{4,3,2,1,0:T(8,128)(2,1)S(1)}, bf16[1,1,8,512,512]{4,3,2,1,0:T(8,128)(2,1)}, u32[]{:S(2)}) copy-start(bf16[1,1,8,512,512]{4,3,2,1,0:T(8,128)(2,1)} %param.6) | copy-start | bytes 12582916
  4.9 0.9 copy-start.2
  5.8 21.9 %copy-start.1 = (bf16[1,1,8,512,512]{4,3,2,1,0:T(8,128)(2,1)S(1)}, bf16[1,1,8,512,512]{4,3,2,1,0:T(8,128)(2,1)}, u32[]{:S(2)}) copy-start(bf16[1,1,8,512,512]{4,3,2,1,0:T(8,128)(2,1)} %param.6) | copy-start | bytes 12582916
  6.6 70.4 %copy-start.3 = (bf16[2048,32]{0,1:T(8,128)(2,1)S(1)}, bf16[2048,32]{0,1:T(8,128)(2,1)}, u32[]{:S(2)}) copy-start(bf16[2048,32]{0,1:T(8,128)(2,1)} %param.9) | copy-start | bytes 393220
  6.6 70.4 %copy-start.4 = (f32[2048]{0:T(1024)S(1)}, f32[2048]{0:T(1024)}, u32[]{:S(2)}) copy-start(f32[2048]{0:T(1024)} %param.11) | copy-start | bytes 24580
